TPU v7x, 256 devices: a whole 4x4x8 slice. The times are simulated.
256 devices in a mesh: slab: 64 (over x, z, core), spd: 4 (over y).
Axes of the slice: x: 4, y: 4, z: 8, core: 2. Of those that a mesh axis runs over, the one named last changes fastest.
Arguments:
- mode_shapes: bfloat16 [131072, 512], P('slab'), may hold values from -6 to 6
- unbalance: bfloat16 [2, 131072], P(None, 'slab'), may hold values from -1 to 1
- connectivity: int32 [8, 131072], P(None, 'slab'), may hold values from 0 to 3071, as said below
- stress_weights: bfloat16 [8, 131072], P(None, 'slab'), may hold values from -0.01171875 to 0.01171875
- face_low_nodes: int32 [32768], P('slab'), may hold values from 0 to 2047
- face_high_nodes: int32 [32768], P('slab'), may hold values from 0 to 2047
- natural_freq: float32 [256], replicated, may hold values from 0.5 to 4
- damping_ratio: float32 [256], replicated, may hold values from 0.003 to 0.02
- coupling: float32 [256, 256], replicated, may hold values from -1 to 1
- speed_index: int32 [1024], P('spd'), may hold values from 0 to 4095
Outputs:
- stress_peak: float32 [131072], P('slab')
Inputs may be any that keep to these rules, and one draw needn't show every extreme that they name: For an element e with i = e mod 2048, connectivity[k, e] - i lies in 0 to 1024, and the 8 nodes of an element are distinct.
All inputs are finite; a program needn't handle non-finite values.
Results may differ from a plain program's by a relative error of at most 0.0027.
Values may be sent and summed in bfloat16 or wider, within the bound.
No kernel may reach another device: no remote copies, remote signals or barrier semaphores. Data moves between devices by JAX's collectives and lax.ppermute only.
A program may use at most 64 MiB of HBM per device.

v0:
```python
import math

import jax
import jax.numpy as jnp
from jax import lax
from jax.sharding import PartitionSpec as P

ITERS = 6
NGRID = 4096


def from_behind(x, axis, by):
    count = lax.axis_size(axis)
    pairs = [(i, i + by) for i in range(count) if 0 <= i + by < count]
    return lax.ppermute(x, axis, pairs)


def modal_solve(force_re, force_im, omega, natural_freq, damping_ratio, coupling):
    count = natural_freq.shape[0]
    off_diagonal = 1.0 - jnp.eye(count, dtype=jnp.float32)
    row_scale = damping_ratio * natural_freq * (1.5 / math.sqrt(count))
    coupled = coupling * row_scale[:, None] * off_diagonal
    omega_sq = omega * omega
    denom_re = (natural_freq * natural_freq)[:, None] - omega_sq[None, :]
    denom_im = 2.0 * (damping_ratio * natural_freq)[:, None] * omega[None, :]
    inverse = 1.0 / (denom_re * denom_re + denom_im * denom_im)
    load_re = force_re[:, None] * omega_sq[None, :]
    load_im = force_im[:, None] * omega_sq[None, :]

    def divide(top_re, top_im):
        return (
            (top_re * denom_re + top_im * denom_im) * inverse,
            (top_im * denom_re - top_re * denom_im) * inverse,
        )

    coord_re, coord_im = divide(load_re, load_im)
    for sweep in range(ITERS):
        product_re = jnp.dot(coupled, coord_re, precision=lax.Precision.HIGHEST)
        product_im = jnp.dot(coupled, coord_im, precision=lax.Precision.HIGHEST)
        coord_re, coord_im = divide(
            load_re + omega[None, :] * product_im, load_im - omega[None, :] * product_re
        )
    return (coord_re, coord_im)


def peak_of(stress_modes, coord_re, coord_im):
    columns = jnp.concatenate(
        [jnp.concatenate([coord_re, -coord_im], 0), jnp.concatenate([coord_im, coord_re], 0)], 1
    )
    stress = jnp.dot(stress_modes, columns, preferred_element_type=jnp.float32)
    speed_count = coord_re.shape[1]
    magnitude = jnp.sqrt(stress[:, :speed_count] ** 2 + stress[:, speed_count:] ** 2)
    return jnp.max(magnitude, axis=1)


def element_modes(extended, connectivity, stress_weights, rows):
    corners = connectivity.shape[0]
    block = min(128, rows)
    blocks = rows // block
    window_len = block + extended.shape[0] - rows
    links = connectivity.reshape(corners, blocks, block).transpose(1, 0, 2)
    weights = stress_weights.reshape(corners, blocks, block).transpose(1, 0, 2)
    columns = jnp.arange(window_len, dtype=jnp.int32)

    def one_block(item):
        number, link, weight = item
        start = number * block
        window = lax.dynamic_slice_in_dim(extended, start, window_len, 0)
        local = link - start
        table = jnp.sum(
            jnp.where(
                local[:, :, None] == columns[None, None, :],
                weight.astype(jnp.float32)[:, :, None],
                0.0,
            ),
            axis=0,
        )
        return jnp.dot(table.astype(jnp.bfloat16), window, preferred_element_type=jnp.float32)

    result = lax.map(one_block, (jnp.arange(blocks, dtype=jnp.int32), links, weights))
    return result.reshape(rows, extended.shape[1]).astype(jnp.bfloat16)


def on_device(
    mode_shapes,
    unbalance,
    connectivity,
    stress_weights,
    face_low_nodes,
    face_high_nodes,
    natural_freq,
    damping_ratio,
    coupling,
    speed_index,
):
    rows = mode_shapes.shape[0]
    count = natural_freq.shape[0]
    product = jnp.dot(unbalance, mode_shapes, preferred_element_type=jnp.float32)
    partial_force = jnp.stack(
        [product[0, :count] - product[1, count:], product[0, count:] + product[1, :count]]
    )
    modal_force = lax.psum(partial_force, "slab")
    from_below = from_behind(mode_shapes[face_high_nodes], "slab", 1)
    from_above = from_behind(mode_shapes[face_low_nodes], "slab", -1)
    extended = jnp.concatenate([from_below, mode_shapes, from_above], 0)
    stress_modes = element_modes(extended, connectivity, stress_weights, rows)
    omega = 0.25 + 4.0 * speed_index.astype(jnp.float32) / NGRID
    coord_re, coord_im = modal_solve(
        modal_force[0], modal_force[1], omega, natural_freq, damping_ratio, coupling
    )
    local_peak = peak_of(stress_modes, coord_re.astype(jnp.bfloat16), coord_im.astype(jnp.bfloat16))
    return lax.pmax(local_peak, "spd")


def solution(mesh):
    return jax.shard_map(
        on_device,
        mesh=mesh,
        in_specs=(
            P("slab", None),
            P(None, "slab"),
            P(None, "slab"),
            P(None, "slab"),
            P("slab"),
            P("slab"),
            P(),
            P(),
            P(),
            P("spd"),
        ),
        out_specs=P("slab"),
        check_vma=False,
    )
```

profile of v0, /device:TPU:0, one launch (start us, length us, event | category | flops | bytes accessed | tf_op | source)
XLA Modules:
  0.0 260.8 jit_solution(5199750676198050881)
XLA Ops:
  0.0 0.7 compare_select_fusion
  0.7 4.0 %gather_fusion.1 = bf16[512,512]{1,0:T(8,128)(2,1)S(1)} fusion(bf16[2048,512]{1,0:T(8,128)(2,1)} %param.12, s32[1024]{0:T(1024)S(1)} %pad_clamp_fusion), kind=kCustom, calls=%fused_computation.1 | custom fusion | bytes 1050624 | tf_op jit(solution)/shard_map/gather | solution.py:104
  4.7 1.3 collective-permute-start.1
  6.1 2.6 %gather_fusion = bf16[512,512]{1,0:T(8,128)(2,1)} fusion(bf16[2048,512]{1,0:T(8,128)(2,1)S(1)} %copy-done.1, s32[1024]{0:T(1024)S(1)} %pad_clamp_fusion.1), kind=kCustom, calls=%fused_computation | custom fusion | bytes 1050624 | tf_op jit(solution)/shard_map/gather | solution.py:103
  8.7 4.0 %collective-permute-start = (bf16[512,512]{1,0:T(8,128)(2,1)}, bf16[512,512]{1,0:T(8,128)(2,1)}, u32[]{:S(2)}, u32[]{:S(2)}) collective-permute-start(bf16[512,512]{1,0:T(8,128)(2,1)} %gather_fusion), channel_id=1, source_target_pairs={{0,4},{4,8},{8,12},{12,16},{16,20},{20,24},{24,28},{28,32},{32,36}... | collective-permute-start | bytes 1572872 | tf_op jit(solution)/shard_map/ppermute | solution.py:15
  13.1 128.7 %psum.7 = f32[2,256]{1,0:T(2,128)S(1)} all-reduce(f32[2,256]{1,0:T(2,128)S(1)} %pad_maximum_fusion.1), channel_id=1, replica_groups=mesh['slab'=64,'spd'=4] {'slab'}, use_global_device_ids=true, to_apply=%region_3.4 | all-reduce | flops 512 | bytes 4096 | tf_op jit(solution)/shard_map/psum | solution.py:102
  142.0 1.6 fusion.25
  143.6 1.5 fusion.26
  149.8 0.7 copy-done.15
  151.1 1.8 fusion.72
  152.9 1.1 fusion.157
  154.1 2.7 %pad_maximum_fusion = bf16[3072,512]{1,0:T(8,128)(2,1)} fusion(bf16[512,512]{1,0:T(8,128)(2,1)S(1)} %collective-permute-done.1, bf16[2048,512]{1,0:T(8,128)(2,1)S(1)} %copy-done.1, bf16[512,512]{1,0:T(8,128)(2,1)} %collective-permute-done), kind=kLoop, calls=%fused_computation.13 | loop fusion | flops 9437184 | bytes 6291456 | tf_op jit(solution)/shard_map/concatenate | solution.py:105
  156.8 88.9 %while.11 = (s32[]{:T(128)}, bf16[16,128,512]{2,1,0:T(8,128)(2,1)}, s32[16,8,128]{2,1,0:T(8,128)}, s32[16]{0:T(128)S(1)}, bf16[16,8,128]{2,1,0:T(8,128)(2,1)}, /...) while((s32[]{:T(128)}, bf16[16,128,512]{2,1,0:T(8,128)(2,1)}, ...), condition=%wide.region_2.3_spmd.clone, body=%wide.region_0.2_spmd.clone.sunk | while | flops 154388480 | bytes 2054331 | solution.py:80
  158.1 0.7 bitcast_convert_fusion.2
  158.8 0.7 subtract_bitcast_fusion.2
  160.1 2.3 fusion.170
  163.6 0.7 bitcast_convert_fusion.2
  164.3 0.7 subtract_bitcast_fusion.2
  165.7 2.3 fusion.170
  169.2 0.7 bitcast_convert_fusion.2
  169.9 0.7 subtract_bitcast_fusion.2
  171.2 2.3 fusion.170
  174.7 0.7 bitcast_convert_fusion.2
  175.4 0.7 subtract_bitcast_fusion.2
  176.7 2.3 fusion.170
  180.3 0.7 bitcast_convert_fusion.2
  181.0 0.7 subtract_bitcast_fusion.2
  182.3 2.3 fusion.170
  185.8 0.7 bitcast_convert_fusion.2
  186.5 0.7 subtract_bitcast_fusion.2
  187.8 2.3 fusion.170
  191.4 0.7 bitcast_convert_fusion.2
  192.1 0.7 subtract_bitcast_fusion.2
  193.4 2.3 fusion.170
  196.9 0.7 bitcast_convert_fusion.2
  197.6 0.7 subtract_bitcast_fusion.2
  199.0 2.3 fusion.170
  202.5 0.7 bitcast_convert_fusion.2
  203.2 0.7 subtract_bitcast_fusion.2
  204.5 2.3 fusion.170
  208.0 0.7 bitcast_convert_fusion.2
  208.7 0.7 subtract_bitcast_fusion.2
  210.1 2.3 fusion.170
  213.6 0.7 bitcast_convert_fusion.2
  214.3 0.7 subtract_bitcast_fusion.2
  215.6 2.3 fusion.170
  219.1 0.7 bitcast_convert_fusion.2
  219.8 0.7 subtract_bitcast_fusion.2
  221.2 2.3 fusion.170
  224.7 0.7 bitcast_convert_fusion.2
  225.4 0.7 subtract_bitcast_fusion.2
  226.7 2.3 fusion.170
  230.2 0.7 bitcast_convert_fusion.2
  230.9 0.7 subtract_bitcast_fusion.2
  232.3 2.3 fusion.170
  235.8 0.7 bitcast_convert_fusion.2
  236.5 0.7 subtract_bitcast_fusion.2
  237.8 2.3 fusion.170
  241.4 0.7 bitcast_convert_fusion.2
  242.1 0.7 subtract_bitcast_fusion.2
  243.4 2.3 fusion.170
  245.7 2.9 %fusion.27 = f32[2048,512]{0,1:T(8,128)S(1)} fusion(bf16[2048,512]{1,0:T(8,128)(2,1)} %bitcast.33, bf16[256,256]{1,0:T(8,128)(2,1)S(1)} %get-tuple-element.80, bf16[256,256]{1,0:T(8,128)(2,1)S(1)} %get-tuple-element.70, bf16[256,256]{1,0:T(8,128)(2,1)S(1)} %get-tuple-element.69), kind=kOutput, calls=%fused_computation.73 | convolution fusion | flops 1075838976 | bytes 6684672 | tf_op jit(solution)/shard_map/dot_general | solution.py:50
  248.6 0.8 fusion.14
  249.4 11.4 %pmax.7 = f32[2048]{0:T(1024)} all-reduce(f32[2048]{0:T(1024)S(1)} %fusion.14), channel_id=1, replica_groups=mesh['slab'=64,'spd'=4] {'spd'}, use_global_device_ids=true, to_apply=%region_5.6 | all-reduce | flops 2048 | bytes 16384 | tf_op jit(solution)/shard_map/pmax | solution.py:112
  (84 shorter events, 25.3 us)
Async XLA Ops:
  0.0 12.7 %copy-start = (bf16[2,2048]{1,0:T(2,128)(2,1)S(1)}, bf16[2,2048]{1,0:T(2,128)(2,1)}, u32[]{:S(2)}) copy-start(bf16[2,2048]{1,0:T(2,128)(2,1)} %param.13) | copy-start | bytes 24580
  0.7 5.3 %copy-start.7 = (s32[512]{0:T(512)S(1)}, s32[512]{0:T(512)}, u32[]{:S(2)}) copy-start(s32[512]{0:T(512)} %param.17) | copy-start | bytes 6148
  0.7 5.4 %copy-start.1 = (bf16[2048,512]{1,0:T(8,128)(2,1)S(1)}, bf16[2048,512]{1,0:T(8,128)(2,1)}, u32[]{:S(2)}) copy-start(bf16[2048,512]{1,0:T(8,128)(2,1)} %param.12) | copy-start | bytes 6291460
  4.7 149.4 %collective-permute-start.1 = (bf16[512,512]{1,0:T(8,128)(2,1)S(1)}, bf16[512,512]{1,0:T(8,128)(2,1)S(1)}, u32[]{:S(2)}, u32[]{:S(2)}) collective-permute-start(bf16[512,512]{1,0:T(8,128)(2,1)S(1)} %gather_fusion.1), channel_id=1, source_target_pairs={{4,0},{8,4},{12,8},{16,12},{20,16},{24,20},{28,24},{32,28},{36,32}... | collective-permute-start | bytes 1572872 | tf_op jit(solution)/shard_map/ppermute | solution.py:15
  8.7 133.2 %copy-start.9 = (f32[256]{0:T(256)S(1)}, f32[256]{0:T(256)}, u32[]{:S(2)}) copy-start(f32[256]{0:T(256)} %param.19) | copy-start | bytes 3076
  8.7 133.2 %copy-start.10 = (f32[256]{0:T(256)S(1)}, f32[256]{0:T(256)}, u32[]{:S(2)}) copy-start(f32[256]{0:T(256)} %param.18) | copy-start | bytes 3076
  8.7 133.2 %copy-start.11 = (s32[256]{0:T(256)S(1)}, s32[256]{0:T(256)}, u32[]{:S(2)}) copy-start(s32[256]{0:T(256)} %param.21) | copy-start | bytes 3076
  8.7 145.4 %collective-permute-start = (bf16[512,512]{1,0:T(8,128)(2,1)}, bf16[512,512]{1,0:T(8,128)(2,1)}, u32[]{:S(2)}, u32[]{:S(2)}) collective-permute-start(bf16[512,512]{1,0:T(8,128)(2,1)} %gather_fusion), channel_id=1, source_target_pairs={{0,4},{4,8},{8,12},{12,16},{16,20},{20,24},{24,28},{28,32},{32,36}... | collective-permute-start | bytes 1572872 | tf_op jit(solution)/shard_map/ppermute | solution.py:15
  141.9 6.6 %copy-start.8 = (f32[1,256]{1,0:T(1,128)}, f32[1,256]{1,0:T(1,128)S(1)}, u32[]{:S(2)}) copy-start(f32[1,256]{1,0:T(1,128)S(1)} %get-tuple-element.76) | copy-start | bytes 3076
  141.9 7.7 %copy-start.3 = (f32[256]{0:T(256)}, f32[256]{0:T(256)S(1)}, u32[]{:S(2)}) copy-start(f32[256]{0:T(256)S(1)} %get-tuple-element.82) | copy-start | bytes 3076
  141.9 7.7 %copy-start.5 = (f32[256]{0:T(256)}, f32[256]{0:T(256)S(1)}, u32[]{:S(2)}) copy-start(f32[256]{0:T(256)S(1)} %get-tuple-element.83) | copy-start | bytes 3076
  141.9 7.7 %copy-start.12 = (f32[256]{0:T(256)}, f32[256]{0:T(256)S(1)}, u32[]{:S(2)}) copy-start(f32[256]{0:T(256)S(1)} %get-tuple-element.73) | copy-start | bytes 3076
  141.9 3.1 %copy-start.13 = (f32[256,256]{1,0:T(8,128)S(1)}, f32[256,256]{1,0:T(8,128)}, u32[]{:S(2)}) copy-start(f32[256,256]{1,0:T(8,128)} %param.20) | copy-start | bytes 786436
  149.1 0.7 copy-start.14
  149.8 0.7 copy-start.15
  151.1 1.9 copy-start.2
  151.1 1.8 copy-start.4
  151.1 1.8 copy-start.6
where the time goes:
time: 263 us; the launch traced here: 261 us
  blocking collectives  140 us (53%)
  matrix products  49.6 us (19%)
  other arithmetic  37.8 us (14%)
  local copies, waits for them, and re-layouts  16.9 us (6%)
  loops' own time  10.7 us (4%)
  starting transfers between devices  5.3 us (2%)
    psum x1, blocking collectives, on_device(): modal_force = lax.psum(partial_force, 'slab')  129 us
    dot_general x16, matrix products, one_block(): jnp.dot(table.astype(jnp.bfloat16), window, preferred_element_type=jnp.fl...  36.4 us
    pmax x1, blocking collectives, on_device(): return lax.pmax(local_peak, 'spd')  11.4 us
    convert_element_type x16, other arithmetic, one_block(): weight.astype(jnp.float32)[:, :, None]  11 us
    sub x16, other arithmetic, one_block(): local = link - start  11 us
    another operation x1, loops' own time, element_modes(): lax.map(one_block, (jnp.arange(blocks, dtype=jnp.int32), links, weights))  10.7 us
    reduce_sum x16, other arithmetic, one_block(): jnp.sum(jnp.where(local[:, :, None] == columns[None, None, :], weight.ast...  10.4 us
    dynamic_slice x16, local copies, waits for them, and re-layouts, element_modes(): lax.map(one_block, (jnp.arange(blocks, dtype=jnp.int32), links, weights))  9.32 us
  transfers between devices with their start and end apart: 2, of which 0 were waited for; matrix products, arithmetic and copies ran while one was open for 5% of the time, Pallas kernels for 0%

commit v1 on v0

v1 whole, which is shorter than its diff:
```python
import functools
import math

import jax
import jax.numpy as jnp
from jax import lax
from jax.experimental import pallas as pl
from jax.experimental.pallas import tpu as pltpu
from jax.sharding import PartitionSpec as P

ITERS = 6
NGRID = 4096
X, Z, CORES = 4, 8, 2
BLOCK = 256
WINDOW = 1280
GROUP = 16
NN = (((1,), (0,)), ((), ()))
NT = (((1,), (1,)), ((), ()))


def mm(a, b, dims=NN):
    return lax.dot_general(a, b, dims, preferred_element_type=jnp.float32)


def vmem_call(body, out_shape, operands, scratch=(), flops=0, moved=0):
    spec = pl.BlockSpec(memory_space=pltpu.VMEM)
    many = isinstance(out_shape, (list, tuple))
    return pl.pallas_call(
        body,
        out_shape=out_shape,
        in_specs=[spec] * len(operands),
        out_specs=[spec] * len(out_shape) if many else spec,
        scratch_shapes=list(scratch),
        compiler_params=pltpu.CompilerParams(vmem_limit_bytes=24 << 20),
        cost_estimate=pl.CostEstimate(flops=flops, bytes_accessed=moved, transcendentals=0),
    )(*operands)


def slab_pairs(partner):
    pairs = []
    for x in range(X):
        for z in range(Z):
            for c in range(CORES):
                px, pz, pc = partner(x, z, c)
                pairs.append(((x * Z + z) * CORES + c, (px * Z + pz) * CORES + pc))
    return pairs


ROUNDS = (
    slab_pairs(lambda x, z, c: (x, z, 1 - c)),
    slab_pairs(lambda x, z, c: (x ^ 1, z, c)),
    slab_pairs(lambda x, z, c: (3 - x, z, c)),
    slab_pairs(lambda x, z, c: (x, z ^ 1, c)),
    slab_pairs(lambda x, z, c: (x, z ^ 2, c)),
    slab_pairs(lambda x, z, c: (x, 7 - z, c)),
)


def sum_over_slabs(x):
    for pairs in ROUNDS:
        x = x + lax.ppermute(x, "slab", pairs)
    return x


def from_behind(x, axis, by):
    count = lax.axis_size(axis)
    pairs = [(i, i + by) for i in range(count) if 0 <= i + by < count]
    return lax.ppermute(x, axis, pairs)


def gather_body(nodes, shapes, out, table):
    count, rows = table.shape
    place = jnp.transpose(jnp.broadcast_to(nodes[...], (8, count)))
    column = lax.broadcasted_iota(jnp.int16, (GROUP, rows), 1)
    for r in range(0, count, GROUP):
        here = jnp.broadcast_to(place[r : r + GROUP, 0:1], (GROUP, 128)).astype(jnp.int16)
        here = jnp.concatenate([here] * (rows // 128), 1)
        table[r : r + GROUP, :] = jnp.where(
            here == column, jnp.ones((), jnp.bfloat16), jnp.zeros((), jnp.bfloat16)
        )
    out[...] = mm(table[...], shapes[...]).astype(jnp.bfloat16)


def gather_rows(nodes, shapes):
    count, (rows, width) = nodes.shape[0], shapes.shape
    return vmem_call(
        gather_body,
        jax.ShapeDtypeStruct((count, width), shapes.dtype),
        (nodes.reshape(1, count), shapes),
        [pltpu.VMEM((count, rows), jnp.bfloat16)],
        flops=2 * count * rows * width,
    )


def fill_table(table, links, weights, start):
    place = jnp.transpose(links) - start
    weight = jnp.transpose(weights.astype(jnp.float32))
    corners = links.shape[0]
    column = lax.broadcasted_iota(jnp.int16, (GROUP, WINDOW), 1)
    for r in range(0, BLOCK, GROUP):
        row = jnp.zeros((GROUP, WINDOW), jnp.bfloat16)
        for k in range(corners):
            here = jnp.broadcast_to(place[r : r + GROUP, k : k + 1], (GROUP, 128)).astype(jnp.int16)
            value = jnp.broadcast_to(weight[r : r + GROUP, k : k + 1], (GROUP, 128)).astype(jnp.bfloat16)
            here = jnp.concatenate([here] * (WINDOW // 128), 1)
            value = jnp.concatenate([value] * (WINDOW // 128), 1)
            row = jnp.where(here == column, value, row)
        table[r : r + GROUP, :] = row


def middle_body(links, weights, shapes, out, tables):
    for b in range(2, 6):
        s = pl.ds(b * BLOCK, BLOCK)
        fill_table(tables.at[b % 2], links[:, s], weights[:, s], b * BLOCK)
        first = (b - 2) * BLOCK
        out[pl.ds(first, BLOCK), :] = mm(tables[b % 2], shapes[first : first + WINDOW, :]).astype(jnp.bfloat16)


def low_body(links, weights, below, shapes, out, tables):
    for b in range(2):
        s = pl.ds(b * BLOCK, BLOCK)
        fill_table(tables.at[b], links[:, s], weights[:, s], b * BLOCK)
        halo = (2 - b) * BLOCK
        total = mm(tables[b, :, :halo], below[b * BLOCK :, :])
        total += mm(tables[b, :, halo:], shapes[: WINDOW - halo, :])
        out[s, :] = total.astype(jnp.bfloat16)


def high_body(links, weights, shapes, above, out, tables):
    rows = shapes.shape[0]
    for b in range(2):
        s = pl.ds((6 + b) * BLOCK, BLOCK)
        fill_table(tables.at[b], links[:, s], weights[:, s], (6 + b) * BLOCK)
        halo = (1 + b) * BLOCK
        own = WINDOW - halo
        total = mm(tables[b, :, :own], shapes[rows - own :, :])
        total += mm(tables[b, :, own:], above[:halo, :])
        out[pl.ds(b * BLOCK, BLOCK), :] = total.astype(jnp.bfloat16)


def stress_modes_of(links, weights, below, shapes, above):
    width = shapes.shape[1]
    tables = [pltpu.VMEM((2, BLOCK, WINDOW), jnp.bfloat16)]

    def call(body, blocks, operands):
        return vmem_call(
            body,
            jax.ShapeDtypeStruct((blocks * BLOCK, width), jnp.bfloat16),
            operands,
            tables,
            flops=4 * blocks * BLOCK * WINDOW * width,
        )

    middle = call(middle_body, 4, (links, weights, shapes))
    low = call(low_body, 2, (links, weights, below, shapes))
    high = call(high_body, 2, (links, weights, shapes, above))
    return low, middle, high


def split(x):
    high = x.astype(jnp.bfloat16)
    return high, (x - high.astype(jnp.float32)).astype(jnp.bfloat16)


def prepare_body(speeds, freq, damping, coupling, u_re, u_im, omega_out, c_high, c_low):
    count = freq.shape[1]
    total = speeds.shape[1]
    omega = 0.25 + 4.0 * speeds[...].astype(jnp.float32) / NGRID
    omega = jnp.transpose(jnp.broadcast_to(omega, (8, total)))[:, 0:1]
    omega = jnp.broadcast_to(omega, (total, count))
    f = freq[...]
    zeta = damping[...]
    d_re = f * f - omega * omega
    d_im = 2.0 * (zeta * f) * omega
    scale = omega / (d_re * d_re + d_im * d_im)
    u_re[...] = d_re * scale
    u_im[...] = d_im * scale
    omega_out[...] = omega[:, :128]
    i = lax.broadcasted_iota(jnp.int32, (count, count), 0)
    j = lax.broadcasted_iota(jnp.int32, (count, count), 1)
    coupled = jnp.transpose(coupling[...]) * (zeta * f * (1.5 / math.sqrt(count)))
    c_high[...], c_low[...] = split(jnp.where(i == j, 0.0, coupled))


def prepare(speeds, freq, damping, coupling):
    total, count = speeds.shape[0], freq.shape[0]
    sds = jax.ShapeDtypeStruct
    return vmem_call(
        prepare_body,
        [
            sds((total, count), jnp.float32),
            sds((total, count), jnp.float32),
            sds((total, 128), jnp.float32),
            sds((count, count), jnp.bfloat16),
            sds((count, count), jnp.bfloat16),
        ],
        (speeds.reshape(1, total), freq.reshape(1, count), damping.reshape(1, count), coupling),
        flops=1 << 30,
    )


def solve_into(force, u_re, u_im, omega, c_high, c_low, store):
    f_re, f_im = force[0:1, :], force[1:2, :]
    ch, cl = c_high[...], c_low[...]

    def coupled(y):
        high, low = split(y)
        return mm(high, ch) + (mm(low, ch) + mm(high, cl))

    total, count = u_re.shape
    tile = 256
    tiles = [pl.ds(t, tile) for t in range(0, total, tile)]
    state = []
    for s in tiles:
        ur, ui = u_re[s, :], u_im[s, :]
        state.append((f_re * ur + f_im * ui, f_im * ur - f_re * ui))
    for sweep in range(ITERS):
        after = []
        for s, (yr, yi) in zip(tiles, state):
            pr, pi = coupled(yr), coupled(yi)
            ur, ui = u_re[s, :], u_im[s, :]
            top_re, top_im = f_re + pi, f_im - pr
            after.append((top_re * ur + top_im * ui, top_im * ur - top_re * ui))
        state = after
    for s, (yr, yi) in zip(tiles, state):
        w = omega[s, :]
        w = jnp.concatenate([w] * (count // 128), 1)
        store(s, (yr * w).astype(jnp.bfloat16), (yi * w).astype(jnp.bfloat16))


def peaks_body(force, u_re, u_im, omega, c_high, c_low, low, middle, high, out, for_re, for_im):
    count = u_re.shape[1]
    total = u_re.shape[0]

    def store(s, re, im):
        for_re[s, :count] = re
        for_re[s, count:] = -im
        for_im[s, :count] = im
        for_im[s, count:] = re

    solve_into(force, u_re, u_im, omega, c_high, c_low, store)
    tile = 256
    at = 0
    for part in (low, middle, high):
        for e in range(0, part.shape[0], BLOCK):
            modes = part[e : e + BLOCK, :]
            best = jnp.zeros((8, BLOCK), jnp.float32)
            for s in range(0, total, tile):
                re = mm(for_re[s : s + tile, :], modes, NT)
                im = mm(for_im[s : s + tile, :], modes, NT)
                square = re * re + im * im
                best = jnp.maximum(best, jnp.max(square.reshape(tile // 8, 8, BLOCK), axis=0))
            out[0:1, at : at + BLOCK] = jnp.sqrt(jnp.max(best, axis=0, keepdims=True))
            at += BLOCK


def peaks(force, prepared, parts):
    total, count = prepared[0].shape
    rows = sum(p.shape[0] for p in parts)
    out = vmem_call(
        peaks_body,
        jax.ShapeDtypeStruct((1, rows), jnp.float32),
        (force, *prepared, *parts),
        [pltpu.VMEM((total, 2 * count), jnp.bfloat16)] * 2,
        flops=4 * rows * total * 2 * count,
    )
    return out.reshape(rows)


def on_device(
    mode_shapes,
    unbalance,
    connectivity,
    stress_weights,
    face_low_nodes,
    face_high_nodes,
    natural_freq,
    damping_ratio,
    coupling,
    speed_index,
):
    count = natural_freq.shape[0]
    product = jnp.dot(unbalance, mode_shapes, preferred_element_type=jnp.float32)
    force = jnp.stack(
        [product[0, :count] - product[1, count:], product[0, count:] + product[1, :count]]
    )
    force = sum_over_slabs(force)
    speeds = speed_index
    for pairs in ([(0, 1), (1, 0), (2, 3), (3, 2)], [(0, 3), (3, 0), (1, 2), (2, 1)]):
        speeds = jnp.concatenate([speeds, lax.ppermute(speeds, "spd", pairs)])
    prepared = prepare(speeds, natural_freq, damping_ratio, coupling)
    below = from_behind(gather_rows(face_high_nodes, mode_shapes), "slab", 1)
    above = from_behind(gather_rows(face_low_nodes, mode_shapes), "slab", -1)
    parts = stress_modes_of(connectivity, stress_weights, below, mode_shapes, above)
    return peaks(force, prepared, parts)


def solution(mesh):
    return jax.shard_map(
        on_device,
        mesh=mesh,
        in_specs=(
            P("slab", None),
            P(None, "slab"),
            P(None, "slab"),
            P(None, "slab"),
            P("slab"),
            P("slab"),
            P(),
            P(),
            P(),
            P("spd"),
        ),
        out_specs=P("slab"),
        check_vma=False,
    )
```

time: 263 us -> 53 us (0.20)
  the two profiles are of different devices: /device:TPU:0 before, /device:TPU:32 now
where the time goes in v1:
time: 53 us; the launch traced here: 52.8 us
  Pallas kernels  22.3 us (42%)
  starting transfers between devices  20.2 us (38%)
  waiting for transfers between devices  7.9 us (15%)
  matrix products  1.96 us (4%)
    pallas_call x7, Pallas kernels, vmem_call(): pl.pallas_call(body, out_shape=out_shape, in_specs=[spec] * len(operands)...  22.3 us
    ppermute x6, starting transfers between devices, sum_over_slabs(): x = x + lax.ppermute(x, 'slab', pairs)  10.9 us
    ppermute x6, waiting for transfers between devices, sum_over_slabs(): x = x + lax.ppermute(x, 'slab', pairs)  7.89 us
    ppermute x2, starting transfers between devices, from_behind(): return lax.ppermute(x, axis, pairs)  5.42 us
    ppermute x2, starting transfers between devices, on_device(): speeds = jnp.concatenate([speeds, lax.ppermute(speeds, 'spd', pairs)])  3.93 us
    dot_general x1, matrix products, on_device(): jnp.dot(unbalance, mode_shapes, preferred_element_type=jnp.float32)  1.96 us
  transfers between devices with their start and end apart: 10, of which 3 were waited for; matrix products, arithmetic and copies ran while one was open for 4% of the time, Pallas kernels for 17%

profile of v1, /device:TPU:32, one launch (start us, length us, event | category | flops | bytes accessed | tf_op | source)
XLA Modules:
  0.0 52.8 jit_solution(10605116534404542822)
XLA Ops:
  0.0 0.0 copy-start
  0.0 0.0 copy-start.1
  0.0 0.0 copy-start.5
  0.0 1.7 %collective-permute-start.6 = (s32[256]{0:T(256)}, s32[256]{0:T(256)S(1)}, u32[]{:S(2)}, u32[]{:S(2)}) collective-permute-start(s32[256]{0:T(256)} %param.19), channel_id=1, source_target_pairs={{0,1},{1,0},{2,3},{3,2},{4,5},{5,4},{6,7},{7,6},{8,9},{9,8},{10,11... | collective-permute-start | bytes 3080 | tf_op jit(solution)/shard_map/ppermute | solution.py:290
  1.7 0.0 copy-done
  1.7 2.0 %fusion.1 = f32[2,512]{1,0:T(2,128)S(1)} fusion(bf16[2,2048]{1,0:T(2,128)(2,1)S(1)} %copy-done, bf16[2048,512]{1,0:T(8,128)(2,1)} %shapes.9), kind=kOutput, calls=%fused_computation.6 | convolution fusion | flops 4194304 | bytes 2109440 | tf_op jit(solution)/shard_map/dot_general | solution.py:283
  3.6 0.0 copy-start.6
  3.7 0.1 collective-permute-start
  3.8 0.0 copy-done.1
  3.8 0.0 copy-done.5
  3.8 1.5 %shard_map.101 = bf16[512,512]{1,0:T(8,128)(2,1)S(1)} custom-call(s32[1,512]{1,0:T(1,128)S(1)} %bitcast.9, bf16[2048,512]{1,0:T(8,128)(2,1)S(1)} %copy-done.1), custom_call_target="tpu_custom_call" | custom-call | flops 1073741824 | tf_op jit(solution)/shard_map/pallas_call | solution.py:28
  5.3 0.0 copy-start.9
  5.3 0.0 copy-start.3
  5.3 0.0 copy-start.4
  5.3 2.5 %collective-permute-start.8 = (bf16[512,512]{1,0:T(8,128)(2,1)S(1)}, bf16[512,512]{1,0:T(8,128)(2,1)S(1)}, u32[]{:S(2)}, u32[]{:S(2)}) collective-permute-start(bf16[512,512]{1,0:T(8,128)(2,1)S(1)} %shard_map.101), channel_id=1, source_target_pairs={{0,4},{4,8},{8,12},{12,16},{16,20},{20,24},{24,28},{28,32},{32,36}... | collective-permute-start | bytes 1572872 | tf_op jit(solution)/shard_map/ppermute | solution.py:68
  7.9 0.0 collective-permute-done
  7.9 1.6 %collective-permute-start.1 = (f32[2,256]{1,0:T(2,128)S(1)}, f32[2,256]{1,0:T(2,128)S(1)}, u32[]{:S(2)}, u32[]{:S(2)}) collective-permute-start(f32[2,256]{1,0:T(2,128)S(1)} %fusion), channel_id=1, source_target_pairs={{0,64},{4,68},{8,72},{12,76},{16,80},{20,84},{24,88},{28,92},{32,9... | collective-permute-start | bytes 6152 | tf_op jit(solution)/shard_map/ppermute | solution.py:61
  9.5 0.0 copy-done.6
  9.5 1.5 %shard_map.104 = bf16[512,512]{1,0:T(8,128)(2,1)S(1)} custom-call(s32[1,512]{1,0:T(1,128)S(1)} %bitcast.10, bf16[2048,512]{1,0:T(8,128)(2,1)S(1)} %copy-done.1), custom_call_target="tpu_custom_call" | custom-call | flops 1073741824 | tf_op jit(solution)/shard_map/pallas_call | solution.py:28
  11.0 2.9 %collective-permute-start.9 = (bf16[512,512]{1,0:T(8,128)(2,1)S(1)}, bf16[512,512]{1,0:T(8,128)(2,1)S(1)}, u32[]{:S(2)}, u32[]{:S(2)}) collective-permute-start(bf16[512,512]{1,0:T(8,128)(2,1)S(1)} %shard_map.104), channel_id=1, source_target_pairs={{4,0},{8,4},{12,8},{16,12},{20,16},{24,20},{28,24},{32,28},{36,32}... | collective-permute-start | bytes 1572872 | tf_op jit(solution)/shard_map/ppermute | solution.py:68
  13.9 0.0 collective-permute-done.1
  13.9 2.2 %collective-permute-start.2 = (f32[2,256]{1,0:T(2,128)S(1)}, f32[2,256]{1,0:T(2,128)S(1)}, u32[]{:S(2)}, u32[]{:S(2)}) collective-permute-start(f32[2,256]{1,0:T(2,128)S(1)} %fusion.4), channel_id=1, source_target_pairs={{0,192},{4,196},{8,200},{12,204},{16,208},{20,212},{24,216},{28,22... | collective-permute-start | bytes 6152 | tf_op jit(solution)/shard_map/ppermute | solution.py:61
  16.1 0.0 collective-permute-done.6
  16.1 0.0 copy-done.9
  16.1 2.3 %collective-permute-start.7 = (s32[512]{0:T(512)S(1)}, s32[512]{0:T(512)S(1)}, u32[]{:S(2)}, u32[]{:S(2)}) collective-permute-start(s32[512]{0:T(512)S(1)} %pad_add_fusion.1), channel_id=1, source_target_pairs={{0,3},{3,0},{1,2},{2,1},{4,7},{7,4},{5,6},{6,5},{8,11},{11,8},{9,1... | collective-permute-start | bytes 6152 | tf_op jit(solution)/shard_map/ppermute | solution.py:290
  18.4 0.4 collective-permute-done.2
  18.8 0.0 copy-start.2
  18.8 0.0 copy-start.7
  18.8 0.0 copy-start.8
  18.8 4.0 %collective-permute-start.3 = (f32[2,256]{1,0:T(2,128)S(1)}, f32[2,256]{1,0:T(2,128)S(1)}, u32[]{:S(2)}, u32[]{:S(2)}) collective-permute-start(f32[2,256]{1,0:T(2,128)S(1)} %add.25), channel_id=1, source_target_pairs={{0,8},{4,12},{8,0},{12,4},{16,24},{20,28},{24,16},{28,20},{32,40},... | collective-permute-start | bytes 6152 | tf_op jit(solution)/shard_map/ppermute | solution.py:61
  22.8 0.0 copy-done.3
  22.8 0.0 copy-done.4
  22.8 3.3 %shard_map.103.middle = bf16[1024,512]{1,0:T(8,128)(2,1)S(1)} custom-call(s32[8,2048]{1,0:T(8,128)S(1)} %copy-done.3, bf16[8,2048]{1,0:T(8,128)(2,1)S(1)} %copy-done.4, bf16[2048,512]{1,0:T(8,128)(2,1)S(1)} %copy-done.1), custom_call_target="tpu_custom_call" | custom-call | flops 2684354560 | tf_op jit(solution)/shard_map/pallas_call | solution.py:28
  26.2 0.0 collective-permute-done.3
  26.2 0.1 collective-permute-start.4
  26.3 0.0 collective-permute-done.7
  26.3 4.4 %collective-permute-done.4 = f32[2,256]{1,0:T(2,128)S(1)} collective-permute-done((f32[2,256]{1,0:T(2,128)S(1)}, f32[2,256]{1,0:T(2,128)S(1)}, u32[]{:S(2)}, u32[]{:S(2)}) %collective-permute-start.4) | collective-permute-done | bytes 2080 | tf_op jit(solution)/shard_map/ppermute | solution.py:61
  30.8 2.9 %collective-permute-start.5 = (f32[2,256]{1,0:T(2,128)S(1)}, f32[2,256]{1,0:T(2,128)S(1)}, u32[]{:S(2)}, u32[]{:S(2)}) collective-permute-start(f32[2,256]{1,0:T(2,128)S(1)} %add.27), channel_id=1, source_target_pairs={{0,56},{4,60},{8,48},{12,52},{16,40},{20,44},{24,32},{28,36},{32,2... | collective-permute-start | bytes 6152 | tf_op jit(solution)/shard_map/ppermute | solution.py:61
  33.7 0.0 copy-done.2
  33.7 0.0 copy-done.7
  33.7 0.0 copy-done.8
  33.7 0.6 %shard_map.100 = (f32[1024,256]{1,0:T(8,128)S(1)}, f32[1024,256]{1,0:T(8,128)S(1)}, f32[1024,128]{1,0:T(8,128)S(1)}, bf16[256,256]{1,0:T(8,128)(2,1)S(1)}, bf16[256,256]{1,0:T(8,128)(2,1)S(1)}) custom-call(s32[1,1024]{1,0:T(1,128)S(1)} %bitcast.8, f32[1,256]{1,0:T(1,128)S(1)} %bitcast.11, f32[1,256]{1,0:T(1,128)S(1)} %bitcast.12, f32[256,256]{1,0:T(8,128)S(1)} %copy-done.2), custom_call_target="tpu_custom_call" | custom-call | flops 1073741824 | tf_op jit(solution)/shard_map/pallas_call | solution.py:28
  34.4 3.0 %collective-permute-done.5 = f32[2,256]{1,0:T(2,128)S(1)} collective-permute-done((f32[2,256]{1,0:T(2,128)S(1)}, f32[2,256]{1,0:T(2,128)S(1)}, u32[]{:S(2)}, u32[]{:S(2)}) %collective-permute-start.5) | collective-permute-done | bytes 2080 | tf_op jit(solution)/shard_map/ppermute | solution.py:61
  37.4 0.0 collective-permute-done.8.below
  37.4 2.0 %shard_map.102.low = bf16[512,512]{1,0:T(8,128)(2,1)S(1)} custom-call(s32[8,2048]{1,0:T(8,128)S(1)} %copy-done.3, bf16[8,2048]{1,0:T(8,128)(2,1)S(1)} %copy-done.4, bf16[512,512]{1,0:T(8,128)(2,1)S(1)} %collective-permute-done.8.below, bf16[2048,512]{1,0:T(8,128)(2,1)S(1)} %copy-done.1), custom_call_target="tpu_custom_call" | custom-call | flops 1342177280 | tf_op jit(solution)/shard_map/pallas_call | solution.py:28
  39.4 0.0 collective-permute-done.9.above
  39.4 2.0 %shard_map.105.high = bf16[512,512]{1,0:T(8,128)(2,1)S(1)} custom-call(s32[8,2048]{1,0:T(8,128)S(1)} %copy-done.3, bf16[8,2048]{1,0:T(8,128)(2,1)S(1)} %copy-done.4, bf16[2048,512]{1,0:T(8,128)(2,1)S(1)} %copy-done.1, bf16[512,512]{1,0:T(8,128)(2,1)S(1)} %collective-permute-done.9.above), custom_call_target="tpu_custom_call" | custom-call | flops 1342177280 | tf_op jit(solution)/shard_map/pallas_call | solution.py:28
  41.4 11.4 %shard_map.106 = f32[1,2048]{1,0:T(1,128)} custom-call(f32[2,256]{1,0:T(2,128)S(1)} %add.28.force, f32[1024,256]{1,0:T(8,128)S(1)} %get-tuple-element.10.u_re, f32[1024,256]{1,0:T(8,128)S(1)} %get-tuple-element.11.u_im, f32[1024,128]{1,0:T(8,128)S(1)} %get-tuple-element.12.omega, bf16[256,256]{1,0:T(8,128)(2,1)S(1)} %get-tuple-element.13.c_high, ...), custom_call_target="tpu_custom_call" | custom-call | flops 4294967296 | tf_op jit(solution)/shard_map/pallas_call | solution.py:28
  (10 shorter events, 0.1 us)
Async XLA Ops:
  0.0 1.7 %copy-start = (bf16[2,2048]{1,0:T(2,128)(2,1)S(1)}, bf16[2,2048]{1,0:T(2,128)(2,1)}, u32[]{:S(2)}) copy-start(bf16[2,2048]{1,0:T(2,128)(2,1)} %param.11) | copy-start | bytes 24580
  0.0 3.8 %copy-start.1 = (bf16[2048,512]{1,0:T(8,128)(2,1)S(1)}, bf16[2048,512]{1,0:T(8,128)(2,1)}, u32[]{:S(2)}) copy-start(bf16[2048,512]{1,0:T(8,128)(2,1)} %shapes.9) | copy-start | bytes 6291460
  0.0 3.8 %copy-start.5 = (s32[512]{0:T(512)S(1)}, s32[512]{0:T(512)}, u32[]{:S(2)}) copy-start(s32[512]{0:T(512)} %param.15) | copy-start | bytes 6148
  0.0 16.1 %collective-permute-start.6 = (s32[256]{0:T(256)}, s32[256]{0:T(256)S(1)}, u32[]{:S(2)}, u32[]{:S(2)}) collective-permute-start(s32[256]{0:T(256)} %param.19), channel_id=1, source_target_pairs={{0,1},{1,0},{2,3},{3,2},{4,5},{5,4},{6,7},{7,6},{8,9},{9,8},{10,11... | collective-permute-start | bytes 3080 | tf_op jit(solution)/shard_map/ppermute | solution.py:290
  3.6 5.8 %copy-start.6 = (s32[512]{0:T(512)S(1)}, s32[512]{0:T(512)}, u32[]{:S(2)}) copy-start(s32[512]{0:T(512)} %param.14) | copy-start | bytes 6148
  3.7 4.2 %collective-permute-start = (f32[2,256]{1,0:T(2,128)S(1)}, f32[2,256]{1,0:T(2,128)S(1)}, u32[]{:S(2)}, u32[]{:S(2)}) collective-permute-start(f32[2,256]{1,0:T(2,128)S(1)} %pad_maximum_fusion), channel_id=1, source_target_pairs={{0,4},{4,0},{8,12},{12,8},{16,20},{20,16},{24,28},{28,24},{32,36},... | collective-permute-start | bytes 6152 | tf_op jit(solution)/shard_map/ppermute | solution.py:61
  5.3 10.8 %copy-start.9 = (s32[256]{0:T(256)S(1)}, s32[256]{0:T(256)}, u32[]{:S(2)}) copy-start(s32[256]{0:T(256)} %param.19) | copy-start | bytes 3076
  5.3 17.5 %copy-start.3 = (s32[8,2048]{1,0:T(8,128)S(1)}, s32[8,2048]{1,0:T(8,128)}, u32[]{:S(2)}) copy-start(s32[8,2048]{1,0:T(8,128)} %links.5) | copy-start | bytes 196612
  5.3 17.5 %copy-start.4 = (bf16[8,2048]{1,0:T(8,128)(2,1)S(1)}, bf16[8,2048]{1,0:T(8,128)(2,1)}, u32[]{:S(2)}) copy-start(bf16[8,2048]{1,0:T(8,128)(2,1)} %weights.5) | copy-start | bytes 98308
  5.3 32.1 %collective-permute-start.8 = (bf16[512,512]{1,0:T(8,128)(2,1)S(1)}, bf16[512,512]{1,0:T(8,128)(2,1)S(1)}, u32[]{:S(2)}, u32[]{:S(2)}) collective-permute-start(bf16[512,512]{1,0:T(8,128)(2,1)S(1)} %shard_map.101), channel_id=1, source_target_pairs={{0,4},{4,8},{8,12},{12,16},{16,20},{20,24},{24,28},{28,32},{32,36}... | collective-permute-start | bytes 1572872 | tf_op jit(solution)/shard_map/ppermute | solution.py:68
  7.9 6.0 %collective-permute-start.1 = (f32[2,256]{1,0:T(2,128)S(1)}, f32[2,256]{1,0:T(2,128)S(1)}, u32[]{:S(2)}, u32[]{:S(2)}) collective-permute-start(f32[2,256]{1,0:T(2,128)S(1)} %fusion), channel_id=1, source_target_pairs={{0,64},{4,68},{8,72},{12,76},{16,80},{20,84},{24,88},{28,92},{32,9... | collective-permute-start | bytes 6152 | tf_op jit(solution)/shard_map/ppermute | solution.py:61
  11.0 28.4 %collective-permute-start.9 = (bf16[512,512]{1,0:T(8,128)(2,1)S(1)}, bf16[512,512]{1,0:T(8,128)(2,1)S(1)}, u32[]{:S(2)}, u32[]{:S(2)}) collective-permute-start(bf16[512,512]{1,0:T(8,128)(2,1)S(1)} %shard_map.104), channel_id=1, source_target_pairs={{4,0},{8,4},{12,8},{16,12},{20,16},{24,20},{28,24},{32,28},{36,32}... | collective-permute-start | bytes 1572872 | tf_op jit(solution)/shard_map/ppermute | solution.py:68
  13.9 4.9 %collective-permute-start.2 = (f32[2,256]{1,0:T(2,128)S(1)}, f32[2,256]{1,0:T(2,128)S(1)}, u32[]{:S(2)}, u32[]{:S(2)}) collective-permute-start(f32[2,256]{1,0:T(2,128)S(1)} %fusion.4), channel_id=1, source_target_pairs={{0,192},{4,196},{8,200},{12,204},{16,208},{20,212},{24,216},{28,22... | collective-permute-start | bytes 6152 | tf_op jit(solution)/shard_map/ppermute | solution.py:61
  16.1 10.2 %collective-permute-start.7 = (s32[512]{0:T(512)S(1)}, s32[512]{0:T(512)S(1)}, u32[]{:S(2)}, u32[]{:S(2)}) collective-permute-start(s32[512]{0:T(512)S(1)} %pad_add_fusion.1), channel_id=1, source_target_pairs={{0,3},{3,0},{1,2},{2,1},{4,7},{7,4},{5,6},{6,5},{8,11},{11,8},{9,1... | collective-permute-start | bytes 6152 | tf_op jit(solution)/shard_map/ppermute | solution.py:290
  18.8 14.9 %copy-start.2 = (f32[256,256]{1,0:T(8,128)S(1)}, f32[256,256]{1,0:T(8,128)}, u32[]{:S(2)}) copy-start(f32[256,256]{1,0:T(8,128)} %coupling.1) | copy-start | bytes 786436
  18.8 14.9 %copy-start.7 = (f32[256]{0:T(256)S(1)}, f32[256]{0:T(256)}, u32[]{:S(2)}) copy-start(f32[256]{0:T(256)} %param.16) | copy-start | bytes 3076
  18.8 14.9 %copy-start.8 = (f32[256]{0:T(256)S(1)}, f32[256]{0:T(256)}, u32[]{:S(2)}) copy-start(f32[256]{0:T(256)} %param.17) | copy-start | bytes 3076
  18.8 7.4 %collective-permute-start.3 = (f32[2,256]{1,0:T(2,128)S(1)}, f32[2,256]{1,0:T(2,128)S(1)}, u32[]{:S(2)}, u32[]{:S(2)}) collective-permute-start(f32[2,256]{1,0:T(2,128)S(1)} %add.25), channel_id=1, source_target_pairs={{0,8},{4,12},{8,0},{12,4},{16,24},{20,28},{24,16},{28,20},{32,40},... | collective-permute-start | bytes 6152 | tf_op jit(solution)/shard_map/ppermute | solution.py:61
  26.2 4.6 %collective-permute-start.4 = (f32[2,256]{1,0:T(2,128)S(1)}, f32[2,256]{1,0:T(2,128)S(1)}, u32[]{:S(2)}, u32[]{:S(2)}) collective-permute-start(f32[2,256]{1,0:T(2,128)S(1)} %add.26), channel_id=1, source_target_pairs={{0,16},{4,20},{8,24},{12,28},{16,0},{20,4},{24,8},{28,12},{32,48},... | collective-permute-start | bytes 6152 | tf_op jit(solution)/shard_map/ppermute | solution.py:61
  30.8 6.6 %collective-permute-start.5 = (f32[2,256]{1,0:T(2,128)S(1)}, f32[2,256]{1,0:T(2,128)S(1)}, u32[]{:S(2)}, u32[]{:S(2)}) collective-permute-start(f32[2,256]{1,0:T(2,128)S(1)} %add.27), channel_id=1, source_target_pairs={{0,56},{4,60},{8,48},{12,52},{16,40},{20,44},{24,32},{28,36},{32,2... | collective-permute-start | bytes 6152 | tf_op jit(solution)/shard_map/ppermute | solution.py:61

commit v2 on v0

v2 whole, which is shorter than its diff:
```python
import functools
import math

import jax
import jax.numpy as jnp
from jax import lax
from jax.experimental import pallas as pl
from jax.experimental.pallas import tpu as pltpu
from jax.sharding import PartitionSpec as P

ITERS = 6
NGRID = 4096
X, Y, Z, CORES = 4, 4, 8, 2
BLOCK = 256
WINDOW = 1280
CODE = 64
ROOM0 = 50
MICRO = 3.0
bf16 = jnp.bfloat16
f32 = jnp.float32


def mm(a, b):
    return jnp.dot(a, b, preferred_element_type=f32)


VMEM = pl.BlockSpec(memory_space=pltpu.VMEM)
SMEM = pl.BlockSpec(memory_space=pltpu.SMEM)
HBM = pl.BlockSpec(memory_space=pltpu.HBM)


def call(body, out_shape, operands, scratch=(), specs=None, microseconds=1.0, room=24):
    return pl.pallas_call(
        body,
        out_shape=out_shape,
        in_specs=specs or [VMEM] * len(operands),
        out_specs=[VMEM] * len(out_shape),
        scratch_shapes=list(scratch),
        compiler_params=pltpu.CompilerParams(vmem_limit_bytes=room << 20),
        cost_estimate=pl.CostEstimate(flops=int(1e9 * microseconds), bytes_accessed=0, transcendentals=0),
    )(*operands)


def sds(shape, dtype):
    return jax.ShapeDtypeStruct(shape, dtype)


def slab_of(x, z, c):
    return (x * Z + z) * CORES + c


def slab_pairs(partner):
    return [
        (slab_of(x, z, c), slab_of(*partner(x, z, c)))
        for x in range(X)
        for z in range(Z)
        for c in range(CORES)
    ]


CORE_PAIRS = slab_pairs(lambda x, z, c: (x, z, 1 - c))


def odd_round(partner, mirror=lambda y: y ^ 1):
    pairs = []
    for x in range(X):
        for z in range(Z):
            for y in range(Y):
                pairs.append((slab_of(x, z, 0) * Y + y, slab_of(x, z, 0) * Y + mirror(y)))
                pairs.append((slab_of(x, z, 1) * Y + y, slab_of(*partner(x, z), 1) * Y + y))
    return sorted(pairs)


ROUNDS = (
    odd_round(lambda x, z: (x ^ 1, z)),
    odd_round(lambda x, z: (3 - x, z), lambda y: 3 - y),
    odd_round(lambda x, z: (x, z ^ 1)),
    odd_round(lambda x, z: (x, z ^ 2)),
    odd_round(lambda x, z: (x, 7 - z)),
)
N_SLAB = X * Z * CORES
FAR_PAIRS = [
    (j * Y + y, (j + 1 if j % 2 else j - 1) * Y + y) if 0 < j < N_SLAB - 1 else (j * Y + y, j * Y + (y ^ 1))
    for j in range(N_SLAB)
    for y in range(Y)
]


def first_body(unbalance, shapes, message, shapes_t, landing, load, sems):
    rows, width = shapes.shape
    parts = sems.shape[0] - 1
    step = rows // parts
    load_copy = pltpu.make_async_copy(unbalance, load, sems.at[parts])
    load_copy.start()
    copies = []
    for p in range(parts):
        s = pl.ds(p * step, step)
        copy = pltpu.make_async_copy(shapes.at[s, :], landing.at[s, :], sems.at[p])
        copy.start()
        copies.append(copy)
    load_copy.wait()
    total = jnp.zeros((load.shape[0], width), f32)
    for p in range(parts):
        copies[p].wait()
        block = landing[p * step : (p + 1) * step, :]
        total += mm(load[:, p * step : (p + 1) * step], block)
        shapes_t[:, p * step : (p + 1) * step] = jnp.transpose(block)
    half = width // 2
    message[0:1, :] = total[0:1, :half] - total[1:2, half:]
    message[1:2, :] = total[0:1, half:] + total[1:2, :half]


def first(unbalance, shapes):
    rows, width = shapes.shape
    parts = 8
    return call(
        first_body,
        [sds((2, width // 2), f32), sds((width, rows), bf16)],
        (unbalance, shapes),
        [
            pltpu.VMEM((rows, width), bf16),
            pltpu.VMEM(unbalance.shape, bf16),
            pltpu.SemaphoreType.DMA((parts + 1,)),
        ],
        [HBM, HBM],
        1.5,
        ROOM0,
    )


def gather_rows(nodes, one, shapes_t, table):
    rows = shapes_t.shape[1]
    count = nodes.shape[1]
    here = jnp.broadcast_to(nodes.astype(jnp.int16), (16, count))
    row = lax.broadcasted_iota(jnp.int16, (16, count), 0)
    zero = jnp.zeros((16, count), bf16)
    for r in range(0, rows, 16):
        table[r : r + 16, :] = jnp.where(here == row + jnp.int16(r), one, zero)
    return mm(shapes_t[...], table[...]).astype(bf16)


def near_gather_body(place, message_in, low, high, shapes_t, message_out, out, table):
    width = shapes_t.shape[0]
    nodes = jnp.where(place[0] == 0, high[...], low[...])
    one = jnp.ones((16, nodes.shape[1]), bf16)
    out[:width, :] = gather_rows(nodes, one, shapes_t, table)
    index = message_in[3:4, :].astype(jnp.int32)
    coarse = index // CODE
    fine = index - coarse * CODE
    row = jnp.concatenate([coarse.astype(f32), fine.astype(f32)], 1)
    out[width:, :] = jnp.broadcast_to(row, (16, row.shape[1])).astype(bf16)
    message_out[...] = message_in[...]


def far_gather_body(place, message_in, low, high, shapes_t, message_out, out, table):
    nodes = jnp.where(place[0] == 0, low[...], high[...])
    one = jnp.full((16, nodes.shape[1]), jnp.where(place[1] == 0, 1.0, 0.0), f32).astype(bf16)
    out[...] = gather_rows(nodes, one, shapes_t, table)
    message_out[...] = message_in[...]


def fill_table(table, links, weights, start):
    corners, count = links.shape
    here = (links - start).astype(jnp.int16)
    here = [jnp.broadcast_to(here[k : k + 1, :], (16, count)) for k in range(corners)]
    value = [jnp.broadcast_to(weights[k : k + 1, :], (16, count)) for k in range(corners)]
    row = lax.broadcasted_iota(jnp.int16, (16, count), 0)
    for r in range(0, WINDOW, 16):
        at = row + jnp.int16(r)
        entry = jnp.zeros((16, count), bf16)
        for k in range(corners):
            entry = jnp.where(here[k] == at, value[k], entry)
        table[r : r + 16, :] = entry


def middle_body(force_in, links, weights, shapes_t, force_out, out, tables, *, blocks):
    for i, b in enumerate(blocks):
        s = slice(b * BLOCK, (b + 1) * BLOCK)
        fill_table(tables.at[i % 2], links[:, s], weights[:, s], b * BLOCK)
        start = (b - 2) * BLOCK
        modes = mm(shapes_t[:, start : start + WINDOW], tables[i % 2])
        out[:, i * BLOCK : (i + 1) * BLOCK] = modes.astype(bf16)
    force_out[...] = force_in[...]


def end_body(place, force_in, links, weights, shapes_t, halo, force_out, out, window, tables, *, low_core):
    width, rows = shapes_t.shape
    reach = halo.shape[1]
    own = 1024

    low = place[0] == low_core

    @pl.when(low)
    def _():
        window[:, :reach] = halo[:width, :]
        window[:, reach:] = shapes_t[:, :own]

    @pl.when(jnp.logical_not(low))
    def _():
        window[:, :own] = shapes_t[:, rows - own :]
        window[:, own:] = halo[:width, :]

    base = jnp.where(low, 0, rows - 2 * BLOCK)
    for i in range(2):
        start = pl.multiple_of(base + i * BLOCK, BLOCK)
        fill_table(tables.at[i], links[:, pl.ds(start, BLOCK)], weights[:, pl.ds(start, BLOCK)], start)
        modes = mm(window[:, i * BLOCK : i * BLOCK + WINDOW], tables[i])
        out[:, i * BLOCK : (i + 1) * BLOCK] = modes.astype(bf16)
    force_out[...] = force_in[...]


def split(x):
    high = x.astype(bf16)
    return high, (x - high.astype(f32)).astype(bf16)


def prepare_body(
    place, message_in, speeds, there, halo, freq, damping, coupling, message_out, u_re, u_im, omega_out, c_high, c_low
):
    count = freq.shape[1]
    total = u_re.shape[0]
    tail = halo[halo.shape[0] - 16 :, :].astype(f32)
    tail = tail[0:1, : total // 2] * CODE + tail[0:1, total // 2 :]
    odd = jnp.concatenate([speeds[...].astype(f32), tail], 1)
    even = jnp.concatenate([there[2:3, :], there[3:4, :]], 1)
    index = jnp.where(place[0] == 0, even, odd)
    message_out[...] = message_in[...]
    omega = 0.25 + 4.0 * index / NGRID
    omega = jnp.transpose(jnp.broadcast_to(omega, (8, total)))[:, 0:1]
    omega = jnp.broadcast_to(omega, (total, count))
    f = freq[...]
    zeta = damping[...]
    d_re = f * f - omega * omega
    d_im = 2.0 * (zeta * f) * omega
    scale = omega / (d_re * d_re + d_im * d_im)
    u_re[...] = d_re * scale
    u_im[...] = d_im * scale
    omega_out[...] = omega[:, :128]
    i = lax.broadcasted_iota(jnp.int32, (count, count), 0)
    j = lax.broadcasted_iota(jnp.int32, (count, count), 1)
    coupled = jnp.transpose(coupling[...]) * (zeta * f * (1.5 / math.sqrt(count)))
    c_high[...], c_low[...] = split(jnp.where(i == j, 0.0, coupled))


def prepare(place, message, speeds, there, halo, freq, damping, coupling):
    total, count = 2 * speeds.shape[1], freq.shape[0]
    operands = (place, message, speeds, there, halo, freq.reshape(1, count), damping.reshape(1, count), coupling)
    return call(
        prepare_body,
        [
            sds(message.shape, f32),
            sds((total, count), f32),
            sds((total, count), f32),
            sds((total, 128), f32),
            sds((count, count), bf16),
            sds((count, count), bf16),
        ],
        operands,
        specs=[SMEM] + [VMEM] * 7,
        microseconds=0.9,
    )


def solve_body(place, mine, other, u_re, u_im, omega, c_high, c_low, out):
    force = jnp.where(place[0] == 1, mine[...], other[...])
    f_re, f_im = force[0:1, :], force[1:2, :]
    ch, cl = c_high[...], c_low[...]

    def coupled(y):
        high, low = split(y)
        return mm(high, ch) + (mm(low, ch) + mm(high, cl))

    total, count = u_re.shape
    tile = 256
    tiles = [pl.ds(t, tile) for t in range(0, total, tile)]
    state = []
    for s in tiles:
        ur, ui = u_re[s, :], u_im[s, :]
        state.append((f_re * ur + f_im * ui, f_im * ur - f_re * ui))
    for sweep in range(ITERS):
        after = []
        for s, (yr, yi) in zip(tiles, state):
            pr, pi = coupled(yr), coupled(yi)
            ur, ui = u_re[s, :], u_im[s, :]
            top_re, top_im = f_re + pi, f_im - pr
            after.append((top_re * ur + top_im * ui, top_im * ur - top_re * ui))
        state = after
    for s, (yr, yi) in zip(tiles, state):
        w = jnp.concatenate([omega[s, :]] * (count // 128), 1)
        out[s, :count] = (yr * w).astype(bf16)
        out[s, count:] = (yi * w).astype(bf16)


def solve(place, mine, other, prepared):
    total, count = prepared[0].shape
    operands = (place, mine, other, *prepared)
    return call(
        solve_body, [sds((total, 2 * count), bf16)], operands, specs=[SMEM] + [VMEM] * 7, microseconds=4.0
    )[0]


def peaks_tile(coords, modes, for_re, for_im):
    total, twice = coords.shape
    tile = 256
    best = jnp.zeros((8, modes.shape[1]), f32)
    for s in range(0, total, tile):
        re = mm(for_re[s : s + tile, :], modes)
        im = mm(for_im[s : s + tile, :], modes)
        square = re * re + im * im
        best = jnp.maximum(best, jnp.max(square.reshape(tile // 8, 8, modes.shape[1]), axis=0))
    return best


def parts_of(parts):
    at = 0
    for part in parts:
        for e in range(0, part.shape[1], BLOCK):
            yield at, part, e
            at += BLOCK


def half_peaks_body(coords, far, middle_a, middle_b, near, best, for_re, for_im):
    spread(coords, for_re, for_im)
    for at, part, e in parts_of((far, middle_a, middle_b, near)):
        best[:, at : at + BLOCK] = peaks_tile(coords, part[:, e : e + BLOCK], for_re, for_im)


def spread(coords, for_re, for_im):
    count = coords.shape[1] // 2
    re, im = coords[:, :count], coords[:, count:]
    for_re[:, :count] = re
    for_re[:, count:] = -im
    for_im[:, :count] = im
    for_im[:, count:] = re


def all_peaks_body(place, coords, before, far, middle_a, middle_b, near, out, for_re, for_im):
    spread(coords, for_re, for_im)
    rows = out.shape[1]
    end = far.shape[1]
    even = place[0] == 0
    for at, part, e in parts_of((far, middle_a, middle_b, near)):
        best = jnp.maximum(before[:, at : at + BLOCK], peaks_tile(coords, part[:, e : e + BLOCK], for_re, for_im))
        peak = jnp.sqrt(jnp.max(best, axis=0, keepdims=True))
        to = at
        if part is far:
            to = jnp.where(even, at, at + rows - end)
        if part is near:
            to = jnp.where(even, at, at - rows + end)
        out[0:1, pl.ds(pl.multiple_of(to, BLOCK), BLOCK)] = peak


def peaks(place, coords, parts):
    total, twice = coords.shape
    rows = sum(p.shape[1] for p in parts)
    there = lax.ppermute(coords, "slab", CORE_PAIRS)
    scratch = [pltpu.VMEM((total, twice), bf16)] * 2
    best = call(half_peaks_body, [sds((8, rows), f32)], (coords, *parts), scratch, microseconds=2.5)[0]
    out = call(
        all_peaks_body,
        [sds((1, rows), f32)],
        (place, there, best, *parts),
        scratch,
        [SMEM] + [VMEM] * 6,
        2.5,
    )[0]
    return out.reshape(rows)


def on_device(
    mode_shapes,
    unbalance,
    connectivity,
    stress_weights,
    face_low_nodes,
    face_high_nodes,
    natural_freq,
    damping_ratio,
    coupling,
    speed_index,
):
    rows, width = mode_shapes.shape
    reach = face_low_nodes.shape[0]
    slab = lax.axis_index("slab")
    edge = jnp.logical_or(slab == 0, slab == N_SLAB - 1)
    place = jnp.stack([slab % CORES, edge.astype(jnp.int32)]).astype(jnp.int32)
    low = face_low_nodes.reshape(1, reach)
    high = face_high_nodes.reshape(1, reach)

    speeds = speed_index.reshape(1, -1)
    force, shapes_t = first(unbalance, mode_shapes)
    small = sds((2, width // 2), f32)
    letter = sds((4, width // 2), f32)
    tables = pltpu.VMEM((2, WINDOW, BLOCK), bf16)
    table = pltpu.VMEM((rows, reach), bf16)

    def swap(x, number):
        return lax.ppermute(x, ("slab", "spd"), ROUNDS[number])

    def middle(blocks, force):
        return call(
            functools.partial(middle_body, blocks=blocks),
            [sds(force.shape, f32), sds((width, len(blocks) * BLOCK), bf16)],
            (force, connectivity, stress_weights, shapes_t),
            [tables],
            microseconds=MICRO * 1.2,
        )

    def end(halo, low_core, force):
        return call(
            functools.partial(end_body, low_core=low_core),
            [small, sds((width, 2 * BLOCK), bf16)],
            (place, force, connectivity, stress_weights, shapes_t, halo),
            [pltpu.VMEM((width, 3 * reach), bf16), tables],
            [SMEM] + [VMEM] * 5,
            MICRO * 1.6,
        )

    arrived = lax.ppermute(force, "slab", CORE_PAIRS)
    force, far_rows = call(
        far_gather_body,
        [small, sds((width, reach), bf16)],
        (place, force, low, high, shapes_t),
        [table],
        [SMEM] + [VMEM] * 4,
        MICRO * 1.8,
    )
    far_halo = lax.ppermute(far_rows, ("slab", "spd"), FAR_PAIRS)
    own = speeds.astype(f32)
    message = jnp.concatenate([force + arrived, own, own])
    arrived = swap(message, 0)
    message, middle_a = middle((2, 3), message)
    message = jnp.concatenate([message[:2] + arrived[:2], message[2:3], arrived[2:3]])
    there = swap(message, 1)
    message, near_rows = call(
        near_gather_body,
        [letter, sds((width + 16, reach), bf16)],
        (place, message, low, high, shapes_t),
        [table],
        [SMEM] + [VMEM] * 4,
        MICRO * 1.8,
    )
    near_halo = lax.ppermute(near_rows, "slab", CORE_PAIRS)
    force = message[:2] + there[:2]
    arrived = swap(force, 2)
    force, middle_b = middle((4, 5), force)
    force = force + arrived
    arrived = swap(force, 3)
    force, near = end(near_halo, 1, force)
    force, *prepared = prepare(place, force, speeds, there, near_halo, natural_freq, damping_ratio, coupling)
    force = force + arrived
    arrived = swap(force, 4)
    force, far = end(far_halo, 0, force)
    force = force + arrived
    coords = solve(place, force, lax.ppermute(force, "slab", CORE_PAIRS), prepared)
    return peaks(place, coords, (far, middle_a, middle_b, near))


def solution(mesh):
    return jax.shard_map(
        on_device,
        mesh=mesh,
        in_specs=(
            P("slab", None),
            P(None, "slab"),
            P(None, "slab"),
            P(None, "slab"),
            P("slab"),
            P("slab"),
            P(),
            P(),
            P(),
            P("spd"),
        ),
        out_specs=P("slab"),
        check_vma=False,
    )
```

time: 263 us -> 44.4 us (0.17)
  the two profiles are of different devices: /device:TPU:0 before, /device:TPU:1 now
where the time goes in v2:
time: 44.4 us; the launch traced here: 44.2 us
  Pallas kernels  22 us (50%)
  starting transfers between devices  17.8 us (40%)
  waiting for transfers between devices  3.36 us (8%)
  local copies, waits for them, and re-layouts  0.74 us (2%)
    pallas_call x11, Pallas kernels, call(): pl.pallas_call(body, out_shape=out_shape, in_specs=specs or [VMEM] * len(...  22 us
    ppermute x1, starting transfers between devices, on_device(): near_halo = lax.ppermute(near_rows, 'slab', CORE_PAIRS)  5.74 us
    ppermute x5, starting transfers between devices, swap(): return lax.ppermute(x, ('slab', 'spd'), ROUNDS[number])  5.27 us
    ppermute x1, starting transfers between devices, on_device(): arrived = lax.ppermute(force, 'slab', CORE_PAIRS)  3.33 us
    ppermute x1, starting transfers between devices, on_device(): lax.ppermute(force, 'slab', CORE_PAIRS)  2.98 us
    ppermute x5, waiting for transfers between devices, swap(): return lax.ppermute(x, ('slab', 'spd'), ROUNDS[number])  2.53 us
  transfers between devices with their start and end apart: 10, of which 5 were waited for; matrix products, arithmetic and copies ran while one was open for 0% of the time, Pallas kernels for 28%

profile of v2, /device:TPU:1, one launch (start us, length us, event | category | flops | bytes accessed | tf_op | source)
XLA Modules:
  0.0 44.2 jit_solution(9148998191349383053)
XLA Ops:
  0.0 0.0 copy-start.4
  0.0 0.7 %copy-done.4 = bf16[2,2048]{1,0:T(2,128)(2,1)S(1)} copy-done((bf16[2,2048]{1,0:T(2,128)(2,1)S(1)}, bf16[2,2048]{1,0:T(2,128)(2,1)}, u32[]{:S(2)}) %copy-start.4) | copy-done | bytes 8216
  0.7 0.0 copy-start.5
  0.7 0.0 copy-start.6
  0.7 2.1 %shard_map.100 = (f32[2,256]{1,0:T(2,128)S(1)}, bf16[512,2048]{1,0:T(8,128)(2,1)S(1)}) custom-call(bf16[2,2048]{1,0:T(2,128)(2,1)S(1)} %copy-done.4, bf16[2048,512]{1,0:T(8,128)(2,1)} %shapes.1), custom_call_target="tpu_custom_call" | custom-call | flops 1500000000 | tf_op jit(solution)/shard_map/pallas_call | solution.py:33
  2.8 3.3 %collective-permute-start = (f32[2,256]{1,0:T(2,128)S(1)}, f32[2,256]{1,0:T(2,128)S(1)}, u32[]{:S(2)}, u32[]{:S(2)}) collective-permute-start(f32[2,256]{1,0:T(2,128)S(1)} %get-tuple-element.25.message_in), channel_id=1, source_target_pairs={{0,4},{4,0},{8,12},{12,8},{16,20},{20,16},{24,28},{28,24},{32,36},... | collective-permute-start | bytes 6152 | tf_op jit(solution)/shard_map/ppermute | solution.py:419
  6.1 0.1 pad_add_fusion.place
  6.2 0.0 copy-done.5
  6.2 0.0 copy-done.6
  6.2 0.0 copy-start
  6.2 0.0 copy-start.2
  6.2 0.0 copy-start.3
  6.2 1.8 %shard_map.101 = (f32[2,256]{1,0:T(2,128)S(1)}, bf16[512,512]{1,0:T(8,128)(2,1)S(1)}) custom-call(s32[2]{0:T(128)S(1)} %pad_add_fusion.place, f32[2,256]{1,0:T(2,128)S(1)} %get-tuple-element.25.message_in, s32[1,512]{1,0:T(1,128)S(1)} %bitcast.10, s32[1,512]{1,0:T(1,128)S(1)} %bitcast.12, bf16[512,2048]{1,0:T(8,128)(2,1)S(1)} %get-tuple-element.26.shapes_t), custom_call_target="tpu_custom_call" | custom-call | flops 5400000000 | tf_op jit(solution)/shard_map/pallas_call | solution.py:33
  8.1 0.1 collective-permute-start.6
  8.2 0.0 copy-done
  8.2 0.0 collective-permute-done
  8.2 1.1 %collective-permute-start.1 = (f32[4,256]{1,0:T(4,128)S(1)}, f32[4,256]{1,0:T(4,128)S(1)}, u32[]{:S(2)}, u32[]{:S(2)}) collective-permute-start(f32[4,256]{1,0:T(4,128)S(1)} %pad_maximum_fusion.force_in), channel_id=1, source_target_pairs={{0,1},{1,0},{2,3},{3,2},{4,68},{5,69},{6,70},{7,71},{8,9},{9,8},{1... | collective-permute-start | bytes 12296 | tf_op jit(solution)/shard_map/ppermute | solution.py:398
  9.3 0.0 copy-done.2
  9.3 0.0 copy-done.3
  9.3 1.1 %shard_map.102 = (f32[4,256]{1,0:T(4,128)S(1)}, bf16[512,512]{1,0:T(8,128)(2,1)S(1)}) custom-call(f32[4,256]{1,0:T(4,128)S(1)} %pad_maximum_fusion.force_in, s32[8,2048]{1,0:T(8,128)S(1)} %copy-done.2, bf16[8,2048]{1,0:T(8,128)(2,1)S(1)} %copy-done.3, bf16[512,2048]{1,0:T(8,128)(2,1)S(1)} %get-tuple-element.26.shapes_t), custom_call_target="tpu_custom_call" | custom-call | flops 3600000000 | tf_op jit(solution)/shard_map/pallas_call | solution.py:33
  10.5 0.3 collective-permute-done.1
  10.8 2.3 %collective-permute-start.2 = (f32[4,256]{1,0:T(4,128)S(1)}, f32[4,256]{1,0:T(4,128)S(1)}, u32[]{:S(2)}, u32[]{:S(2)}) collective-permute-start(f32[4,256]{1,0:T(4,128)S(1)} %pad_maximum_fusion.1.message_in), channel_id=1, source_target_pairs={{0,3},{1,2},{2,1},{3,0},{4,196},{5,197},{6,198},{7,199},{8,11},{9,... | collective-permute-start | bytes 12296 | tf_op jit(solution)/shard_map/ppermute | solution.py:398
  13.1 1.8 %shard_map.103 = (f32[4,256]{1,0:T(4,128)S(1)}, bf16[528,512]{1,0:T(8,128)(2,1)S(1)}) custom-call(s32[2]{0:T(128)S(1)} %pad_add_fusion.place, f32[4,256]{1,0:T(4,128)S(1)} %pad_maximum_fusion.1.message_in, s32[1,512]{1,0:T(1,128)S(1)} %bitcast.11, s32[1,512]{1,0:T(1,128)S(1)} %bitcast.13, bf16[512,2048]{1,0:T(8,128)(2,1)S(1)} %get-tuple-element.26.shapes_t), custom_call_target="tpu_custom_call" | custom-call | flops 5400000000 | tf_op jit(solution)/shard_map/pallas_call | solution.py:33
  14.9 5.7 %collective-permute-start.4 = (bf16[528,512]{1,0:T(8,128)(2,1)S(1)}, bf16[528,512]{1,0:T(8,128)(2,1)S(1)}, u32[]{:S(2)}, u32[]{:S(2)}) collective-permute-start(bf16[528,512]{1,0:T(8,128)(2,1)S(1)} %get-tuple-element.31), channel_id=1, source_target_pairs={{0,4},{4,0},{8,12},{12,8},{16,20},{20,16},{24,28},{28,24},{32,36},... | collective-permute-start | bytes 1622024 | tf_op jit(solution)/shard_map/ppermute | solution.py:443
  20.7 0.0 collective-permute-done.2.there
  20.7 0.0 collective-permute-start.3
  20.7 1.1 %shard_map.104 = (f32[2,256]{1,0:T(2,128)S(1)}, bf16[512,512]{1,0:T(8,128)(2,1)S(1)}) custom-call(f32[2,256]{1,0:T(2,128)S(1)} %slice_add_fusion.force_in, s32[8,2048]{1,0:T(8,128)S(1)} %copy-done.2, bf16[8,2048]{1,0:T(8,128)(2,1)S(1)} %copy-done.3, bf16[512,2048]{1,0:T(8,128)(2,1)S(1)} %get-tuple-element.26.shapes_t), custom_call_target="tpu_custom_call" | custom-call | flops 3600000000 | tf_op jit(solution)/shard_map/pallas_call | solution.py:33
  21.8 1.3 %collective-permute-done.3 = f32[2,256]{1,0:T(2,128)S(1)} collective-permute-done((f32[2,256]{1,0:T(2,128)S(1)}, f32[2,256]{1,0:T(2,128)S(1)}, u32[]{:S(2)}, u32[]{:S(2)}) %collective-permute-start.3) | collective-permute-done | bytes 2080 | tf_op jit(solution)/shard_map/ppermute | solution.py:398
  23.1 0.0 copy-start.1
  23.1 0.0 copy-start.7
  23.1 0.0 copy-start.8
  23.1 0.1 collective-permute-start.5
  23.2 0.0 collective-permute-done.4.halo
  23.2 1.6 %shard_map.105 = (f32[2,256]{1,0:T(2,128)S(1)}, bf16[512,512]{1,0:T(8,128)(2,1)S(1)}) custom-call(s32[2]{0:T(128)S(1)} %pad_add_fusion.place, f32[2,256]{1,0:T(2,128)S(1)} %add.26.force_in, s32[8,2048]{1,0:T(8,128)S(1)} %copy-done.2, bf16[8,2048]{1,0:T(8,128)(2,1)S(1)} %copy-done.3, bf16[512,2048]{1,0:T(8,128)(2,1)S(1)} %get-tuple-element.26.shapes_t, ...), custom_call_target="tpu_custom_call" | custom-call | flops 4800000000 | tf_op jit(solution)/shard_map/pallas_call | solution.py:33
  24.9 0.0 copy-done.1
  24.9 0.0 copy-done.7
  24.9 0.0 copy-done.8
  24.9 0.9 %shard_map.106 = (f32[2,256]{1,0:T(2,128)S(1)}, f32[512,256]{1,0:T(8,128)S(1)}, f32[512,256]{1,0:T(8,128)S(1)}, f32[512,128]{1,0:T(8,128)S(1)}, bf16[256,256]{1,...) custom-call(s32[2]{0:T(128)S(1)} %pad_add_fusion.place, f32[2,256]{1,0:T(2,128)S(1)} %get-tuple-element.32.message_in, ...), custom_call_target="tpu_custom_call" | custom-call | flops 900000000 | tf_op jit(solution)/shard_map/pallas_call | solution.py:33
  25.9 0.7 %collective-permute-done.5 = f32[2,256]{1,0:T(2,128)S(1)} collective-permute-done((f32[2,256]{1,0:T(2,128)S(1)}, f32[2,256]{1,0:T(2,128)S(1)}, u32[]{:S(2)}, u32[]{:S(2)}) %collective-permute-start.5) | collective-permute-done | bytes 2080 | tf_op jit(solution)/shard_map/ppermute | solution.py:398
  26.6 1.7 %collective-permute-start.7 = (f32[2,256]{1,0:T(2,128)S(1)}, f32[2,256]{1,0:T(2,128)S(1)}, u32[]{:S(2)}, u32[]{:S(2)}) collective-permute-start(f32[2,256]{1,0:T(2,128)S(1)} %add.27.force_in), channel_id=1, source_target_pairs={{0,1},{1,0},{2,3},{3,2},{4,60},{5,61},{6,62},{7,63},{8,9},{9,8},{1... | collective-permute-start | bytes 6152 | tf_op jit(solution)/shard_map/ppermute | solution.py:398
  28.3 0.0 collective-permute-done.6.halo
  28.3 1.6 %shard_map.107 = (f32[2,256]{1,0:T(2,128)S(1)}, bf16[512,512]{1,0:T(8,128)(2,1)S(1)}) custom-call(s32[2]{0:T(128)S(1)} %pad_add_fusion.place, f32[2,256]{1,0:T(2,128)S(1)} %add.27.force_in, s32[8,2048]{1,0:T(8,128)S(1)} %copy-done.2, bf16[8,2048]{1,0:T(8,128)(2,1)S(1)} %copy-done.3, bf16[512,2048]{1,0:T(8,128)(2,1)S(1)} %get-tuple-element.26.shapes_t, ...), custom_call_target="tpu_custom_call" | custom-call | flops 4800000000 | tf_op jit(solution)/shard_map/pallas_call | solution.py:33
  29.9 0.3 collective-permute-done.7
  30.2 3.0 %collective-permute-start.8 = (f32[2,256]{1,0:T(2,128)S(1)}, f32[2,256]{1,0:T(2,128)S(1)}, u32[]{:S(2)}, u32[]{:S(2)}) collective-permute-start(f32[2,256]{1,0:T(2,128)S(1)} %add.28.mine), channel_id=1, source_target_pairs={{0,4},{4,0},{8,12},{12,8},{16,20},{20,16},{24,28},{28,24},{32,36},... | collective-permute-start | bytes 6152 | tf_op jit(solution)/shard_map/ppermute | solution.py:455
  33.2 0.8 %collective-permute-done.8.other = f32[2,256]{1,0:T(2,128)S(1)} collective-permute-done((f32[2,256]{1,0:T(2,128)S(1)}, f32[2,256]{1,0:T(2,128)S(1)}, u32[]{:S(2)}, u32[]{:S(2)}) %collective-permute-start.8) | collective-permute-done | bytes 2080 | tf_op jit(solution)/shard_map/ppermute | solution.py:455
  34.0 3.9 %shard_map.108.coords = bf16[512,512]{1,0:T(8,128)(2,1)S(1)} custom-call(s32[2]{0:T(128)S(1)} %pad_add_fusion.place, f32[2,256]{1,0:T(2,128)S(1)} %add.28.mine, f32[2,256]{1,0:T(2,128)S(1)} %collective-permute-done.8.other, f32[512,256]{1,0:T(8,128)S(1)} %get-tuple-element.36.u_re, f32[512,256]{1,0:T(8,128)S(1)} %get-tuple-element.37.u_im, ...), custom_call_target="tpu_custom_call" | custom-call | flops 4000000000 | tf_op jit(solution)/shard_map/pallas_call | solution.py:33
  37.9 0.4 collective-permute-start.9
  38.3 2.4 %shard_map.109.before = f32[8,2048]{1,0:T(8,128)S(1)} custom-call(bf16[512,512]{1,0:T(8,128)(2,1)S(1)} %shard_map.108.coords, bf16[512,512]{1,0:T(8,128)(2,1)S(1)} %get-tuple-element.41.far, bf16[512,512]{1,0:T(8,128)(2,1)S(1)} %get-tuple-element.42.middle_a, bf16[512,512]{1,0:T(8,128)(2,1)S(1)} %get-tuple-element.43.middle_b, ...), custom_call_target="tpu_custom_call" | custom-call | flops 2500000000 | tf_op jit(solution)/shard_map/pallas_call | solution.py:33
  40.7 0.0 collective-permute-done.9.coords
  40.7 3.5 %shard_map.110 = f32[1,2048]{1,0:T(1,128)} custom-call(s32[2]{0:T(128)S(1)} %pad_add_fusion.place, bf16[512,512]{1,0:T(8,128)(2,1)S(1)} %collective-permute-done.9.coords, f32[8,2048]{1,0:T(8,128)S(1)} %shard_map.109.before, bf16[512,512]{1,0:T(8,128)(2,1)S(1)} %get-tuple-element.41.far, bf16[512,512]{1,0:T(8,128)(2,1)S(1)} %get-tuple-element.42.middle_a, ...), custom_call_target="tpu_custom_call" | custom-call | flops 2500000000 | tf_op jit(solution)/shard_map/pallas_call | solution.py:33
  (11 shorter events, 0.1 us)
Async XLA Ops:
  0.0 0.7 %copy-start.4 = (bf16[2,2048]{1,0:T(2,128)(2,1)S(1)}, bf16[2,2048]{1,0:T(2,128)(2,1)}, u32[]{:S(2)}) copy-start(bf16[2,2048]{1,0:T(2,128)(2,1)} %unbalance.1) | copy-start | bytes 24580
  0.7 5.5 %copy-start.5 = (s32[512]{0:T(512)S(1)}, s32[512]{0:T(512)}, u32[]{:S(2)}) copy-start(s32[512]{0:T(512)} %param.14) | copy-start | bytes 6148
  0.7 5.5 %copy-start.6 = (s32[512]{0:T(512)S(1)}, s32[512]{0:T(512)}, u32[]{:S(2)}) copy-start(s32[512]{0:T(512)} %param.15) | copy-start | bytes 6148
  2.8 5.4 %collective-permute-start = (f32[2,256]{1,0:T(2,128)S(1)}, f32[2,256]{1,0:T(2,128)S(1)}, u32[]{:S(2)}, u32[]{:S(2)}) collective-permute-start(f32[2,256]{1,0:T(2,128)S(1)} %get-tuple-element.25.message_in), channel_id=1, source_target_pairs={{0,4},{4,0},{8,12},{12,8},{16,20},{20,16},{24,28},{28,24},{32,36},... | collective-permute-start | bytes 6152 | tf_op jit(solution)/shard_map/ppermute | solution.py:419
  6.2 1.9 %copy-start = (s32[256]{0:T(256)S(1)}, s32[256]{0:T(256)}, u32[]{:S(2)}) copy-start(s32[256]{0:T(256)} %param.19) | copy-start | bytes 3076
  6.2 3.1 %copy-start.2 = (s32[8,2048]{1,0:T(8,128)S(1)}, s32[8,2048]{1,0:T(8,128)}, u32[]{:S(2)}) copy-start(s32[8,2048]{1,0:T(8,128)} %links.7) | copy-start | bytes 196612
  6.2 3.1 %copy-start.3 = (bf16[8,2048]{1,0:T(8,128)(2,1)S(1)}, bf16[8,2048]{1,0:T(8,128)(2,1)}, u32[]{:S(2)}) copy-start(bf16[8,2048]{1,0:T(8,128)(2,1)} %weights.7) | copy-start | bytes 98308
  8.1 20.2 %collective-permute-start.6 = (bf16[512,512]{1,0:T(8,128)(2,1)S(1)}, bf16[512,512]{1,0:T(8,128)(2,1)S(1)}, u32[]{:S(2)}, u32[]{:S(2)}) collective-permute-start(bf16[512,512]{1,0:T(8,128)(2,1)S(1)} %get-tuple-element.34), channel_id=1, source_target_pairs={{0,1},{1,0},{2,3},{3,2},{4,8},{5,9},{6,10},{7,11},{8,4},{9,5},{10,... | collective-permute-start | bytes 1572872 | tf_op jit(solution)/shard_map/ppermute | solution.py:428
  8.2 2.5 %collective-permute-start.1 = (f32[4,256]{1,0:T(4,128)S(1)}, f32[4,256]{1,0:T(4,128)S(1)}, u32[]{:S(2)}, u32[]{:S(2)}) collective-permute-start(f32[4,256]{1,0:T(4,128)S(1)} %pad_maximum_fusion.force_in), channel_id=1, source_target_pairs={{0,1},{1,0},{2,3},{3,2},{4,68},{5,69},{6,70},{7,71},{8,9},{9,8},{1... | collective-permute-start | bytes 12296 | tf_op jit(solution)/shard_map/ppermute | solution.py:398
  10.8 9.9 %collective-permute-start.2 = (f32[4,256]{1,0:T(4,128)S(1)}, f32[4,256]{1,0:T(4,128)S(1)}, u32[]{:S(2)}, u32[]{:S(2)}) collective-permute-start(f32[4,256]{1,0:T(4,128)S(1)} %pad_maximum_fusion.1.message_in), channel_id=1, source_target_pairs={{0,3},{1,2},{2,1},{3,0},{4,196},{5,197},{6,198},{7,199},{8,11},{9,... | collective-permute-start | bytes 12296 | tf_op jit(solution)/shard_map/ppermute | solution.py:398
  14.9 8.3 %collective-permute-start.4 = (bf16[528,512]{1,0:T(8,128)(2,1)S(1)}, bf16[528,512]{1,0:T(8,128)(2,1)S(1)}, u32[]{:S(2)}, u32[]{:S(2)}) collective-permute-start(bf16[528,512]{1,0:T(8,128)(2,1)S(1)} %get-tuple-element.31), channel_id=1, source_target_pairs={{0,4},{4,0},{8,12},{12,8},{16,20},{20,16},{24,28},{28,24},{32,36},... | collective-permute-start | bytes 1622024 | tf_op jit(solution)/shard_map/ppermute | solution.py:443
  20.7 2.4 %collective-permute-start.3 = (f32[2,256]{1,0:T(2,128)S(1)}, f32[2,256]{1,0:T(2,128)S(1)}, u32[]{:S(2)}, u32[]{:S(2)}) collective-permute-start(f32[2,256]{1,0:T(2,128)S(1)} %slice_add_fusion.force_in), channel_id=1, source_target_pairs={{0,1},{1,0},{2,3},{3,2},{4,12},{5,13},{6,14},{7,15},{8,9},{9,8},{1... | collective-permute-start | bytes 6152 | tf_op jit(solution)/shard_map/ppermute | solution.py:398
  23.1 1.8 %copy-start.1 = (f32[256,256]{1,0:T(8,128)S(1)}, f32[256,256]{1,0:T(8,128)}, u32[]{:S(2)}) copy-start(f32[256,256]{1,0:T(8,128)} %coupling.1) | copy-start | bytes 786436
  23.1 1.8 %copy-start.7 = (f32[256]{0:T(256)S(1)}, f32[256]{0:T(256)}, u32[]{:S(2)}) copy-start(f32[256]{0:T(256)} %param.16) | copy-start | bytes 3076
  23.1 1.8 %copy-start.8 = (f32[256]{0:T(256)S(1)}, f32[256]{0:T(256)}, u32[]{:S(2)}) copy-start(f32[256]{0:T(256)} %param.17) | copy-start | bytes 3076
  23.1 3.4 %collective-permute-start.5 = (f32[2,256]{1,0:T(2,128)S(1)}, f32[2,256]{1,0:T(2,128)S(1)}, u32[]{:S(2)}, u32[]{:S(2)}) collective-permute-start(f32[2,256]{1,0:T(2,128)S(1)} %add.26.force_in), channel_id=1, source_target_pairs={{0,1},{1,0},{2,3},{3,2},{4,20},{5,21},{6,22},{7,23},{8,9},{9,8},{1... | collective-permute-start | bytes 6152 | tf_op jit(solution)/shard_map/ppermute | solution.py:398
  26.6 3.6 %collective-permute-start.7 = (f32[2,256]{1,0:T(2,128)S(1)}, f32[2,256]{1,0:T(2,128)S(1)}, u32[]{:S(2)}, u32[]{:S(2)}) collective-permute-start(f32[2,256]{1,0:T(2,128)S(1)} %add.27.force_in), channel_id=1, source_target_pairs={{0,1},{1,0},{2,3},{3,2},{4,60},{5,61},{6,62},{7,63},{8,9},{9,8},{1... | collective-permute-start | bytes 6152 | tf_op jit(solution)/shard_map/ppermute | solution.py:398
  30.2 3.8 %collective-permute-start.8 = (f32[2,256]{1,0:T(2,128)S(1)}, f32[2,256]{1,0:T(2,128)S(1)}, u32[]{:S(2)}, u32[]{:S(2)}) collective-permute-start(f32[2,256]{1,0:T(2,128)S(1)} %add.28.mine), channel_id=1, source_target_pairs={{0,4},{4,0},{8,12},{12,8},{16,20},{20,16},{24,28},{28,24},{32,36},... | collective-permute-start | bytes 6152 | tf_op jit(solution)/shard_map/ppermute | solution.py:455
  37.9 2.8 %collective-permute-start.9 = (bf16[512,512]{1,0:T(8,128)(2,1)S(1)}, bf16[512,512]{1,0:T(8,128)(2,1)S(1)}, u32[]{:S(2)}, u32[]{:S(2)}) collective-permute-start(bf16[512,512]{1,0:T(8,128)(2,1)S(1)} %shard_map.108.coords), channel_id=1, source_target_pairs={{0,4},{4,0},{8,12},{12,8},{16,20},{20,16},{24,28},{28,24},{32,36},... | collective-permute-start | bytes 1572872 | tf_op jit(solution)/shard_map/ppermute | solution.py:356

commit v3 on v2

--- a/solution.py
+++ b/solution.py
@@ -9,6 +9,7 @@
 from jax.sharding import PartitionSpec as P
 
 ITERS = 6
+EARLY = 4
 NGRID = 4096
 X, Y, Z, CORES = 4, 4, 8, 2
 BLOCK = 256
@@ -36,7 +37,7 @@
         in_specs=specs or [VMEM] * len(operands),
         out_specs=[VMEM] * len(out_shape),
         scratch_shapes=list(scratch),
-        compiler_params=pltpu.CompilerParams(vmem_limit_bytes=room << 20),
+        compiler_params=pltpu.CompilerParams(vmem_limit_bytes=int(room * 2**20)),
         cost_estimate=pl.CostEstimate(flops=int(1e9 * microseconds), bytes_accessed=0, transcendentals=0),
     )(*operands)
 
@@ -112,7 +113,7 @@
 
 def first(unbalance, shapes):
     rows, width = shapes.shape
-    parts = 8
+    parts = 4
     return call(
         first_body,
         [sds((2, width // 2), f32), sds((width, rows), bf16)],
@@ -266,7 +267,9 @@
     f_re, f_im = force[0:1, :], force[1:2, :]
     ch, cl = c_high[...], c_low[...]
 
-    def coupled(y):
+    def coupled(y, sweep):
+        if sweep < EARLY:
+            return mm(y.astype(bf16), ch)
         high, low = split(y)
         return mm(high, ch) + (mm(low, ch) + mm(high, cl))
 
@@ -280,7 +283,7 @@
     for sweep in range(ITERS):
         after = []
         for s, (yr, yi) in zip(tiles, state):
-            pr, pi = coupled(yr), coupled(yi)
+            pr, pi = coupled(yr, sweep), coupled(yi, sweep)
             ur, ui = u_re[s, :], u_im[s, :]
             top_re, top_im = f_re + pi, f_im - pr
             after.append((top_re * ur + top_im * ui, top_im * ur - top_re * ui))
@@ -417,19 +420,19 @@
         )
 
     arrived = lax.ppermute(force, "slab", CORE_PAIRS)
-    force, far_rows = call(
+    force, middle_a = middle((2, 3), force)
+    own = speeds.astype(f32)
+    message = jnp.concatenate([force + arrived, own, own])
+    arrived = swap(message, 0)
+    message, far_rows = call(
         far_gather_body,
-        [small, sds((width, reach), bf16)],
-        (place, force, low, high, shapes_t),
+        [letter, sds((width, reach), bf16)],
+        (place, message, low, high, shapes_t),
         [table],
         [SMEM] + [VMEM] * 4,
         MICRO * 1.8,
     )
     far_halo = lax.ppermute(far_rows, ("slab", "spd"), FAR_PAIRS)
-    own = speeds.astype(f32)
-    message = jnp.concatenate([force + arrived, own, own])
-    arrived = swap(message, 0)
-    message, middle_a = middle((2, 3), message)
     message = jnp.concatenate([message[:2] + arrived[:2], message[2:3], arrived[2:3]])
     there = swap(message, 1)
     message, near_rows = call(
@@ -447,10 +450,10 @@
     force = force + arrived
     arrived = swap(force, 3)
     force, near = end(near_halo, 1, force)
-    force, *prepared = prepare(place, force, speeds, there, near_halo, natural_freq, damping_ratio, coupling)
     force = force + arrived
     arrived = swap(force, 4)
     force, far = end(far_halo, 0, force)
+    force, *prepared = prepare(place, force, speeds, there, near_halo, natural_freq, damping_ratio, coupling)
     force = force + arrived
     coords = solve(place, force, lax.ppermute(force, "slab", CORE_PAIRS), prepared)
     return peaks(place, coords, (far, middle_a, middle_b, near))

time: 44.4 us -> 40.1 us (0.903)
  the two profiles are of different devices: /device:TPU:1 before, /device:TPU:19 now
where the time goes in v3:
time: 40.1 us; the launch traced here: 39.9 us
  Pallas kernels  20.4 us (51%)
  starting transfers between devices  15.3 us (38%)
  waiting for transfers between devices  3.13 us (8%)
  local copies, waits for them, and re-layouts  0.77 us (2%)
    pallas_call x11, Pallas kernels, call(): pl.pallas_call(body, out_shape=out_shape, in_specs=specs or [VMEM] * len(...  20.4 us
    ppermute x5, starting transfers between devices, swap(): return lax.ppermute(x, ('slab', 'spd'), ROUNDS[number])  5.46 us
    ppermute x1, starting transfers between devices, on_device(): near_halo = lax.ppermute(near_rows, 'slab', CORE_PAIRS)  3.62 us
    ppermute x1, starting transfers between devices, on_device(): far_halo = lax.ppermute(far_rows, ('slab', 'spd'), FAR_PAIRS)  2.7 us
    ppermute x1, starting transfers between devices, on_device(): lax.ppermute(force, 'slab', CORE_PAIRS)  2.35 us
    ppermute x5, waiting for transfers between devices, swap(): return lax.ppermute(x, ('slab', 'spd'), ROUNDS[number])  2.3 us
    ppermute x1, waiting for transfers between devices, on_device(): lax.ppermute(force, 'slab', CORE_PAIRS)  0.82 us
  transfers between devices with their start and end apart: 10, of which 3 were waited for; matrix products, arithmetic and copies ran while one was open for 0% of the time, Pallas kernels for 31%

profile of v3, /device:TPU:19, one launch (start us, length us, event | category | flops | bytes accessed | tf_op | source)
XLA Modules:
  0.0 39.9 jit_solution(16004373614057415682)
XLA Ops:
  0.0 0.0 copy-start.3
  0.0 0.0 copy-start.2
  0.0 0.0 copy-start.4
  0.0 0.7 %copy-done.4 = bf16[2,2048]{1,0:T(2,128)(2,1)S(1)} copy-done((bf16[2,2048]{1,0:T(2,128)(2,1)S(1)}, bf16[2,2048]{1,0:T(2,128)(2,1)}, u32[]{:S(2)}) %copy-start.4) | copy-done | bytes 8216
  0.7 1.9 %shard_map.100 = (f32[2,256]{1,0:T(2,128)S(1)}, bf16[512,2048]{1,0:T(8,128)(2,1)S(1)}) custom-call(bf16[2,2048]{1,0:T(2,128)(2,1)S(1)} %copy-done.4, bf16[2048,512]{1,0:T(8,128)(2,1)} %shapes.1), custom_call_target="tpu_custom_call" | custom-call | flops 1500000000 | tf_op jit(solution)/shard_map/pallas_call | solution.py:34
  2.6 0.8 %collective-permute-start = (f32[2,256]{1,0:T(2,128)S(1)}, f32[2,256]{1,0:T(2,128)S(1)}, u32[]{:S(2)}, u32[]{:S(2)}) collective-permute-start(f32[2,256]{1,0:T(2,128)S(1)} %get-tuple-element.25.force_in), channel_id=1, source_target_pairs={{0,4},{4,0},{8,12},{12,8},{16,20},{20,16},{24,28},{28,24},{32,36},... | collective-permute-start | bytes 6152 | tf_op jit(solution)/shard_map/ppermute | solution.py:422
  3.4 0.0 copy-done.3
  3.4 0.0 copy-done.2
  3.4 0.0 copy-start
  3.4 0.0 copy-start.5
  3.4 0.0 copy-start.6
  3.4 1.1 %shard_map.101 = (f32[2,256]{1,0:T(2,128)S(1)}, bf16[512,512]{1,0:T(8,128)(2,1)S(1)}) custom-call(f32[2,256]{1,0:T(2,128)S(1)} %get-tuple-element.25.force_in, s32[8,2048]{1,0:T(8,128)S(1)} %copy-done.2, bf16[8,2048]{1,0:T(8,128)(2,1)S(1)} %copy-done.3, bf16[512,2048]{1,0:T(8,128)(2,1)S(1)} %get-tuple-element.26.shapes_t), custom_call_target="tpu_custom_call" | custom-call | flops 3600000000 | tf_op jit(solution)/shard_map/pallas_call | solution.py:34
  4.6 0.1 pad_add_fusion.place
  4.7 0.0 copy-done
  4.7 0.0 collective-permute-done
  4.7 0.3 collective-permute-start.1
  5.0 0.0 copy-done.5
  5.0 0.0 copy-done.6
  5.0 1.8 %shard_map.102 = (f32[4,256]{1,0:T(4,128)S(1)}, bf16[512,512]{1,0:T(8,128)(2,1)S(1)}) custom-call(s32[2]{0:T(128)S(1)} %pad_add_fusion.place, f32[4,256]{1,0:T(4,128)S(1)} %pad_maximum_fusion.message_in, s32[1,512]{1,0:T(1,128)S(1)} %bitcast.10, s32[1,512]{1,0:T(1,128)S(1)} %bitcast.12, bf16[512,2048]{1,0:T(8,128)(2,1)S(1)} %get-tuple-element.26.shapes_t), custom_call_target="tpu_custom_call" | custom-call | flops 5400000000 | tf_op jit(solution)/shard_map/pallas_call | solution.py:34
  6.9 2.7 %collective-permute-start.6 = (bf16[512,512]{1,0:T(8,128)(2,1)S(1)}, bf16[512,512]{1,0:T(8,128)(2,1)S(1)}, u32[]{:S(2)}, u32[]{:S(2)}) collective-permute-start(bf16[512,512]{1,0:T(8,128)(2,1)S(1)} %get-tuple-element.33), channel_id=1, source_target_pairs={{0,1},{1,0},{2,3},{3,2},{4,8},{5,9},{6,10},{7,11},{8,4},{9,5},{10,... | collective-permute-start | bytes 1572872 | tf_op jit(solution)/shard_map/ppermute | solution.py:435
  9.6 0.0 collective-permute-done.1
  9.6 1.3 %collective-permute-start.2 = (f32[4,256]{1,0:T(4,128)S(1)}, f32[4,256]{1,0:T(4,128)S(1)}, u32[]{:S(2)}, u32[]{:S(2)}) collective-permute-start(f32[4,256]{1,0:T(4,128)S(1)} %pad_maximum_fusion.1.message_in), channel_id=1, source_target_pairs={{0,3},{1,2},{2,1},{3,0},{4,196},{5,197},{6,198},{7,199},{8,11},{9,... | collective-permute-start | bytes 12296 | tf_op jit(solution)/shard_map/ppermute | solution.py:401
  10.9 1.8 %shard_map.103 = (f32[4,256]{1,0:T(4,128)S(1)}, bf16[528,512]{1,0:T(8,128)(2,1)S(1)}) custom-call(s32[2]{0:T(128)S(1)} %pad_add_fusion.place, f32[4,256]{1,0:T(4,128)S(1)} %pad_maximum_fusion.1.message_in, s32[1,512]{1,0:T(1,128)S(1)} %bitcast.11, s32[1,512]{1,0:T(1,128)S(1)} %bitcast.13, bf16[512,2048]{1,0:T(8,128)(2,1)S(1)} %get-tuple-element.26.shapes_t), custom_call_target="tpu_custom_call" | custom-call | flops 5400000000 | tf_op jit(solution)/shard_map/pallas_call | solution.py:34
  12.7 3.6 %collective-permute-start.4 = (bf16[528,512]{1,0:T(8,128)(2,1)S(1)}, bf16[528,512]{1,0:T(8,128)(2,1)S(1)}, u32[]{:S(2)}, u32[]{:S(2)}) collective-permute-start(bf16[528,512]{1,0:T(8,128)(2,1)S(1)} %get-tuple-element.31), channel_id=1, source_target_pairs={{0,4},{4,0},{8,12},{12,8},{16,20},{20,16},{24,28},{28,24},{32,36},... | collective-permute-start | bytes 1622024 | tf_op jit(solution)/shard_map/ppermute | solution.py:446
  16.3 0.0 collective-permute-done.2.there
  16.3 0.0 collective-permute-start.3
  16.3 1.2 %shard_map.104 = (f32[2,256]{1,0:T(2,128)S(1)}, bf16[512,512]{1,0:T(8,128)(2,1)S(1)}) custom-call(f32[2,256]{1,0:T(2,128)S(1)} %slice_add_fusion.force_in, s32[8,2048]{1,0:T(8,128)S(1)} %copy-done.2, bf16[8,2048]{1,0:T(8,128)(2,1)S(1)} %copy-done.3, bf16[512,2048]{1,0:T(8,128)(2,1)S(1)} %get-tuple-element.26.shapes_t), custom_call_target="tpu_custom_call" | custom-call | flops 3600000000 | tf_op jit(solution)/shard_map/pallas_call | solution.py:34
  17.5 1.6 %collective-permute-done.3 = f32[2,256]{1,0:T(2,128)S(1)} collective-permute-done((f32[2,256]{1,0:T(2,128)S(1)}, f32[2,256]{1,0:T(2,128)S(1)}, u32[]{:S(2)}, u32[]{:S(2)}) %collective-permute-start.3) | collective-permute-done | bytes 2080 | tf_op jit(solution)/shard_map/ppermute | solution.py:401
  19.1 1.0 %collective-permute-start.5 = (f32[2,256]{1,0:T(2,128)S(1)}, f32[2,256]{1,0:T(2,128)S(1)}, u32[]{:S(2)}, u32[]{:S(2)}) collective-permute-start(f32[2,256]{1,0:T(2,128)S(1)} %add.26.force_in), channel_id=1, source_target_pairs={{0,1},{1,0},{2,3},{3,2},{4,20},{5,21},{6,22},{7,23},{8,9},{9,8},{1... | collective-permute-start | bytes 6152 | tf_op jit(solution)/shard_map/ppermute | solution.py:401
  20.0 0.0 collective-permute-done.4.halo
  20.0 1.6 %shard_map.105 = (f32[2,256]{1,0:T(2,128)S(1)}, bf16[512,512]{1,0:T(8,128)(2,1)S(1)}) custom-call(s32[2]{0:T(128)S(1)} %pad_add_fusion.place, f32[2,256]{1,0:T(2,128)S(1)} %add.26.force_in, s32[8,2048]{1,0:T(8,128)S(1)} %copy-done.2, bf16[8,2048]{1,0:T(8,128)(2,1)S(1)} %copy-done.3, bf16[512,2048]{1,0:T(8,128)(2,1)S(1)} %get-tuple-element.26.shapes_t, ...), custom_call_target="tpu_custom_call" | custom-call | flops 4800000000 | tf_op jit(solution)/shard_map/pallas_call | solution.py:34
  21.7 0.7 %collective-permute-done.5 = f32[2,256]{1,0:T(2,128)S(1)} collective-permute-done((f32[2,256]{1,0:T(2,128)S(1)}, f32[2,256]{1,0:T(2,128)S(1)}, u32[]{:S(2)}, u32[]{:S(2)}) %collective-permute-start.5) | collective-permute-done | bytes 2080 | tf_op jit(solution)/shard_map/ppermute | solution.py:401
  22.4 0.0 copy-start.1
  22.4 0.0 copy-start.7
  22.4 0.0 copy-start.8
  22.4 2.9 %collective-permute-start.7 = (f32[2,256]{1,0:T(2,128)S(1)}, f32[2,256]{1,0:T(2,128)S(1)}, u32[]{:S(2)}, u32[]{:S(2)}) collective-permute-start(f32[2,256]{1,0:T(2,128)S(1)} %add.27.force_in), channel_id=1, source_target_pairs={{0,1},{1,0},{2,3},{3,2},{4,60},{5,61},{6,62},{7,63},{8,9},{9,8},{1... | collective-permute-start | bytes 6152 | tf_op jit(solution)/shard_map/ppermute | solution.py:401
  25.3 0.0 collective-permute-done.6.halo
  25.3 1.6 %shard_map.106 = (f32[2,256]{1,0:T(2,128)S(1)}, bf16[512,512]{1,0:T(8,128)(2,1)S(1)}) custom-call(s32[2]{0:T(128)S(1)} %pad_add_fusion.place, f32[2,256]{1,0:T(2,128)S(1)} %add.27.force_in, s32[8,2048]{1,0:T(8,128)S(1)} %copy-done.2, bf16[8,2048]{1,0:T(8,128)(2,1)S(1)} %copy-done.3, bf16[512,2048]{1,0:T(8,128)(2,1)S(1)} %get-tuple-element.26.shapes_t, ...), custom_call_target="tpu_custom_call" | custom-call | flops 4800000000 | tf_op jit(solution)/shard_map/pallas_call | solution.py:34
  26.9 0.0 copy-done.1
  26.9 0.0 copy-done.7
  26.9 0.0 copy-done.8
  26.9 0.9 %shard_map.107 = (f32[2,256]{1,0:T(2,128)S(1)}, f32[512,256]{1,0:T(8,128)S(1)}, f32[512,256]{1,0:T(8,128)S(1)}, f32[512,128]{1,0:T(8,128)S(1)}, bf16[256,256]{1,...) custom-call(s32[2]{0:T(128)S(1)} %pad_add_fusion.place, f32[2,256]{1,0:T(2,128)S(1)} %get-tuple-element.34.message_in, ...), custom_call_target="tpu_custom_call" | custom-call | flops 900000000 | tf_op jit(solution)/shard_map/pallas_call | solution.py:34
  27.9 0.0 collective-permute-done.7
  27.9 2.3 %collective-permute-start.8 = (f32[2,256]{1,0:T(2,128)S(1)}, f32[2,256]{1,0:T(2,128)S(1)}, u32[]{:S(2)}, u32[]{:S(2)}) collective-permute-start(f32[2,256]{1,0:T(2,128)S(1)} %add.28.mine), channel_id=1, source_target_pairs={{0,4},{4,0},{8,12},{12,8},{16,20},{20,16},{24,28},{28,24},{32,36},... | collective-permute-start | bytes 6152 | tf_op jit(solution)/shard_map/ppermute | solution.py:458
  30.3 0.8 %collective-permute-done.8.other = f32[2,256]{1,0:T(2,128)S(1)} collective-permute-done((f32[2,256]{1,0:T(2,128)S(1)}, f32[2,256]{1,0:T(2,128)S(1)}, u32[]{:S(2)}, u32[]{:S(2)}) %collective-permute-start.8) | collective-permute-done | bytes 2080 | tf_op jit(solution)/shard_map/ppermute | solution.py:458
  31.1 2.5 %shard_map.108.coords = bf16[512,512]{1,0:T(8,128)(2,1)S(1)} custom-call(s32[2]{0:T(128)S(1)} %pad_add_fusion.place, f32[2,256]{1,0:T(2,128)S(1)} %add.28.mine, f32[2,256]{1,0:T(2,128)S(1)} %collective-permute-done.8.other, f32[512,256]{1,0:T(8,128)S(1)} %get-tuple-element.36.u_re, f32[512,256]{1,0:T(8,128)S(1)} %get-tuple-element.37.u_im, ...), custom_call_target="tpu_custom_call" | custom-call | flops 4000000000 | tf_op jit(solution)/shard_map/pallas_call | solution.py:34
  33.6 0.4 %collective-permute-start.9 = (bf16[512,512]{1,0:T(8,128)(2,1)S(1)}, bf16[512,512]{1,0:T(8,128)(2,1)S(1)}, u32[]{:S(2)}, u32[]{:S(2)}) collective-permute-start(bf16[512,512]{1,0:T(8,128)(2,1)S(1)} %shard_map.108.coords), channel_id=1, source_target_pairs={{0,4},{4,0},{8,12},{12,8},{16,20},{20,16},{24,28},{28,24},{32,36},... | collective-permute-start | bytes 1572872 | tf_op jit(solution)/shard_map/ppermute | solution.py:359
  34.0 2.4 %shard_map.109.before = f32[8,2048]{1,0:T(8,128)S(1)} custom-call(bf16[512,512]{1,0:T(8,128)(2,1)S(1)} %shard_map.108.coords, bf16[512,512]{1,0:T(8,128)(2,1)S(1)} %get-tuple-element.41.far, bf16[512,512]{1,0:T(8,128)(2,1)S(1)} %get-tuple-element.42.middle_a, bf16[512,512]{1,0:T(8,128)(2,1)S(1)} %get-tuple-element.43.middle_b, ...), custom_call_target="tpu_custom_call" | custom-call | flops 2500000000 | tf_op jit(solution)/shard_map/pallas_call | solution.py:34
  36.4 0.0 collective-permute-done.9.coords
  36.4 3.5 %shard_map.110 = f32[1,2048]{1,0:T(1,128)} custom-call(s32[2]{0:T(128)S(1)} %pad_add_fusion.place, bf16[512,512]{1,0:T(8,128)(2,1)S(1)} %collective-permute-done.9.coords, f32[8,2048]{1,0:T(8,128)S(1)} %shard_map.109.before, bf16[512,512]{1,0:T(8,128)(2,1)S(1)} %get-tuple-element.41.far, bf16[512,512]{1,0:T(8,128)(2,1)S(1)} %get-tuple-element.42.middle_a, ...), custom_call_target="tpu_custom_call" | custom-call | flops 2500000000 | tf_op jit(solution)/shard_map/pallas_call | solution.py:34
  (11 shorter events, 0.1 us)
Async XLA Ops:
  0.0 3.4 %copy-start.3 = (bf16[8,2048]{1,0:T(8,128)(2,1)S(1)}, bf16[8,2048]{1,0:T(8,128)(2,1)}, u32[]{:S(2)}) copy-start(bf16[8,2048]{1,0:T(8,128)(2,1)} %weights.7) | copy-start | bytes 98308
  0.0 3.4 %copy-start.2 = (s32[8,2048]{1,0:T(8,128)S(1)}, s32[8,2048]{1,0:T(8,128)}, u32[]{:S(2)}) copy-start(s32[8,2048]{1,0:T(8,128)} %links.7) | copy-start | bytes 196612
  0.0 0.7 %copy-start.4 = (bf16[2,2048]{1,0:T(2,128)(2,1)S(1)}, bf16[2,2048]{1,0:T(2,128)(2,1)}, u32[]{:S(2)}) copy-start(bf16[2,2048]{1,0:T(2,128)(2,1)} %unbalance.1) | copy-start | bytes 24580
  2.6 2.0 %collective-permute-start = (f32[2,256]{1,0:T(2,128)S(1)}, f32[2,256]{1,0:T(2,128)S(1)}, u32[]{:S(2)}, u32[]{:S(2)}) collective-permute-start(f32[2,256]{1,0:T(2,128)S(1)} %get-tuple-element.25.force_in), channel_id=1, source_target_pairs={{0,4},{4,0},{8,12},{12,8},{16,20},{20,16},{24,28},{28,24},{32,36},... | collective-permute-start | bytes 6152 | tf_op jit(solution)/shard_map/ppermute | solution.py:422
  3.4 1.3 %copy-start = (s32[256]{0:T(256)S(1)}, s32[256]{0:T(256)}, u32[]{:S(2)}) copy-start(s32[256]{0:T(256)} %param.19) | copy-start | bytes 3076
  3.4 1.6 %copy-start.5 = (s32[512]{0:T(512)S(1)}, s32[512]{0:T(512)}, u32[]{:S(2)}) copy-start(s32[512]{0:T(512)} %param.14) | copy-start | bytes 6148
  3.4 1.6 %copy-start.6 = (s32[512]{0:T(512)S(1)}, s32[512]{0:T(512)}, u32[]{:S(2)}) copy-start(s32[512]{0:T(512)} %param.15) | copy-start | bytes 6148
  4.7 4.9 %collective-permute-start.1 = (f32[4,256]{1,0:T(4,128)S(1)}, f32[4,256]{1,0:T(4,128)S(1)}, u32[]{:S(2)}, u32[]{:S(2)}) collective-permute-start(f32[4,256]{1,0:T(4,128)S(1)} %pad_maximum_fusion.message_in), channel_id=1, source_target_pairs={{0,1},{1,0},{2,3},{3,2},{4,68},{5,69},{6,70},{7,71},{8,9},{9,8},{1... | collective-permute-start | bytes 12296 | tf_op jit(solution)/shard_map/ppermute | solution.py:401
  6.9 18.4 %collective-permute-start.6 = (bf16[512,512]{1,0:T(8,128)(2,1)S(1)}, bf16[512,512]{1,0:T(8,128)(2,1)S(1)}, u32[]{:S(2)}, u32[]{:S(2)}) collective-permute-start(bf16[512,512]{1,0:T(8,128)(2,1)S(1)} %get-tuple-element.33), channel_id=1, source_target_pairs={{0,1},{1,0},{2,3},{3,2},{4,8},{5,9},{6,10},{7,11},{8,4},{9,5},{10,... | collective-permute-start | bytes 1572872 | tf_op jit(solution)/shard_map/ppermute | solution.py:435
  9.6 6.7 %collective-permute-start.2 = (f32[4,256]{1,0:T(4,128)S(1)}, f32[4,256]{1,0:T(4,128)S(1)}, u32[]{:S(2)}, u32[]{:S(2)}) collective-permute-start(f32[4,256]{1,0:T(4,128)S(1)} %pad_maximum_fusion.1.message_in), channel_id=1, source_target_pairs={{0,3},{1,2},{2,1},{3,0},{4,196},{5,197},{6,198},{7,199},{8,11},{9,... | collective-permute-start | bytes 12296 | tf_op jit(solution)/shard_map/ppermute | solution.py:401
  12.7 7.3 %collective-permute-start.4 = (bf16[528,512]{1,0:T(8,128)(2,1)S(1)}, bf16[528,512]{1,0:T(8,128)(2,1)S(1)}, u32[]{:S(2)}, u32[]{:S(2)}) collective-permute-start(bf16[528,512]{1,0:T(8,128)(2,1)S(1)} %get-tuple-element.31), channel_id=1, source_target_pairs={{0,4},{4,0},{8,12},{12,8},{16,20},{20,16},{24,28},{28,24},{32,36},... | collective-permute-start | bytes 1622024 | tf_op jit(solution)/shard_map/ppermute | solution.py:446
  16.3 2.7 %collective-permute-start.3 = (f32[2,256]{1,0:T(2,128)S(1)}, f32[2,256]{1,0:T(2,128)S(1)}, u32[]{:S(2)}, u32[]{:S(2)}) collective-permute-start(f32[2,256]{1,0:T(2,128)S(1)} %slice_add_fusion.force_in), channel_id=1, source_target_pairs={{0,1},{1,0},{2,3},{3,2},{4,12},{5,13},{6,14},{7,15},{8,9},{9,8},{1... | collective-permute-start | bytes 6152 | tf_op jit(solution)/shard_map/ppermute | solution.py:401
  19.1 3.3 %collective-permute-start.5 = (f32[2,256]{1,0:T(2,128)S(1)}, f32[2,256]{1,0:T(2,128)S(1)}, u32[]{:S(2)}, u32[]{:S(2)}) collective-permute-start(f32[2,256]{1,0:T(2,128)S(1)} %add.26.force_in), channel_id=1, source_target_pairs={{0,1},{1,0},{2,3},{3,2},{4,20},{5,21},{6,22},{7,23},{8,9},{9,8},{1... | collective-permute-start | bytes 6152 | tf_op jit(solution)/shard_map/ppermute | solution.py:401
  22.4 4.5 %copy-start.1 = (f32[256,256]{1,0:T(8,128)S(1)}, f32[256,256]{1,0:T(8,128)}, u32[]{:S(2)}) copy-start(f32[256,256]{1,0:T(8,128)} %coupling.1) | copy-start | bytes 786436
  22.4 4.5 %copy-start.7 = (f32[256]{0:T(256)S(1)}, f32[256]{0:T(256)}, u32[]{:S(2)}) copy-start(f32[256]{0:T(256)} %param.16) | copy-start | bytes 3076
  22.4 4.5 %copy-start.8 = (f32[256]{0:T(256)S(1)}, f32[256]{0:T(256)}, u32[]{:S(2)}) copy-start(f32[256]{0:T(256)} %param.17) | copy-start | bytes 3076
  22.4 5.5 %collective-permute-start.7 = (f32[2,256]{1,0:T(2,128)S(1)}, f32[2,256]{1,0:T(2,128)S(1)}, u32[]{:S(2)}, u32[]{:S(2)}) collective-permute-start(f32[2,256]{1,0:T(2,128)S(1)} %add.27.force_in), channel_id=1, source_target_pairs={{0,1},{1,0},{2,3},{3,2},{4,60},{5,61},{6,62},{7,63},{8,9},{9,8},{1... | collective-permute-start | bytes 6152 | tf_op jit(solution)/shard_map/ppermute | solution.py:401
  27.9 3.2 %collective-permute-start.8 = (f32[2,256]{1,0:T(2,128)S(1)}, f32[2,256]{1,0:T(2,128)S(1)}, u32[]{:S(2)}, u32[]{:S(2)}) collective-permute-start(f32[2,256]{1,0:T(2,128)S(1)} %add.28.mine), channel_id=1, source_target_pairs={{0,4},{4,0},{8,12},{12,8},{16,20},{20,16},{24,28},{28,24},{32,36},... | collective-permute-start | bytes 6152 | tf_op jit(solution)/shard_map/ppermute | solution.py:458
  33.6 2.8 %collective-permute-start.9 = (bf16[512,512]{1,0:T(8,128)(2,1)S(1)}, bf16[512,512]{1,0:T(8,128)(2,1)S(1)}, u32[]{:S(2)}, u32[]{:S(2)}) collective-permute-start(bf16[512,512]{1,0:T(8,128)(2,1)S(1)} %shard_map.108.coords), channel_id=1, source_target_pairs={{0,4},{4,0},{8,12},{12,8},{16,20},{20,16},{24,28},{28,24},{32,36},... | collective-permute-start | bytes 1572872 | tf_op jit(solution)/shard_map/ppermute | solution.py:359

commit v4 on v3

--- a/solution.py
+++ b/solution.py
@@ -16,7 +16,7 @@
 WINDOW = 1280
 CODE = 64
 ROOM0 = 50
-MICRO = 3.0
+MICRO = 8.0
 bf16 = jnp.bfloat16
 f32 = jnp.float32
 
@@ -26,7 +26,6 @@
 
 
 VMEM = pl.BlockSpec(memory_space=pltpu.VMEM)
-SMEM = pl.BlockSpec(memory_space=pltpu.SMEM)
 HBM = pl.BlockSpec(memory_space=pltpu.HBM)
 
 
@@ -44,6 +43,15 @@
 
 def sds(shape, dtype):
     return jax.ShapeDtypeStruct(shape, dtype)
+
+
+def odd_core():
+    return lax.rem(lax.axis_index("slab"), CORES)
+
+
+def end_slab():
+    slab = lax.axis_index("slab")
+    return jnp.logical_or(slab == 0, slab == N_SLAB - 1)
 
 
 def slab_of(x, z, c):
@@ -140,12 +148,12 @@
     return mm(shapes_t[...], table[...]).astype(bf16)
 
 
-def near_gather_body(place, message_in, low, high, shapes_t, message_out, out, table):
+def near_gather_body(message_in, speeds, low, high, shapes_t, message_out, out, table):
     width = shapes_t.shape[0]
-    nodes = jnp.where(place[0] == 0, high[...], low[...])
+    nodes = jnp.where(odd_core() == 0, high[...], low[...])
     one = jnp.ones((16, nodes.shape[1]), bf16)
     out[:width, :] = gather_rows(nodes, one, shapes_t, table)
-    index = message_in[3:4, :].astype(jnp.int32)
+    index = speeds[...].astype(jnp.int32)
     coarse = index // CODE
     fine = index - coarse * CODE
     row = jnp.concatenate([coarse.astype(f32), fine.astype(f32)], 1)
@@ -153,9 +161,9 @@
     message_out[...] = message_in[...]
 
 
-def far_gather_body(place, message_in, low, high, shapes_t, message_out, out, table):
-    nodes = jnp.where(place[0] == 0, low[...], high[...])
-    one = jnp.full((16, nodes.shape[1]), jnp.where(place[1] == 0, 1.0, 0.0), f32).astype(bf16)
+def far_gather_body(message_in, low, high, shapes_t, message_out, out, table):
+    nodes = jnp.where(odd_core() == 0, low[...], high[...])
+    one = jnp.full((16, nodes.shape[1]), jnp.where(end_slab(), 0.0, 1.0), f32).astype(bf16)
     out[...] = gather_rows(nodes, one, shapes_t, table)
     message_out[...] = message_in[...]
 
@@ -184,12 +192,12 @@
     force_out[...] = force_in[...]
 
 
-def end_body(place, force_in, links, weights, shapes_t, halo, force_out, out, window, tables, *, low_core):
+def end_body(force_in, links, weights, shapes_t, halo, force_out, out, window, tables, *, low_core):
     width, rows = shapes_t.shape
     reach = halo.shape[1]
     own = 1024
 
-    low = place[0] == low_core
+    low = odd_core() == low_core
 
     @pl.when(low)
     def _():
@@ -216,7 +224,7 @@
 
 
 def prepare_body(
-    place, message_in, speeds, there, halo, freq, damping, coupling, message_out, u_re, u_im, omega_out, c_high, c_low
+    message_in, speeds, there, halo, freq, damping, coupling, message_out, u_re, u_im, omega_out, c_high, c_low
 ):
     count = freq.shape[1]
     total = u_re.shape[0]
@@ -224,7 +232,7 @@
     tail = tail[0:1, : total // 2] * CODE + tail[0:1, total // 2 :]
     odd = jnp.concatenate([speeds[...].astype(f32), tail], 1)
     even = jnp.concatenate([there[2:3, :], there[3:4, :]], 1)
-    index = jnp.where(place[0] == 0, even, odd)
+    index = jnp.where(odd_core() == 0, even, odd)
     message_out[...] = message_in[...]
     omega = 0.25 + 4.0 * index / NGRID
     omega = jnp.transpose(jnp.broadcast_to(omega, (8, total)))[:, 0:1]
@@ -243,9 +251,9 @@
     c_high[...], c_low[...] = split(jnp.where(i == j, 0.0, coupled))
 
 
-def prepare(place, message, speeds, there, halo, freq, damping, coupling):
+def prepare(message, speeds, there, halo, freq, damping, coupling):
     total, count = 2 * speeds.shape[1], freq.shape[0]
-    operands = (place, message, speeds, there, halo, freq.reshape(1, count), damping.reshape(1, count), coupling)
+    operands = (message, speeds, there, halo, freq.reshape(1, count), damping.reshape(1, count), coupling)
     return call(
         prepare_body,
         [
@@ -257,13 +265,13 @@
             sds((count, count), bf16),
         ],
         operands,
-        specs=[SMEM] + [VMEM] * 7,
+        specs=[VMEM] * 7,
         microseconds=0.9,
     )
 
 
-def solve_body(place, mine, other, u_re, u_im, omega, c_high, c_low, out):
-    force = jnp.where(place[0] == 1, mine[...], other[...])
+def solve_body(mine, other, u_re, u_im, omega, c_high, c_low, for_re, for_im):
+    force = jnp.where(odd_core() == 1, mine[...], other[...])
     f_re, f_im = force[0:1, :], force[1:2, :]
     ch, cl = c_high[...], c_low[...]
 
@@ -290,20 +298,22 @@
         state = after
     for s, (yr, yi) in zip(tiles, state):
         w = jnp.concatenate([omega[s, :]] * (count // 128), 1)
-        out[s, :count] = (yr * w).astype(bf16)
-        out[s, count:] = (yi * w).astype(bf16)
-
-
-def solve(place, mine, other, prepared):
+        re, im = (yr * w).astype(bf16), (yi * w).astype(bf16)
+        for_re[s, :count] = re
+        for_re[s, count:] = -im
+        for_im[s, :count] = im
+        for_im[s, count:] = re
+
+
+def solve(mine, other, prepared):
     total, count = prepared[0].shape
-    operands = (place, mine, other, *prepared)
-    return call(
-        solve_body, [sds((total, 2 * count), bf16)], operands, specs=[SMEM] + [VMEM] * 7, microseconds=4.0
-    )[0]
-
-
-def peaks_tile(coords, modes, for_re, for_im):
-    total, twice = coords.shape
+    operands = (mine, other, *prepared)
+    shape = sds((total, 2 * count), bf16)
+    return call(solve_body, [shape, shape], operands, specs=[VMEM] * 7, microseconds=4.0)
+
+
+def peaks_tile(modes, for_re, for_im):
+    total = for_im.shape[0]
     tile = 256
     best = jnp.zeros((8, modes.shape[1]), f32)
     for s in range(0, total, tile):
@@ -322,28 +332,20 @@
             at += BLOCK
 
 
-def half_peaks_body(coords, far, middle_a, middle_b, near, best, for_re, for_im):
-    spread(coords, for_re, for_im)
+def half_peaks_body(for_re, for_im, far, middle_a, middle_b, near, best):
     for at, part, e in parts_of((far, middle_a, middle_b, near)):
-        best[:, at : at + BLOCK] = peaks_tile(coords, part[:, e : e + BLOCK], for_re, for_im)
-
-
-def spread(coords, for_re, for_im):
-    count = coords.shape[1] // 2
-    re, im = coords[:, :count], coords[:, count:]
-    for_re[:, :count] = re
-    for_re[:, count:] = -im
-    for_im[:, :count] = im
-    for_im[:, count:] = re
-
-
-def all_peaks_body(place, coords, before, far, middle_a, middle_b, near, out, for_re, for_im):
-    spread(coords, for_re, for_im)
+        best[:, at : at + BLOCK] = peaks_tile(part[:, e : e + BLOCK], for_re, for_im)
+
+
+def all_peaks_body(for_im, before, far, middle_a, middle_b, near, out, for_re):
+    count = for_im.shape[1] // 2
+    for_re[:, :count] = for_im[:, count:]
+    for_re[:, count:] = -for_im[:, :count]
     rows = out.shape[1]
     end = far.shape[1]
-    even = place[0] == 0
+    even = odd_core() == 0
     for at, part, e in parts_of((far, middle_a, middle_b, near)):
-        best = jnp.maximum(before[:, at : at + BLOCK], peaks_tile(coords, part[:, e : e + BLOCK], for_re, for_im))
+        best = jnp.maximum(before[:, at : at + BLOCK], peaks_tile(part[:, e : e + BLOCK], for_re, for_im))
         peak = jnp.sqrt(jnp.max(best, axis=0, keepdims=True))
         to = at
         if part is far:
@@ -353,18 +355,17 @@
         out[0:1, pl.ds(pl.multiple_of(to, BLOCK), BLOCK)] = peak
 
 
-def peaks(place, coords, parts):
-    total, twice = coords.shape
+def peaks(for_re, for_im, parts):
+    total, twice = for_im.shape
     rows = sum(p.shape[1] for p in parts)
-    there = lax.ppermute(coords, "slab", CORE_PAIRS)
-    scratch = [pltpu.VMEM((total, twice), bf16)] * 2
-    best = call(half_peaks_body, [sds((8, rows), f32)], (coords, *parts), scratch, microseconds=2.5)[0]
+    there = lax.ppermute(for_im, "slab", CORE_PAIRS)
+    best = call(half_peaks_body, [sds((8, rows), f32)], (for_re, for_im, *parts), microseconds=2.5)[0]
     out = call(
         all_peaks_body,
         [sds((1, rows), f32)],
-        (place, there, best, *parts),
-        scratch,
-        [SMEM] + [VMEM] * 6,
+        (there, best, *parts),
+        [pltpu.VMEM((total, twice), bf16)],
+        [VMEM] * 6,
         2.5,
     )[0]
     return out.reshape(rows)
@@ -384,9 +385,6 @@
 ):
     rows, width = mode_shapes.shape
     reach = face_low_nodes.shape[0]
-    slab = lax.axis_index("slab")
-    edge = jnp.logical_or(slab == 0, slab == N_SLAB - 1)
-    place = jnp.stack([slab % CORES, edge.astype(jnp.int32)]).astype(jnp.int32)
     low = face_low_nodes.reshape(1, reach)
     high = face_high_nodes.reshape(1, reach)
 
@@ -413,9 +411,9 @@
         return call(
             functools.partial(end_body, low_core=low_core),
             [small, sds((width, 2 * BLOCK), bf16)],
-            (place, force, connectivity, stress_weights, shapes_t, halo),
+            (force, connectivity, stress_weights, shapes_t, halo),
             [pltpu.VMEM((width, 3 * reach), bf16), tables],
-            [SMEM] + [VMEM] * 5,
+            [VMEM] * 5,
             MICRO * 1.6,
         )
 
@@ -427,36 +425,36 @@
     message, far_rows = call(
         far_gather_body,
         [letter, sds((width, reach), bf16)],
-        (place, message, low, high, shapes_t),
+        (message, low, high, shapes_t),
         [table],
-        [SMEM] + [VMEM] * 4,
+        [VMEM] * 4,
         MICRO * 1.8,
     )
     far_halo = lax.ppermute(far_rows, ("slab", "spd"), FAR_PAIRS)
     message = jnp.concatenate([message[:2] + arrived[:2], message[2:3], arrived[2:3]])
     there = swap(message, 1)
-    message, near_rows = call(
+    message, middle_b = middle((4, 5), message)
+    force = message[:2] + there[:2]
+    arrived, neighbour = swap(force, 2), arrived[2:3]
+    force, near_rows = call(
         near_gather_body,
-        [letter, sds((width + 16, reach), bf16)],
-        (place, message, low, high, shapes_t),
+        [small, sds((width + 16, reach), bf16)],
+        (force, neighbour, low, high, shapes_t),
         [table],
-        [SMEM] + [VMEM] * 4,
+        [VMEM] * 5,
         MICRO * 1.8,
     )
     near_halo = lax.ppermute(near_rows, "slab", CORE_PAIRS)
-    force = message[:2] + there[:2]
-    arrived = swap(force, 2)
-    force, middle_b = middle((4, 5), force)
     force = force + arrived
     arrived = swap(force, 3)
-    force, near = end(near_halo, 1, force)
+    force, far = end(far_halo, 0, force)
     force = force + arrived
     arrived = swap(force, 4)
-    force, far = end(far_halo, 0, force)
-    force, *prepared = prepare(place, force, speeds, there, near_halo, natural_freq, damping_ratio, coupling)
+    force, near = end(near_halo, 1, force)
+    force, *prepared = prepare(force, speeds, there, near_halo, natural_freq, damping_ratio, coupling)
     force = force + arrived
-    coords = solve(place, force, lax.ppermute(force, "slab", CORE_PAIRS), prepared)
-    return peaks(place, coords, (far, middle_a, middle_b, near))
+    for_re, for_im = solve(force, lax.ppermute(force, "slab", CORE_PAIRS), prepared)
+    return peaks(for_re, for_im, (far, middle_a, middle_b, near))
 
 
 def solution(mesh):

time: 40.1 us -> 37.8 us (0.943)
  Pallas kernels: 20.4 us -> 16.7 us
  waiting for transfers between devices: 3.13 us -> 4.56 us
    pallas_call x11, Pallas kernels: 20.4 us -> 16.7 us  [call(): pl.pallas_call(body, out_shape=out_shape, in_specs=specs or [VMEM] * len(...]
    ppermute x1, starting transfers between devices: 3.62 us -> 6.1 us  [on_device(): near_halo = lax.ppermute(near_rows, 'slab', CORE_PAIRS)]
    ppermute x1, starting transfers between devices: 2.35 us -> 0.66 us  [on_device(): lax.ppermute(force, 'slab', CORE_PAIRS)]
    ppermute x5, waiting for transfers between devices: 2.3 us -> 3.73 us  [swap(): return lax.ppermute(x, ('slab', 'spd'), ROUNDS[number])]
    ppermute x5, starting transfers between devices: 5.46 us -> 4.35 us  [swap(): return lax.ppermute(x, ('slab', 'spd'), ROUNDS[number])]
  transfers between devices with their start and end apart: 10 -> 10, of which waited for: 3 -> 4; matrix products, arithmetic and copies ran while one was open for 0% -> 0% of each run, Pallas kernels for 31% -> 26%
where the time goes in v4:
time: 37.8 us; the launch traced here: 37.2 us
  Pallas kernels  16.7 us (44%)
  starting transfers between devices  15 us (40%)
  waiting for transfers between devices  4.56 us (12%)
  local copies, waits for them, and re-layouts  0.77 us (2%)
    pallas_call x11, Pallas kernels, call(): pl.pallas_call(body, out_shape=out_shape, in_specs=specs or [VMEM] * len(...  16.7 us
    ppermute x1, starting transfers between devices, on_device(): near_halo = lax.ppermute(near_rows, 'slab', CORE_PAIRS)  6.1 us
    ppermute x5, starting transfers between devices, swap(): return lax.ppermute(x, ('slab', 'spd'), ROUNDS[number])  4.35 us
    ppermute x5, waiting for transfers between devices, swap(): return lax.ppermute(x, ('slab', 'spd'), ROUNDS[number])  3.73 us
    ppermute x1, starting transfers between devices, on_device(): far_halo = lax.ppermute(far_rows, ('slab', 'spd'), FAR_PAIRS)  2.68 us
    ppermute x1, waiting for transfers between devices, on_device(): lax.ppermute(force, 'slab', CORE_PAIRS)  0.82 us
    ppermute x1, starting transfers between devices, on_device(): arrived = lax.ppermute(force, 'slab', CORE_PAIRS)  0.76 us
    unnamed x18, local copies, waits for them, and re-layouts  0.76 us
  transfers between devices with their start and end apart: 10, of which 4 were waited for; matrix products, arithmetic and copies ran while one was open for 0% of the time, Pallas kernels for 26%

profile of v4, /device:TPU:19, one launch (start us, length us, event | category | flops | bytes accessed | tf_op | source)
XLA Modules:
  0.0 37.2 jit_solution(8109907506510899663)
XLA Ops:
  0.0 0.0 copy-start.2
  0.0 0.0 copy-start.3
  0.0 0.0 copy-start.4
  0.0 0.7 %copy-done.4 = bf16[2,2048]{1,0:T(2,128)(2,1)S(1)} copy-done((bf16[2,2048]{1,0:T(2,128)(2,1)S(1)}, bf16[2,2048]{1,0:T(2,128)(2,1)}, u32[]{:S(2)}) %copy-start.4) | copy-done | bytes 8216
  0.7 1.9 %shard_map.100 = (f32[2,256]{1,0:T(2,128)S(1)}, bf16[512,2048]{1,0:T(8,128)(2,1)S(1)}) custom-call(bf16[2,2048]{1,0:T(2,128)(2,1)S(1)} %copy-done.4, bf16[2048,512]{1,0:T(8,128)(2,1)} %shapes.1), custom_call_target="tpu_custom_call" | custom-call | flops 1500000000 | tf_op jit(solution)/shard_map/pallas_call | solution.py:33
  2.6 0.8 %collective-permute-start = (f32[2,256]{1,0:T(2,128)S(1)}, f32[2,256]{1,0:T(2,128)S(1)}, u32[]{:S(2)}, u32[]{:S(2)}) collective-permute-start(f32[2,256]{1,0:T(2,128)S(1)} %get-tuple-element.27.force_in), channel_id=1, source_target_pairs={{0,4},{4,0},{8,12},{12,8},{16,20},{20,16},{24,28},{28,24},{32,36},... | collective-permute-start | bytes 6152 | tf_op jit(solution)/shard_map/ppermute | solution.py:420
  3.4 0.0 copy-done.2
  3.4 0.0 copy-done.3
  3.4 0.0 copy-start
  3.4 0.0 copy-start.5
  3.4 0.0 copy-start.6
  3.4 1.1 %shard_map.101 = (f32[2,256]{1,0:T(2,128)S(1)}, bf16[512,512]{1,0:T(8,128)(2,1)S(1)}) custom-call(f32[2,256]{1,0:T(2,128)S(1)} %get-tuple-element.27.force_in, s32[8,2048]{1,0:T(8,128)S(1)} %copy-done.2, bf16[8,2048]{1,0:T(8,128)(2,1)S(1)} %copy-done.3, bf16[512,2048]{1,0:T(8,128)(2,1)S(1)} %get-tuple-element.28.shapes_t), custom_call_target="tpu_custom_call" | custom-call | flops 9600000000 | tf_op jit(solution)/shard_map/pallas_call | solution.py:33
  4.6 0.0 copy-done
  4.6 0.0 collective-permute-done
  4.6 0.3 collective-permute-start.1
  5.0 0.0 copy-done.5
  5.0 0.0 copy-done.6
  5.0 1.3 %shard_map.102 = (f32[4,256]{1,0:T(4,128)S(1)}, bf16[512,512]{1,0:T(8,128)(2,1)S(1)}) custom-call(f32[4,256]{1,0:T(4,128)S(1)} %pad_maximum_fusion.message_in, s32[1,512]{1,0:T(1,128)S(1)} %bitcast.8, s32[1,512]{1,0:T(1,128)S(1)} %bitcast.10, bf16[512,2048]{1,0:T(8,128)(2,1)S(1)} %get-tuple-element.28.shapes_t), custom_call_target="tpu_custom_call" | custom-call | flops 14400000000 | tf_op jit(solution)/shard_map/pallas_call | solution.py:33
  6.3 2.7 %collective-permute-start.4 = (bf16[512,512]{1,0:T(8,128)(2,1)S(1)}, bf16[512,512]{1,0:T(8,128)(2,1)S(1)}, u32[]{:S(2)}, u32[]{:S(2)}) collective-permute-start(bf16[512,512]{1,0:T(8,128)(2,1)S(1)} %get-tuple-element.33), channel_id=1, source_target_pairs={{0,1},{1,0},{2,3},{3,2},{4,8},{5,9},{6,10},{7,11},{8,4},{9,5},{10,... | collective-permute-start | bytes 1572872 | tf_op jit(solution)/shard_map/ppermute | solution.py:433
  9.0 0.0 collective-permute-done.1
  9.0 1.3 %collective-permute-start.2 = (f32[4,256]{1,0:T(4,128)S(1)}, f32[4,256]{1,0:T(4,128)S(1)}, u32[]{:S(2)}, u32[]{:S(2)}) collective-permute-start(f32[4,256]{1,0:T(4,128)S(1)} %pad_maximum_fusion.1.force_in), channel_id=1, source_target_pairs={{0,3},{1,2},{2,1},{3,0},{4,196},{5,197},{6,198},{7,199},{8,11},{9,... | collective-permute-start | bytes 12296 | tf_op jit(solution)/shard_map/ppermute | solution.py:399
  10.3 1.1 %shard_map.103 = (f32[4,256]{1,0:T(4,128)S(1)}, bf16[512,512]{1,0:T(8,128)(2,1)S(1)}) custom-call(f32[4,256]{1,0:T(4,128)S(1)} %pad_maximum_fusion.1.force_in, s32[8,2048]{1,0:T(8,128)S(1)} %copy-done.2, bf16[8,2048]{1,0:T(8,128)(2,1)S(1)} %copy-done.3, bf16[512,2048]{1,0:T(8,128)(2,1)S(1)} %get-tuple-element.28.shapes_t), custom_call_target="tpu_custom_call" | custom-call | flops 9600000000 | tf_op jit(solution)/shard_map/pallas_call | solution.py:33
  11.4 0.1 collective-permute-done.2.there
  11.5 1.9 %collective-permute-start.3 = (f32[2,256]{1,0:T(2,128)S(1)}, f32[2,256]{1,0:T(2,128)S(1)}, u32[]{:S(2)}, u32[]{:S(2)}) collective-permute-start(f32[2,256]{1,0:T(2,128)S(1)} %slice_add_fusion.message_in), channel_id=1, source_target_pairs={{0,1},{1,0},{2,3},{3,2},{4,12},{5,13},{6,14},{7,15},{8,9},{9,8},{1... | collective-permute-start | bytes 6152 | tf_op jit(solution)/shard_map/ppermute | solution.py:399
  13.5 1.3 %shard_map.104 = (f32[2,256]{1,0:T(2,128)S(1)}, bf16[528,512]{1,0:T(8,128)(2,1)S(1)}) custom-call(f32[2,256]{1,0:T(2,128)S(1)} %slice_add_fusion.message_in, f32[1,256]{1,0:T(1,128)S(1)} %slice.26.speeds, s32[1,512]{1,0:T(1,128)S(1)} %bitcast.9, s32[1,512]{1,0:T(1,128)S(1)} %bitcast.11, bf16[512,2048]{1,0:T(8,128)(2,1)S(1)} %get-tuple-element.28.shapes_t), custom_call_target="tpu_custom_call" | custom-call | flops 14400000000 | tf_op jit(solution)/shard_map/pallas_call | solution.py:33
  14.7 6.1 %collective-permute-start.6 = (bf16[528,512]{1,0:T(8,128)(2,1)S(1)}, bf16[528,512]{1,0:T(8,128)(2,1)S(1)}, u32[]{:S(2)}, u32[]{:S(2)}) collective-permute-start(bf16[528,512]{1,0:T(8,128)(2,1)S(1)} %get-tuple-element.35), channel_id=1, source_target_pairs={{0,4},{4,0},{8,12},{12,8},{16,20},{20,16},{24,28},{28,24},{32,36},... | collective-permute-start | bytes 1622024 | tf_op jit(solution)/shard_map/ppermute | solution.py:447
  20.8 0.0 collective-permute-done.3
  20.8 0.0 collective-permute-start.5
  20.8 0.0 collective-permute-done.4.halo
  20.9 1.1 %shard_map.105 = (f32[2,256]{1,0:T(2,128)S(1)}, bf16[512,512]{1,0:T(8,128)(2,1)S(1)}) custom-call(f32[2,256]{1,0:T(2,128)S(1)} %add.21.force_in, s32[8,2048]{1,0:T(8,128)S(1)} %copy-done.2, bf16[8,2048]{1,0:T(8,128)(2,1)S(1)} %copy-done.3, bf16[512,2048]{1,0:T(8,128)(2,1)S(1)} %get-tuple-element.28.shapes_t, bf16[512,512]{1,0:T(8,128)(2,1)S(1)} %collective-permute-done.4.halo), custom_call_target="tpu_custom_call" | custom-call | flops 12800000000 | tf_op jit(solution)/shard_map/pallas_call | solution.py:33
  22.0 2.2 %collective-permute-done.5 = f32[2,256]{1,0:T(2,128)S(1)} collective-permute-done((f32[2,256]{1,0:T(2,128)S(1)}, f32[2,256]{1,0:T(2,128)S(1)}, u32[]{:S(2)}, u32[]{:S(2)}) %collective-permute-start.5) | collective-permute-done | bytes 2080 | tf_op jit(solution)/shard_map/ppermute | solution.py:399
  24.2 0.0 copy-start.1
  24.2 0.0 copy-start.7
  24.2 0.0 copy-start.8
  24.2 0.8 %collective-permute-start.7 = (f32[2,256]{1,0:T(2,128)S(1)}, f32[2,256]{1,0:T(2,128)S(1)}, u32[]{:S(2)}, u32[]{:S(2)}) collective-permute-start(f32[2,256]{1,0:T(2,128)S(1)} %add.22.force_in), channel_id=1, source_target_pairs={{0,1},{1,0},{2,3},{3,2},{4,60},{5,61},{6,62},{7,63},{8,9},{9,8},{1... | collective-permute-start | bytes 6152 | tf_op jit(solution)/shard_map/ppermute | solution.py:399
  25.0 0.0 collective-permute-done.6.halo
  25.0 1.1 %shard_map.106 = (f32[2,256]{1,0:T(2,128)S(1)}, bf16[512,512]{1,0:T(8,128)(2,1)S(1)}) custom-call(f32[2,256]{1,0:T(2,128)S(1)} %add.22.force_in, s32[8,2048]{1,0:T(8,128)S(1)} %copy-done.2, bf16[8,2048]{1,0:T(8,128)(2,1)S(1)} %copy-done.3, bf16[512,2048]{1,0:T(8,128)(2,1)S(1)} %get-tuple-element.28.shapes_t, bf16[528,512]{1,0:T(8,128)(2,1)S(1)} %collective-permute-done.6.halo), custom_call_target="tpu_custom_call" | custom-call | flops 12800000000 | tf_op jit(solution)/shard_map/pallas_call | solution.py:33
  26.1 0.0 copy-done.1
  26.1 0.0 copy-done.7
  26.1 0.0 copy-done.8
  26.1 0.4 %shard_map.107 = (f32[2,256]{1,0:T(2,128)S(1)}, f32[512,256]{1,0:T(8,128)S(1)}, f32[512,256]{1,0:T(8,128)S(1)}, f32[512,128]{1,0:T(8,128)S(1)}, bf16[256,256]{1,...) custom-call(f32[2,256]{1,0:T(2,128)S(1)} %get-tuple-element.36.message_in, s32[1,256]{1,0:T(1,128)S(1)} %bitcast.7, ...), custom_call_target="tpu_custom_call" | custom-call | flops 900000000 | tf_op jit(solution)/shard_map/pallas_call | solution.py:33
  26.5 1.4 %collective-permute-done.7 = f32[2,256]{1,0:T(2,128)S(1)} collective-permute-done((f32[2,256]{1,0:T(2,128)S(1)}, f32[2,256]{1,0:T(2,128)S(1)}, u32[]{:S(2)}, u32[]{:S(2)}) %collective-permute-start.7) | collective-permute-done | bytes 2080 | tf_op jit(solution)/shard_map/ppermute | solution.py:399
  27.9 0.7 %collective-permute-start.8 = (f32[2,256]{1,0:T(2,128)S(1)}, f32[2,256]{1,0:T(2,128)S(1)}, u32[]{:S(2)}, u32[]{:S(2)}) collective-permute-start(f32[2,256]{1,0:T(2,128)S(1)} %add.23.mine), channel_id=1, source_target_pairs={{0,4},{4,0},{8,12},{12,8},{16,20},{20,16},{24,28},{28,24},{32,36},... | collective-permute-start | bytes 6152 | tf_op jit(solution)/shard_map/ppermute | solution.py:456
  28.6 0.8 %collective-permute-done.8.other = f32[2,256]{1,0:T(2,128)S(1)} collective-permute-done((f32[2,256]{1,0:T(2,128)S(1)}, f32[2,256]{1,0:T(2,128)S(1)}, u32[]{:S(2)}, u32[]{:S(2)}) %collective-permute-start.8) | collective-permute-done | bytes 2080 | tf_op jit(solution)/shard_map/ppermute | solution.py:456
  29.4 2.0 %shard_map.108 = (bf16[512,512]{1,0:T(8,128)(2,1)S(1)}, bf16[512,512]{1,0:T(8,128)(2,1)S(1)}) custom-call(f32[2,256]{1,0:T(2,128)S(1)} %add.23.mine, f32[2,256]{1,0:T(2,128)S(1)} %collective-permute-done.8.other, f32[512,256]{1,0:T(8,128)S(1)} %get-tuple-element.38.u_re, f32[512,256]{1,0:T(8,128)S(1)} %get-tuple-element.39.u_im, ...), custom_call_target="tpu_custom_call" | custom-call | flops 4000000000 | tf_op jit(solution)/shard_map/pallas_call | solution.py:33
  31.4 0.4 %collective-permute-start.9 = (bf16[512,512]{1,0:T(8,128)(2,1)S(1)}, bf16[512,512]{1,0:T(8,128)(2,1)S(1)}, u32[]{:S(2)}, u32[]{:S(2)}) collective-permute-start(bf16[512,512]{1,0:T(8,128)(2,1)S(1)} %get-tuple-element.43.for_im), channel_id=1, source_target_pairs={{0,4},{4,0},{8,12},{12,8},{16,20},{20,16},{24,28},{28,24},{32,36},... | collective-permute-start | bytes 1572872 | tf_op jit(solution)/shard_map/ppermute | solution.py:361
  31.9 2.4 %shard_map.109.before = f32[8,2048]{1,0:T(8,128)S(1)} custom-call(bf16[512,512]{1,0:T(8,128)(2,1)S(1)} %get-tuple-element.44.for_re, bf16[512,512]{1,0:T(8,128)(2,1)S(1)} %get-tuple-element.43.for_im, bf16[512,512]{1,0:T(8,128)(2,1)S(1)} %get-tuple-element.45.far, bf16[512,512]{1,0:T(8,128)(2,1)S(1)} %get-tuple-element.46.middle_a, ...), custom_call_target="tpu_custom_call" | custom-call | flops 2500000000 | tf_op jit(solution)/shard_map/pallas_call | solution.py:33
  34.2 0.0 collective-permute-done.9.for_im
  34.3 3.0 %shard_map.110 = f32[1,2048]{1,0:T(1,128)} custom-call(bf16[512,512]{1,0:T(8,128)(2,1)S(1)} %collective-permute-done.9.for_im, f32[8,2048]{1,0:T(8,128)S(1)} %shard_map.109.before, bf16[512,512]{1,0:T(8,128)(2,1)S(1)} %get-tuple-element.45.far, bf16[512,512]{1,0:T(8,128)(2,1)S(1)} %get-tuple-element.46.middle_a, ...), custom_call_target="tpu_custom_call" | custom-call | flops 2500000000 | tf_op jit(solution)/shard_map/pallas_call | solution.py:33
  (11 shorter events, 0.1 us)
Async XLA Ops:
  0.0 3.4 %copy-start.2 = (s32[8,2048]{1,0:T(8,128)S(1)}, s32[8,2048]{1,0:T(8,128)}, u32[]{:S(2)}) copy-start(s32[8,2048]{1,0:T(8,128)} %links.7) | copy-start | bytes 196612
  0.0 3.4 %copy-start.3 = (bf16[8,2048]{1,0:T(8,128)(2,1)S(1)}, bf16[8,2048]{1,0:T(8,128)(2,1)}, u32[]{:S(2)}) copy-start(bf16[8,2048]{1,0:T(8,128)(2,1)} %weights.7) | copy-start | bytes 98308
  0.0 0.7 %copy-start.4 = (bf16[2,2048]{1,0:T(2,128)(2,1)S(1)}, bf16[2,2048]{1,0:T(2,128)(2,1)}, u32[]{:S(2)}) copy-start(bf16[2,2048]{1,0:T(2,128)(2,1)} %unbalance.1) | copy-start | bytes 24580
  2.6 2.0 %collective-permute-start = (f32[2,256]{1,0:T(2,128)S(1)}, f32[2,256]{1,0:T(2,128)S(1)}, u32[]{:S(2)}, u32[]{:S(2)}) collective-permute-start(f32[2,256]{1,0:T(2,128)S(1)} %get-tuple-element.27.force_in), channel_id=1, source_target_pairs={{0,4},{4,0},{8,12},{12,8},{16,20},{20,16},{24,28},{28,24},{32,36},... | collective-permute-start | bytes 6152 | tf_op jit(solution)/shard_map/ppermute | solution.py:420
  3.4 1.2 %copy-start = (s32[256]{0:T(256)S(1)}, s32[256]{0:T(256)}, u32[]{:S(2)}) copy-start(s32[256]{0:T(256)} %param.19) | copy-start | bytes 3076
  3.4 1.6 %copy-start.5 = (s32[512]{0:T(512)S(1)}, s32[512]{0:T(512)}, u32[]{:S(2)}) copy-start(s32[512]{0:T(512)} %param.14) | copy-start | bytes 6148
  3.4 1.6 %copy-start.6 = (s32[512]{0:T(512)S(1)}, s32[512]{0:T(512)}, u32[]{:S(2)}) copy-start(s32[512]{0:T(512)} %param.15) | copy-start | bytes 6148
  4.6 4.3 %collective-permute-start.1 = (f32[4,256]{1,0:T(4,128)S(1)}, f32[4,256]{1,0:T(4,128)S(1)}, u32[]{:S(2)}, u32[]{:S(2)}) collective-permute-start(f32[4,256]{1,0:T(4,128)S(1)} %pad_maximum_fusion.message_in), channel_id=1, source_target_pairs={{0,1},{1,0},{2,3},{3,2},{4,68},{5,69},{6,70},{7,71},{8,9},{9,8},{1... | collective-permute-start | bytes 12296 | tf_op jit(solution)/shard_map/ppermute | solution.py:399
  6.3 14.6 %collective-permute-start.4 = (bf16[512,512]{1,0:T(8,128)(2,1)S(1)}, bf16[512,512]{1,0:T(8,128)(2,1)S(1)}, u32[]{:S(2)}, u32[]{:S(2)}) collective-permute-start(bf16[512,512]{1,0:T(8,128)(2,1)S(1)} %get-tuple-element.33), channel_id=1, source_target_pairs={{0,1},{1,0},{2,3},{3,2},{4,8},{5,9},{6,10},{7,11},{8,4},{9,5},{10,... | collective-permute-start | bytes 1572872 | tf_op jit(solution)/shard_map/ppermute | solution.py:433
  9.0 2.5 %collective-permute-start.2 = (f32[4,256]{1,0:T(4,128)S(1)}, f32[4,256]{1,0:T(4,128)S(1)}, u32[]{:S(2)}, u32[]{:S(2)}) collective-permute-start(f32[4,256]{1,0:T(4,128)S(1)} %pad_maximum_fusion.1.force_in), channel_id=1, source_target_pairs={{0,3},{1,2},{2,1},{3,0},{4,196},{5,197},{6,198},{7,199},{8,11},{9,... | collective-permute-start | bytes 12296 | tf_op jit(solution)/shard_map/ppermute | solution.py:399
  11.5 9.3 %collective-permute-start.3 = (f32[2,256]{1,0:T(2,128)S(1)}, f32[2,256]{1,0:T(2,128)S(1)}, u32[]{:S(2)}, u32[]{:S(2)}) collective-permute-start(f32[2,256]{1,0:T(2,128)S(1)} %slice_add_fusion.message_in), channel_id=1, source_target_pairs={{0,1},{1,0},{2,3},{3,2},{4,12},{5,13},{6,14},{7,15},{8,9},{9,8},{1... | collective-permute-start | bytes 6152 | tf_op jit(solution)/shard_map/ppermute | solution.py:399
  14.7 10.2 %collective-permute-start.6 = (bf16[528,512]{1,0:T(8,128)(2,1)S(1)}, bf16[528,512]{1,0:T(8,128)(2,1)S(1)}, u32[]{:S(2)}, u32[]{:S(2)}) collective-permute-start(bf16[528,512]{1,0:T(8,128)(2,1)S(1)} %get-tuple-element.35), channel_id=1, source_target_pairs={{0,4},{4,0},{8,12},{12,8},{16,20},{20,16},{24,28},{28,24},{32,36},... | collective-permute-start | bytes 1622024 | tf_op jit(solution)/shard_map/ppermute | solution.py:447
  20.8 3.3 %collective-permute-start.5 = (f32[2,256]{1,0:T(2,128)S(1)}, f32[2,256]{1,0:T(2,128)S(1)}, u32[]{:S(2)}, u32[]{:S(2)}) collective-permute-start(f32[2,256]{1,0:T(2,128)S(1)} %add.21.force_in), channel_id=1, source_target_pairs={{0,1},{1,0},{2,3},{3,2},{4,20},{5,21},{6,22},{7,23},{8,9},{9,8},{1... | collective-permute-start | bytes 6152 | tf_op jit(solution)/shard_map/ppermute | solution.py:399
  24.2 1.9 %copy-start.1 = (f32[256,256]{1,0:T(8,128)S(1)}, f32[256,256]{1,0:T(8,128)}, u32[]{:S(2)}) copy-start(f32[256,256]{1,0:T(8,128)} %coupling.1) | copy-start | bytes 786436
  24.2 1.9 %copy-start.7 = (f32[256]{0:T(256)S(1)}, f32[256]{0:T(256)}, u32[]{:S(2)}) copy-start(f32[256]{0:T(256)} %param.16) | copy-start | bytes 3076
  24.2 1.9 %copy-start.8 = (f32[256]{0:T(256)S(1)}, f32[256]{0:T(256)}, u32[]{:S(2)}) copy-start(f32[256]{0:T(256)} %param.17) | copy-start | bytes 3076
  24.2 3.7 %collective-permute-start.7 = (f32[2,256]{1,0:T(2,128)S(1)}, f32[2,256]{1,0:T(2,128)S(1)}, u32[]{:S(2)}, u32[]{:S(2)}) collective-permute-start(f32[2,256]{1,0:T(2,128)S(1)} %add.22.force_in), channel_id=1, source_target_pairs={{0,1},{1,0},{2,3},{3,2},{4,60},{5,61},{6,62},{7,63},{8,9},{9,8},{1... | collective-permute-start | bytes 6152 | tf_op jit(solution)/shard_map/ppermute | solution.py:399
  27.9 1.5 %collective-permute-start.8 = (f32[2,256]{1,0:T(2,128)S(1)}, f32[2,256]{1,0:T(2,128)S(1)}, u32[]{:S(2)}, u32[]{:S(2)}) collective-permute-start(f32[2,256]{1,0:T(2,128)S(1)} %add.23.mine), channel_id=1, source_target_pairs={{0,4},{4,0},{8,12},{12,8},{16,20},{20,16},{24,28},{28,24},{32,36},... | collective-permute-start | bytes 6152 | tf_op jit(solution)/shard_map/ppermute | solution.py:456
  31.4 2.8 %collective-permute-start.9 = (bf16[512,512]{1,0:T(8,128)(2,1)S(1)}, bf16[512,512]{1,0:T(8,128)(2,1)S(1)}, u32[]{:S(2)}, u32[]{:S(2)}) collective-permute-start(bf16[512,512]{1,0:T(8,128)(2,1)S(1)} %get-tuple-element.43.for_im), channel_id=1, source_target_pairs={{0,4},{4,0},{8,12},{12,8},{16,20},{20,16},{24,28},{28,24},{32,36},... | collective-permute-start | bytes 1572872 | tf_op jit(solution)/shard_map/ppermute | solution.py:361

commit v5 on v4

--- a/solution.py
+++ b/solution.py
@@ -15,7 +15,7 @@
 BLOCK = 256
 WINDOW = 1280
 CODE = 64
-ROOM0 = 50
+ROOM0 = 51
 MICRO = 8.0
 bf16 = jnp.bfloat16
 f32 = jnp.float32
@@ -95,46 +95,31 @@
 ]
 
 
-def first_body(unbalance, shapes, message, shapes_t, landing, load, sems):
-    rows, width = shapes.shape
-    parts = sems.shape[0] - 1
-    step = rows // parts
-    load_copy = pltpu.make_async_copy(unbalance, load, sems.at[parts])
-    load_copy.start()
+def load_body(shapes, landing, sems):
+    parts = sems.shape[0]
+    step = shapes.shape[0] // parts
     copies = []
     for p in range(parts):
         s = pl.ds(p * step, step)
         copy = pltpu.make_async_copy(shapes.at[s, :], landing.at[s, :], sems.at[p])
         copy.start()
         copies.append(copy)
-    load_copy.wait()
-    total = jnp.zeros((load.shape[0], width), f32)
-    for p in range(parts):
-        copies[p].wait()
-        block = landing[p * step : (p + 1) * step, :]
-        total += mm(load[:, p * step : (p + 1) * step], block)
-        shapes_t[:, p * step : (p + 1) * step] = jnp.transpose(block)
-    half = width // 2
-    message[0:1, :] = total[0:1, :half] - total[1:2, half:]
-    message[1:2, :] = total[0:1, half:] + total[1:2, :half]
-
-
-def first(unbalance, shapes):
-    rows, width = shapes.shape
-    parts = 4
-    return call(
-        first_body,
-        [sds((2, width // 2), f32), sds((width, rows), bf16)],
-        (unbalance, shapes),
-        [
-            pltpu.VMEM((rows, width), bf16),
-            pltpu.VMEM(unbalance.shape, bf16),
-            pltpu.SemaphoreType.DMA((parts + 1,)),
-        ],
-        [HBM, HBM],
-        1.5,
-        ROOM0,
-    )
+    for copy in copies:
+        copy.wait()
+
+
+def force_body(unbalance, shapes, force):
+    total = mm(unbalance[...], shapes[...])
+    half = total.shape[1] // 2
+    force[0:1, :] = total[0:1, :half] - total[1:2, half:]
+    force[1:2, :] = total[0:1, half:] + total[1:2, :half]
+
+
+def turn_body(force_in, shapes, force_out, shapes_t):
+    rows = shapes.shape[0]
+    for r in range(0, rows, 2 * BLOCK):
+        shapes_t[:, r : r + 2 * BLOCK] = jnp.transpose(shapes[r : r + 2 * BLOCK, :])
+    force_out[...] = force_in[...]
 
 
 def gather_rows(nodes, one, shapes_t, table):
@@ -192,7 +177,7 @@
     force_out[...] = force_in[...]
 
 
-def end_body(force_in, links, weights, shapes_t, halo, force_out, out, window, tables, *, low_core):
+def end_body(force_in, links, weights, shapes_t, halo, force_out, out, window, tables, *, low_core, inner):
     width, rows = shapes_t.shape
     reach = halo.shape[1]
     own = 1024
@@ -215,6 +200,11 @@
         fill_table(tables.at[i], links[:, pl.ds(start, BLOCK)], weights[:, pl.ds(start, BLOCK)], start)
         modes = mm(window[:, i * BLOCK : i * BLOCK + WINDOW], tables[i])
         out[:, i * BLOCK : (i + 1) * BLOCK] = modes.astype(bf16)
+    for i, b in enumerate(inner):
+        s = slice(b * BLOCK, (b + 1) * BLOCK)
+        fill_table(tables.at[i % 2], links[:, s], weights[:, s], b * BLOCK)
+        modes = mm(shapes_t[:, (b - 2) * BLOCK : (b - 2) * BLOCK + WINDOW], tables[i % 2])
+        out[:, (2 + i) * BLOCK : (3 + i) * BLOCK] = modes.astype(bf16)
     force_out[...] = force_in[...]
 
 
@@ -332,26 +322,29 @@
             at += BLOCK
 
 
-def half_peaks_body(for_re, for_im, far, middle_a, middle_b, near, best):
-    for at, part, e in parts_of((far, middle_a, middle_b, near)):
+def half_peaks_body(for_re, for_im, far, middle, near, best):
+    for at, part, e in parts_of((far, middle, near)):
         best[:, at : at + BLOCK] = peaks_tile(part[:, e : e + BLOCK], for_re, for_im)
 
 
-def all_peaks_body(for_im, before, far, middle_a, middle_b, near, out, for_re):
+def all_peaks_body(for_im, before, far, middle, near, out, for_re):
     count = for_im.shape[1] // 2
     for_re[:, :count] = for_im[:, count:]
     for_re[:, count:] = -for_im[:, :count]
     rows = out.shape[1]
-    end = far.shape[1]
     even = odd_core() == 0
-    for at, part, e in parts_of((far, middle_a, middle_b, near)):
+    for at, part, e in parts_of((far, middle, near)):
         best = jnp.maximum(before[:, at : at + BLOCK], peaks_tile(part[:, e : e + BLOCK], for_re, for_im))
         peak = jnp.sqrt(jnp.max(best, axis=0, keepdims=True))
-        to = at
-        if part is far:
-            to = jnp.where(even, at, at + rows - end)
-        if part is near:
-            to = jnp.where(even, at, at - rows + end)
+        first, last = e, rows - 2 * BLOCK + e
+        if part is middle:
+            to = 2 * BLOCK + e
+        elif part is near:
+            to = jnp.where(even, last, first)
+        elif e < 2 * BLOCK:
+            to = jnp.where(even, first, last)
+        else:
+            to = 5 * BLOCK
         out[0:1, pl.ds(pl.multiple_of(to, BLOCK), BLOCK)] = peak
 
 
@@ -365,7 +358,7 @@
         [sds((1, rows), f32)],
         (there, best, *parts),
         [pltpu.VMEM((total, twice), bf16)],
-        [VMEM] * 6,
+        [VMEM] * 5,
         2.5,
     )[0]
     return out.reshape(rows)
@@ -389,7 +382,16 @@
     high = face_high_nodes.reshape(1, reach)
 
     speeds = speed_index.reshape(1, -1)
-    force, shapes_t = first(unbalance, mode_shapes)
+    shapes = call(
+        load_body,
+        [sds((rows, width), bf16)],
+        (mode_shapes,),
+        [pltpu.SemaphoreType.DMA((4,))],
+        [HBM],
+        1.5,
+        ROOM0,
+    )[0]
+    force = call(force_body, [sds((2, width // 2), f32)], (unbalance, shapes), microseconds=0.5)[0]
     small = sds((2, width // 2), f32)
     letter = sds((4, width // 2), f32)
     tables = pltpu.VMEM((2, WINDOW, BLOCK), bf16)
@@ -404,13 +406,13 @@
             [sds(force.shape, f32), sds((width, len(blocks) * BLOCK), bf16)],
             (force, connectivity, stress_weights, shapes_t),
             [tables],
-            microseconds=MICRO * 1.2,
+            microseconds=MICRO * 2.2,
         )
 
-    def end(halo, low_core, force):
+    def end(halo, low_core, inner, force):
         return call(
-            functools.partial(end_body, low_core=low_core),
-            [small, sds((width, 2 * BLOCK), bf16)],
+            functools.partial(end_body, low_core=low_core, inner=inner),
+            [small, sds((width, (2 + len(inner)) * BLOCK), bf16)],
             (force, connectivity, stress_weights, shapes_t, halo),
             [pltpu.VMEM((width, 3 * reach), bf16), tables],
             [VMEM] * 5,
@@ -418,7 +420,9 @@
         )
 
     arrived = lax.ppermute(force, "slab", CORE_PAIRS)
-    force, middle_a = middle((2, 3), force)
+    force, shapes_t = call(
+        turn_body, [small, sds((width, rows), bf16)], (force, shapes), microseconds=MICRO * 0.6
+    )
     own = speeds.astype(f32)
     message = jnp.concatenate([force + arrived, own, own])
     arrived = swap(message, 0)
@@ -433,7 +437,7 @@
     far_halo = lax.ppermute(far_rows, ("slab", "spd"), FAR_PAIRS)
     message = jnp.concatenate([message[:2] + arrived[:2], message[2:3], arrived[2:3]])
     there = swap(message, 1)
-    message, middle_b = middle((4, 5), message)
+    message, central = middle((2, 3, 4), message)
     force = message[:2] + there[:2]
     arrived, neighbour = swap(force, 2), arrived[2:3]
     force, near_rows = call(
@@ -447,14 +451,14 @@
     near_halo = lax.ppermute(near_rows, "slab", CORE_PAIRS)
     force = force + arrived
     arrived = swap(force, 3)
-    force, far = end(far_halo, 0, force)
+    force, far = end(far_halo, 0, (5,), force)
     force = force + arrived
     arrived = swap(force, 4)
-    force, near = end(near_halo, 1, force)
+    force, near = end(near_halo, 1, (), force)
     force, *prepared = prepare(force, speeds, there, near_halo, natural_freq, damping_ratio, coupling)
     force = force + arrived
     for_re, for_im = solve(force, lax.ppermute(force, "slab", CORE_PAIRS), prepared)
-    return peaks(for_re, for_im, (far, middle_a, middle_b, near))
+    return peaks(for_re, for_im, (far, central, near))
 
 
 def solution(mesh):

time: 37.8 us -> 36.8 us (0.974)
  waiting for transfers between devices: 4.56 us -> 3.83 us
  local copies, waits for them, and re-layouts: 0.77 us -> 0.05 us
  Pallas kernels: 16.7 us -> 17.2 us
    ppermute x5, waiting for transfers between devices: 3.73 us -> 2.84 us  [swap(): return lax.ppermute(x, ('slab', 'spd'), ROUNDS[number])]
    unnamed x18, local copies, waits for them, and re-layouts: 0.76 us -> 0.04 us
    pallas_call x11 -> x12, Pallas kernels: 16.7 us -> 17.2 us  [call(): pl.pallas_call(body, out_shape=out_shape, in_specs=specs or [VMEM] * len(...]
    ppermute x1, starting transfers between devices: 6.1 us -> 5.58 us  [on_device(): near_halo = lax.ppermute(near_rows, 'slab', CORE_PAIRS)]
  transfers between devices with their start and end apart: 10 -> 10, of which waited for: 4 -> 4; matrix products, arithmetic and copies ran while one was open for 0% -> 0% of each run, Pallas kernels for 26% -> 28%
where the time goes in v5:
time: 36.8 us; the launch traced here: 36.2 us
  Pallas kernels  17.2 us (47%)
  starting transfers between devices  14.8 us (40%)
  waiting for transfers between devices  3.83 us (10%)
    pallas_call x12, Pallas kernels, call(): pl.pallas_call(body, out_shape=out_shape, in_specs=specs or [VMEM] * len(...  17.2 us
    ppermute x1, starting transfers between devices, on_device(): near_halo = lax.ppermute(near_rows, 'slab', CORE_PAIRS)  5.58 us
    ppermute x5, starting transfers between devices, swap(): return lax.ppermute(x, ('slab', 'spd'), ROUNDS[number])  4.42 us
    ppermute x1, starting transfers between devices, on_device(): far_halo = lax.ppermute(far_rows, ('slab', 'spd'), FAR_PAIRS)  2.97 us
    ppermute x5, waiting for transfers between devices, swap(): return lax.ppermute(x, ('slab', 'spd'), ROUNDS[number])  2.84 us
    ppermute x1, waiting for transfers between devices, on_device(): lax.ppermute(force, 'slab', CORE_PAIRS)  0.82 us
    ppermute x1, starting transfers between devices, on_device(): arrived = lax.ppermute(force, 'slab', CORE_PAIRS)  0.76 us
  transfers between devices with their start and end apart: 10, of which 4 were waited for; matrix products, arithmetic and copies ran while one was open for 0% of the time, Pallas kernels for 28%

profile of v5, /device:TPU:19, one launch (start us, length us, event | category | flops | bytes accessed | tf_op | source)
XLA Modules:
  0.0 36.2 jit_solution(3082747517727696313)
XLA Ops:
  0.0 0.0 copy-start
  0.0 1.6 %shard_map.100.shapes = bf16[2048,512]{1,0:T(8,128)(2,1)S(1)} custom-call(bf16[2048,512]{1,0:T(8,128)(2,1)} %shapes.1), custom_call_target="tpu_custom_call" | custom-call | flops 1500000000 | tf_op jit(solution)/shard_map/pallas_call | solution.py:33
  1.6 0.0 copy-done
  1.6 0.4 %shard_map.101.force_in = f32[2,256]{1,0:T(2,128)S(1)} custom-call(bf16[2,2048]{1,0:T(2,128)(2,1)S(1)} %copy-done, bf16[2048,512]{1,0:T(8,128)(2,1)S(1)} %shard_map.100.shapes), custom_call_target="tpu_custom_call" | custom-call | flops 500000000 | tf_op jit(solution)/shard_map/pallas_call | solution.py:33
  2.0 0.0 copy-start.1
  2.0 0.0 copy-start.5
  2.0 0.0 copy-start.6
  2.0 0.8 %collective-permute-start = (f32[2,256]{1,0:T(2,128)S(1)}, f32[2,256]{1,0:T(2,128)S(1)}, u32[]{:S(2)}, u32[]{:S(2)}) collective-permute-start(f32[2,256]{1,0:T(2,128)S(1)} %shard_map.101.force_in), channel_id=1, source_target_pairs={{0,4},{4,0},{8,12},{12,8},{16,20},{20,16},{24,28},{28,24},{32,36},... | collective-permute-start | bytes 6152 | tf_op jit(solution)/shard_map/ppermute | solution.py:422
  2.7 0.6 %shard_map.102 = (f32[2,256]{1,0:T(2,128)S(1)}, bf16[512,2048]{1,0:T(8,128)(2,1)S(1)}) custom-call(f32[2,256]{1,0:T(2,128)S(1)} %shard_map.101.force_in, bf16[2048,512]{1,0:T(8,128)(2,1)S(1)} %shard_map.100.shapes), custom_call_target="tpu_custom_call" | custom-call | flops 4800000000 | tf_op jit(solution)/shard_map/pallas_call | solution.py:33
  3.4 0.0 copy-done.1
  3.4 0.2 collective-permute-done
  3.6 0.3 collective-permute-start.1
  3.9 0.0 copy-done.5
  3.9 0.0 copy-done.6
  3.9 0.0 copy-start.3
  3.9 0.0 copy-start.4
  3.9 1.3 %shard_map.103 = (f32[4,256]{1,0:T(4,128)S(1)}, bf16[512,512]{1,0:T(8,128)(2,1)S(1)}) custom-call(f32[4,256]{1,0:T(4,128)S(1)} %pad_maximum_fusion.message_in, s32[1,512]{1,0:T(1,128)S(1)} %bitcast.8, s32[1,512]{1,0:T(1,128)S(1)} %bitcast.10, bf16[512,2048]{1,0:T(8,128)(2,1)S(1)} %get-tuple-element.26.shapes_t), custom_call_target="tpu_custom_call" | custom-call | flops 14400000000 | tf_op jit(solution)/shard_map/pallas_call | solution.py:33
  5.2 3.0 %collective-permute-start.4 = (bf16[512,512]{1,0:T(8,128)(2,1)S(1)}, bf16[512,512]{1,0:T(8,128)(2,1)S(1)}, u32[]{:S(2)}, u32[]{:S(2)}) collective-permute-start(bf16[512,512]{1,0:T(8,128)(2,1)S(1)} %get-tuple-element.30), channel_id=1, source_target_pairs={{0,1},{1,0},{2,3},{3,2},{4,8},{5,9},{6,10},{7,11},{8,4},{9,5},{10,... | collective-permute-start | bytes 1572872 | tf_op jit(solution)/shard_map/ppermute | solution.py:437
  8.2 0.0 collective-permute-done.1
  8.2 1.3 %collective-permute-start.2 = (f32[4,256]{1,0:T(4,128)S(1)}, f32[4,256]{1,0:T(4,128)S(1)}, u32[]{:S(2)}, u32[]{:S(2)}) collective-permute-start(f32[4,256]{1,0:T(4,128)S(1)} %pad_maximum_fusion.1.force_in), channel_id=1, source_target_pairs={{0,3},{1,2},{2,1},{3,0},{4,196},{5,197},{6,198},{7,199},{8,11},{9,... | collective-permute-start | bytes 12296 | tf_op jit(solution)/shard_map/ppermute | solution.py:401
  9.5 0.0 copy-done.3
  9.5 0.0 copy-done.4
  9.5 1.6 %shard_map.104 = (f32[4,256]{1,0:T(4,128)S(1)}, bf16[512,768]{1,0:T(8,128)(2,1)S(1)}) custom-call(f32[4,256]{1,0:T(4,128)S(1)} %pad_maximum_fusion.1.force_in, s32[8,2048]{1,0:T(8,128)S(1)} %copy-done.3, bf16[8,2048]{1,0:T(8,128)(2,1)S(1)} %copy-done.4, bf16[512,2048]{1,0:T(8,128)(2,1)S(1)} %get-tuple-element.26.shapes_t), custom_call_target="tpu_custom_call" | custom-call | flops 17600000000 | tf_op jit(solution)/shard_map/pallas_call | solution.py:33
  11.2 0.0 collective-permute-done.2.there
  11.2 1.7 %collective-permute-start.3 = (f32[2,256]{1,0:T(2,128)S(1)}, f32[2,256]{1,0:T(2,128)S(1)}, u32[]{:S(2)}, u32[]{:S(2)}) collective-permute-start(f32[2,256]{1,0:T(2,128)S(1)} %slice_add_fusion.message_in), channel_id=1, source_target_pairs={{0,1},{1,0},{2,3},{3,2},{4,12},{5,13},{6,14},{7,15},{8,9},{9,8},{1... | collective-permute-start | bytes 6152 | tf_op jit(solution)/shard_map/ppermute | solution.py:401
  12.9 1.3 %shard_map.105 = (f32[2,256]{1,0:T(2,128)S(1)}, bf16[528,512]{1,0:T(8,128)(2,1)S(1)}) custom-call(f32[2,256]{1,0:T(2,128)S(1)} %slice_add_fusion.message_in, f32[1,256]{1,0:T(1,128)S(1)} %slice.26.speeds, s32[1,512]{1,0:T(1,128)S(1)} %bitcast.9, s32[1,512]{1,0:T(1,128)S(1)} %bitcast.11, bf16[512,2048]{1,0:T(8,128)(2,1)S(1)} %get-tuple-element.26.shapes_t), custom_call_target="tpu_custom_call" | custom-call | flops 14400000000 | tf_op jit(solution)/shard_map/pallas_call | solution.py:33
  14.2 5.6 %collective-permute-start.6 = (bf16[528,512]{1,0:T(8,128)(2,1)S(1)}, bf16[528,512]{1,0:T(8,128)(2,1)S(1)}, u32[]{:S(2)}, u32[]{:S(2)}) collective-permute-start(bf16[528,512]{1,0:T(8,128)(2,1)S(1)} %get-tuple-element.32), channel_id=1, source_target_pairs={{0,4},{4,0},{8,12},{12,8},{16,20},{20,16},{24,28},{28,24},{32,36},... | collective-permute-start | bytes 1622024 | tf_op jit(solution)/shard_map/ppermute | solution.py:451
  19.8 0.0 collective-permute-done.3
  19.8 0.0 collective-permute-start.5
  19.8 0.0 collective-permute-done.4.halo
  19.8 1.6 %shard_map.106 = (f32[2,256]{1,0:T(2,128)S(1)}, bf16[512,768]{1,0:T(8,128)(2,1)S(1)}) custom-call(f32[2,256]{1,0:T(2,128)S(1)} %add.21.force_in, s32[8,2048]{1,0:T(8,128)S(1)} %copy-done.3, bf16[8,2048]{1,0:T(8,128)(2,1)S(1)} %copy-done.4, bf16[512,2048]{1,0:T(8,128)(2,1)S(1)} %get-tuple-element.26.shapes_t, bf16[512,512]{1,0:T(8,128)(2,1)S(1)} %collective-permute-done.4.halo), custom_call_target="tpu_custom_call" | custom-call | flops 12800000000 | tf_op jit(solution)/shard_map/pallas_call | solution.py:33
  21.4 1.7 %collective-permute-done.5 = f32[2,256]{1,0:T(2,128)S(1)} collective-permute-done((f32[2,256]{1,0:T(2,128)S(1)}, f32[2,256]{1,0:T(2,128)S(1)}, u32[]{:S(2)}, u32[]{:S(2)}) %collective-permute-start.5) | collective-permute-done | bytes 2080 | tf_op jit(solution)/shard_map/ppermute | solution.py:401
  23.1 0.0 copy-start.2
  23.1 0.0 copy-start.7
  23.1 0.0 copy-start.8
  23.1 1.1 %collective-permute-start.7 = (f32[2,256]{1,0:T(2,128)S(1)}, f32[2,256]{1,0:T(2,128)S(1)}, u32[]{:S(2)}, u32[]{:S(2)}) collective-permute-start(f32[2,256]{1,0:T(2,128)S(1)} %add.22.force_in), channel_id=1, source_target_pairs={{0,1},{1,0},{2,3},{3,2},{4,60},{5,61},{6,62},{7,63},{8,9},{9,8},{1... | collective-permute-start | bytes 6152 | tf_op jit(solution)/shard_map/ppermute | solution.py:401
  24.2 0.0 collective-permute-done.6.halo
  24.2 1.1 %shard_map.107 = (f32[2,256]{1,0:T(2,128)S(1)}, bf16[512,512]{1,0:T(8,128)(2,1)S(1)}) custom-call(f32[2,256]{1,0:T(2,128)S(1)} %add.22.force_in, s32[8,2048]{1,0:T(8,128)S(1)} %copy-done.3, bf16[8,2048]{1,0:T(8,128)(2,1)S(1)} %copy-done.4, bf16[512,2048]{1,0:T(8,128)(2,1)S(1)} %get-tuple-element.26.shapes_t, bf16[528,512]{1,0:T(8,128)(2,1)S(1)} %collective-permute-done.6.halo), custom_call_target="tpu_custom_call" | custom-call | flops 12800000000 | tf_op jit(solution)/shard_map/pallas_call | solution.py:33
  25.3 0.0 copy-done.2
  25.3 0.0 copy-done.7
  25.3 0.0 copy-done.8
  25.3 0.4 %shard_map.108 = (f32[2,256]{1,0:T(2,128)S(1)}, f32[512,256]{1,0:T(8,128)S(1)}, f32[512,256]{1,0:T(8,128)S(1)}, f32[512,128]{1,0:T(8,128)S(1)}, bf16[256,256]{1,...) custom-call(f32[2,256]{1,0:T(2,128)S(1)} %get-tuple-element.33.message_in, s32[1,256]{1,0:T(1,128)S(1)} %bitcast.7, ...), custom_call_target="tpu_custom_call" | custom-call | flops 900000000 | tf_op jit(solution)/shard_map/pallas_call | solution.py:33
  25.7 1.1 %collective-permute-done.7 = f32[2,256]{1,0:T(2,128)S(1)} collective-permute-done((f32[2,256]{1,0:T(2,128)S(1)}, f32[2,256]{1,0:T(2,128)S(1)}, u32[]{:S(2)}, u32[]{:S(2)}) %collective-permute-start.7) | collective-permute-done | bytes 2080 | tf_op jit(solution)/shard_map/ppermute | solution.py:401
  26.9 0.7 %collective-permute-start.8 = (f32[2,256]{1,0:T(2,128)S(1)}, f32[2,256]{1,0:T(2,128)S(1)}, u32[]{:S(2)}, u32[]{:S(2)}) collective-permute-start(f32[2,256]{1,0:T(2,128)S(1)} %add.23.mine), channel_id=1, source_target_pairs={{0,4},{4,0},{8,12},{12,8},{16,20},{20,16},{24,28},{28,24},{32,36},... | collective-permute-start | bytes 6152 | tf_op jit(solution)/shard_map/ppermute | solution.py:460
  27.5 0.8 %collective-permute-done.8.other = f32[2,256]{1,0:T(2,128)S(1)} collective-permute-done((f32[2,256]{1,0:T(2,128)S(1)}, f32[2,256]{1,0:T(2,128)S(1)}, u32[]{:S(2)}, u32[]{:S(2)}) %collective-permute-start.8) | collective-permute-done | bytes 2080 | tf_op jit(solution)/shard_map/ppermute | solution.py:460
  28.4 2.0 %shard_map.109 = (bf16[512,512]{1,0:T(8,128)(2,1)S(1)}, bf16[512,512]{1,0:T(8,128)(2,1)S(1)}) custom-call(f32[2,256]{1,0:T(2,128)S(1)} %add.23.mine, f32[2,256]{1,0:T(2,128)S(1)} %collective-permute-done.8.other, f32[512,256]{1,0:T(8,128)S(1)} %get-tuple-element.35.u_re, f32[512,256]{1,0:T(8,128)S(1)} %get-tuple-element.36.u_im, ...), custom_call_target="tpu_custom_call" | custom-call | flops 4000000000 | tf_op jit(solution)/shard_map/pallas_call | solution.py:33
  30.4 0.4 %collective-permute-start.9 = (bf16[512,512]{1,0:T(8,128)(2,1)S(1)}, bf16[512,512]{1,0:T(8,128)(2,1)S(1)}, u32[]{:S(2)}, u32[]{:S(2)}) collective-permute-start(bf16[512,512]{1,0:T(8,128)(2,1)S(1)} %get-tuple-element.40.for_im), channel_id=1, source_target_pairs={{0,4},{4,0},{8,12},{12,8},{16,20},{20,16},{24,28},{28,24},{32,36},... | collective-permute-start | bytes 1572872 | tf_op jit(solution)/shard_map/ppermute | solution.py:354
  30.8 2.4 %shard_map.110.before = f32[8,2048]{1,0:T(8,128)S(1)} custom-call(bf16[512,512]{1,0:T(8,128)(2,1)S(1)} %get-tuple-element.41.for_re, bf16[512,512]{1,0:T(8,128)(2,1)S(1)} %get-tuple-element.40.for_im, bf16[512,768]{1,0:T(8,128)(2,1)S(1)} %get-tuple-element.42.far, bf16[512,768]{1,0:T(8,128)(2,1)S(1)} %get-tuple-element.43.middle, ...), custom_call_target="tpu_custom_call" | custom-call | flops 2500000000 | tf_op jit(solution)/shard_map/pallas_call | solution.py:33
  33.2 0.0 collective-permute-done.9.for_im
  33.2 3.0 %shard_map.111 = f32[1,2048]{1,0:T(1,128)} custom-call(bf16[512,512]{1,0:T(8,128)(2,1)S(1)} %collective-permute-done.9.for_im, f32[8,2048]{1,0:T(8,128)S(1)} %shard_map.110.before, bf16[512,768]{1,0:T(8,128)(2,1)S(1)} %get-tuple-element.42.far, bf16[512,768]{1,0:T(8,128)(2,1)S(1)} %get-tuple-element.43.middle, bf16[512,512]{1,0:T(8,128)(2,1)S(1)} %get-tuple-element.44.near), custom_call_target="tpu_custom_call" | custom-call | flops 2500000000 | tf_op jit(solution)/shard_map/pallas_call | solution.py:33
  (11 shorter events, 0.1 us)
Async XLA Ops:
  0.0 1.6 %copy-start = (bf16[2,2048]{1,0:T(2,128)(2,1)S(1)}, bf16[2,2048]{1,0:T(2,128)(2,1)}, u32[]{:S(2)}) copy-start(bf16[2,2048]{1,0:T(2,128)(2,1)} %unbalance.1) | copy-start | bytes 24580
  2.0 1.4 %copy-start.1 = (s32[256]{0:T(256)S(1)}, s32[256]{0:T(256)}, u32[]{:S(2)}) copy-start(s32[256]{0:T(256)} %param.19) | copy-start | bytes 3076
  2.0 2.0 %copy-start.5 = (s32[512]{0:T(512)S(1)}, s32[512]{0:T(512)}, u32[]{:S(2)}) copy-start(s32[512]{0:T(512)} %param.14) | copy-start | bytes 6148
  2.0 2.0 %copy-start.6 = (s32[512]{0:T(512)S(1)}, s32[512]{0:T(512)}, u32[]{:S(2)}) copy-start(s32[512]{0:T(512)} %param.15) | copy-start | bytes 6148
  2.0 1.6 %collective-permute-start = (f32[2,256]{1,0:T(2,128)S(1)}, f32[2,256]{1,0:T(2,128)S(1)}, u32[]{:S(2)}, u32[]{:S(2)}) collective-permute-start(f32[2,256]{1,0:T(2,128)S(1)} %shard_map.101.force_in), channel_id=1, source_target_pairs={{0,4},{4,0},{8,12},{12,8},{16,20},{20,16},{24,28},{28,24},{32,36},... | collective-permute-start | bytes 6152 | tf_op jit(solution)/shard_map/ppermute | solution.py:422
  3.6 4.6 %collective-permute-start.1 = (f32[4,256]{1,0:T(4,128)S(1)}, f32[4,256]{1,0:T(4,128)S(1)}, u32[]{:S(2)}, u32[]{:S(2)}) collective-permute-start(f32[4,256]{1,0:T(4,128)S(1)} %pad_maximum_fusion.message_in), channel_id=1, source_target_pairs={{0,1},{1,0},{2,3},{3,2},{4,68},{5,69},{6,70},{7,71},{8,9},{9,8},{1... | collective-permute-start | bytes 12296 | tf_op jit(solution)/shard_map/ppermute | solution.py:401
  3.9 5.6 %copy-start.3 = (s32[8,2048]{1,0:T(8,128)S(1)}, s32[8,2048]{1,0:T(8,128)}, u32[]{:S(2)}) copy-start(s32[8,2048]{1,0:T(8,128)} %links.5) | copy-start | bytes 196612
  3.9 5.6 %copy-start.4 = (bf16[8,2048]{1,0:T(8,128)(2,1)S(1)}, bf16[8,2048]{1,0:T(8,128)(2,1)}, u32[]{:S(2)}) copy-start(bf16[8,2048]{1,0:T(8,128)(2,1)} %weights.5) | copy-start | bytes 98308
  5.2 14.6 %collective-permute-start.4 = (bf16[512,512]{1,0:T(8,128)(2,1)S(1)}, bf16[512,512]{1,0:T(8,128)(2,1)S(1)}, u32[]{:S(2)}, u32[]{:S(2)}) collective-permute-start(bf16[512,512]{1,0:T(8,128)(2,1)S(1)} %get-tuple-element.30), channel_id=1, source_target_pairs={{0,1},{1,0},{2,3},{3,2},{4,8},{5,9},{6,10},{7,11},{8,4},{9,5},{10,... | collective-permute-start | bytes 1572872 | tf_op jit(solution)/shard_map/ppermute | solution.py:437
  8.2 3.0 %collective-permute-start.2 = (f32[4,256]{1,0:T(4,128)S(1)}, f32[4,256]{1,0:T(4,128)S(1)}, u32[]{:S(2)}, u32[]{:S(2)}) collective-permute-start(f32[4,256]{1,0:T(4,128)S(1)} %pad_maximum_fusion.1.force_in), channel_id=1, source_target_pairs={{0,3},{1,2},{2,1},{3,0},{4,196},{5,197},{6,198},{7,199},{8,11},{9,... | collective-permute-start | bytes 12296 | tf_op jit(solution)/shard_map/ppermute | solution.py:401
  11.2 8.6 %collective-permute-start.3 = (f32[2,256]{1,0:T(2,128)S(1)}, f32[2,256]{1,0:T(2,128)S(1)}, u32[]{:S(2)}, u32[]{:S(2)}) collective-permute-start(f32[2,256]{1,0:T(2,128)S(1)} %slice_add_fusion.message_in), channel_id=1, source_target_pairs={{0,1},{1,0},{2,3},{3,2},{4,12},{5,13},{6,14},{7,15},{8,9},{9,8},{1... | collective-permute-start | bytes 6152 | tf_op jit(solution)/shard_map/ppermute | solution.py:401
  14.2 10.0 %collective-permute-start.6 = (bf16[528,512]{1,0:T(8,128)(2,1)S(1)}, bf16[528,512]{1,0:T(8,128)(2,1)S(1)}, u32[]{:S(2)}, u32[]{:S(2)}) collective-permute-start(bf16[528,512]{1,0:T(8,128)(2,1)S(1)} %get-tuple-element.32), channel_id=1, source_target_pairs={{0,4},{4,0},{8,12},{12,8},{16,20},{20,16},{24,28},{28,24},{32,36},... | collective-permute-start | bytes 1622024 | tf_op jit(solution)/shard_map/ppermute | solution.py:451
  19.8 3.3 %collective-permute-start.5 = (f32[2,256]{1,0:T(2,128)S(1)}, f32[2,256]{1,0:T(2,128)S(1)}, u32[]{:S(2)}, u32[]{:S(2)}) collective-permute-start(f32[2,256]{1,0:T(2,128)S(1)} %add.21.force_in), channel_id=1, source_target_pairs={{0,1},{1,0},{2,3},{3,2},{4,20},{5,21},{6,22},{7,23},{8,9},{9,8},{1... | collective-permute-start | bytes 6152 | tf_op jit(solution)/shard_map/ppermute | solution.py:401
  23.1 2.2 %copy-start.2 = (f32[256,256]{1,0:T(8,128)S(1)}, f32[256,256]{1,0:T(8,128)}, u32[]{:S(2)}) copy-start(f32[256,256]{1,0:T(8,128)} %coupling.1) | copy-start | bytes 786436
  23.1 2.2 %copy-start.7 = (f32[256]{0:T(256)S(1)}, f32[256]{0:T(256)}, u32[]{:S(2)}) copy-start(f32[256]{0:T(256)} %param.16) | copy-start | bytes 3076
  23.1 2.2 %copy-start.8 = (f32[256]{0:T(256)S(1)}, f32[256]{0:T(256)}, u32[]{:S(2)}) copy-start(f32[256]{0:T(256)} %param.17) | copy-start | bytes 3076
  23.1 3.7 %collective-permute-start.7 = (f32[2,256]{1,0:T(2,128)S(1)}, f32[2,256]{1,0:T(2,128)S(1)}, u32[]{:S(2)}, u32[]{:S(2)}) collective-permute-start(f32[2,256]{1,0:T(2,128)S(1)} %add.22.force_in), channel_id=1, source_target_pairs={{0,1},{1,0},{2,3},{3,2},{4,60},{5,61},{6,62},{7,63},{8,9},{9,8},{1... | collective-permute-start | bytes 6152 | tf_op jit(solution)/shard_map/ppermute | solution.py:401
  26.9 1.5 %collective-permute-start.8 = (f32[2,256]{1,0:T(2,128)S(1)}, f32[2,256]{1,0:T(2,128)S(1)}, u32[]{:S(2)}, u32[]{:S(2)}) collective-permute-start(f32[2,256]{1,0:T(2,128)S(1)} %add.23.mine), channel_id=1, source_target_pairs={{0,4},{4,0},{8,12},{12,8},{16,20},{20,16},{24,28},{28,24},{32,36},... | collective-permute-start | bytes 6152 | tf_op jit(solution)/shard_map/ppermute | solution.py:460
  30.4 2.8 %collective-permute-start.9 = (bf16[512,512]{1,0:T(8,128)(2,1)S(1)}, bf16[512,512]{1,0:T(8,128)(2,1)S(1)}, u32[]{:S(2)}, u32[]{:S(2)}) collective-permute-start(bf16[512,512]{1,0:T(8,128)(2,1)S(1)} %get-tuple-element.40.for_im), channel_id=1, source_target_pairs={{0,4},{4,0},{8,12},{12,8},{16,20},{20,16},{24,28},{28,24},{32,36},... | collective-permute-start | bytes 1572872 | tf_op jit(solution)/shard_map/ppermute | solution.py:354

commit v6 on v5

--- a/solution.py
+++ b/solution.py
@@ -70,19 +70,31 @@
 CORE_PAIRS = slab_pairs(lambda x, z, c: (x, z, 1 - c))
 
 
-def odd_round(partner, mirror=lambda y: y ^ 1):
+def near_row(x, z, y):
+    return y ^ 1
+
+
+def mirror_row(x, z, y):
+    return Y - 1 - y
+
+
+def patient(x, z):
+    return z == 0 and x > 0
+
+
+def odd_round(partner, row=near_row):
     pairs = []
     for x in range(X):
         for z in range(Z):
             for y in range(Y):
-                pairs.append((slab_of(x, z, 0) * Y + y, slab_of(x, z, 0) * Y + mirror(y)))
+                pairs.append((slab_of(x, z, 0) * Y + y, slab_of(x, z, 0) * Y + row(x, z, y)))
                 pairs.append((slab_of(x, z, 1) * Y + y, slab_of(*partner(x, z), 1) * Y + y))
     return sorted(pairs)
 
 
 ROUNDS = (
-    odd_round(lambda x, z: (x ^ 1, z)),
-    odd_round(lambda x, z: (3 - x, z), lambda y: 3 - y),
+    odd_round(lambda x, z: (x ^ 1, z), lambda x, z, y: (mirror_row if patient(x, z) else near_row)(x, z, y)),
+    odd_round(lambda x, z: (3 - x, z), lambda x, z, y: (near_row if patient(x, z) else mirror_row)(x, z, y)),
     odd_round(lambda x, z: (x, z ^ 1)),
     odd_round(lambda x, z: (x, z ^ 2)),
     odd_round(lambda x, z: (x, 7 - z)),

time: 36.8 us -> 35.9 us (0.976)
  waiting for transfers between devices: 3.83 us -> 2.69 us
  starting transfers between devices: 14.8 us -> 15.2 us
    ppermute x5, starting transfers between devices: 4.42 us -> 5.67 us  [swap(): return lax.ppermute(x, ('slab', 'spd'), ROUNDS[number])]
    ppermute x1, starting transfers between devices: 5.58 us -> 4.37 us  [on_device(): near_halo = lax.ppermute(near_rows, 'slab', CORE_PAIRS)]
    ppermute x5, waiting for transfers between devices: 2.84 us -> 1.71 us  [swap(): return lax.ppermute(x, ('slab', 'spd'), ROUNDS[number])]
    ppermute x1, starting transfers between devices: 0.66 us -> 1.04 us  [on_device(): lax.ppermute(force, 'slab', CORE_PAIRS)]
  transfers between devices with their start and end apart: 10 -> 10, of which waited for: 4 -> 3; matrix products, arithmetic and copies ran while one was open for 0% -> 0% of each run, Pallas kernels for 28% -> 29%
where the time goes in v6:
time: 35.9 us; the launch traced here: 35.5 us
  Pallas kernels  17.2 us (48%)
  starting transfers between devices  15.2 us (42%)
  waiting for transfers between devices  2.69 us (7%)
    pallas_call x12, Pallas kernels, call(): pl.pallas_call(body, out_shape=out_shape, in_specs=specs or [VMEM] * len(...  17.2 us
    ppermute x5, starting transfers between devices, swap(): return lax.ppermute(x, ('slab', 'spd'), ROUNDS[number])  5.67 us
    ppermute x1, starting transfers between devices, on_device(): near_halo = lax.ppermute(near_rows, 'slab', CORE_PAIRS)  4.37 us
    ppermute x1, starting transfers between devices, on_device(): far_halo = lax.ppermute(far_rows, ('slab', 'spd'), FAR_PAIRS)  2.97 us
    ppermute x5, waiting for transfers between devices, swap(): return lax.ppermute(x, ('slab', 'spd'), ROUNDS[number])  1.71 us
    ppermute x1, starting transfers between devices, on_device(): lax.ppermute(force, 'slab', CORE_PAIRS)  1.04 us
    ppermute x1, waiting for transfers between devices, on_device(): lax.ppermute(force, 'slab', CORE_PAIRS)  0.82 us
    ppermute x1, starting transfers between devices, on_device(): arrived = lax.ppermute(force, 'slab', CORE_PAIRS)  0.76 us
  transfers between devices with their start and end apart: 10, of which 3 were waited for; matrix products, arithmetic and copies ran while one was open for 0% of the time, Pallas kernels for 29%

profile of v6, /device:TPU:19, one launch (start us, length us, event | category | flops | bytes accessed | tf_op | source)
XLA Modules:
  0.0 35.5 jit_solution(7997322408892399855)
XLA Ops:
  0.0 0.0 copy-start
  0.0 1.6 %shard_map.100.shapes = bf16[2048,512]{1,0:T(8,128)(2,1)S(1)} custom-call(bf16[2048,512]{1,0:T(8,128)(2,1)} %shapes.1), custom_call_target="tpu_custom_call" | custom-call | flops 1500000000 | tf_op jit(solution)/shard_map/pallas_call | solution.py:33
  1.6 0.0 copy-done
  1.6 0.4 %shard_map.101.force_in = f32[2,256]{1,0:T(2,128)S(1)} custom-call(bf16[2,2048]{1,0:T(2,128)(2,1)S(1)} %copy-done, bf16[2048,512]{1,0:T(8,128)(2,1)S(1)} %shard_map.100.shapes), custom_call_target="tpu_custom_call" | custom-call | flops 500000000 | tf_op jit(solution)/shard_map/pallas_call | solution.py:33
  2.0 0.0 copy-start.1
  2.0 0.0 copy-start.5
  2.0 0.0 copy-start.6
  2.0 0.8 %collective-permute-start = (f32[2,256]{1,0:T(2,128)S(1)}, f32[2,256]{1,0:T(2,128)S(1)}, u32[]{:S(2)}, u32[]{:S(2)}) collective-permute-start(f32[2,256]{1,0:T(2,128)S(1)} %shard_map.101.force_in), channel_id=1, source_target_pairs={{0,4},{4,0},{8,12},{12,8},{16,20},{20,16},{24,28},{28,24},{32,36},... | collective-permute-start | bytes 6152 | tf_op jit(solution)/shard_map/ppermute | solution.py:434
  2.7 0.6 %shard_map.102 = (f32[2,256]{1,0:T(2,128)S(1)}, bf16[512,2048]{1,0:T(8,128)(2,1)S(1)}) custom-call(f32[2,256]{1,0:T(2,128)S(1)} %shard_map.101.force_in, bf16[2048,512]{1,0:T(8,128)(2,1)S(1)} %shard_map.100.shapes), custom_call_target="tpu_custom_call" | custom-call | flops 4800000000 | tf_op jit(solution)/shard_map/pallas_call | solution.py:33
  3.4 0.0 copy-done.1
  3.4 0.2 collective-permute-done
  3.6 0.3 collective-permute-start.1
  3.9 0.0 copy-done.5
  3.9 0.0 copy-done.6
  3.9 0.0 copy-start.3
  3.9 0.0 copy-start.4
  3.9 1.3 %shard_map.103 = (f32[4,256]{1,0:T(4,128)S(1)}, bf16[512,512]{1,0:T(8,128)(2,1)S(1)}) custom-call(f32[4,256]{1,0:T(4,128)S(1)} %pad_maximum_fusion.message_in, s32[1,512]{1,0:T(1,128)S(1)} %bitcast.8, s32[1,512]{1,0:T(1,128)S(1)} %bitcast.10, bf16[512,2048]{1,0:T(8,128)(2,1)S(1)} %get-tuple-element.26.shapes_t), custom_call_target="tpu_custom_call" | custom-call | flops 14400000000 | tf_op jit(solution)/shard_map/pallas_call | solution.py:33
  5.2 3.0 %collective-permute-start.4 = (bf16[512,512]{1,0:T(8,128)(2,1)S(1)}, bf16[512,512]{1,0:T(8,128)(2,1)S(1)}, u32[]{:S(2)}, u32[]{:S(2)}) collective-permute-start(bf16[512,512]{1,0:T(8,128)(2,1)S(1)} %get-tuple-element.30), channel_id=1, source_target_pairs={{0,1},{1,0},{2,3},{3,2},{4,8},{5,9},{6,10},{7,11},{8,4},{9,5},{10,... | collective-permute-start | bytes 1572872 | tf_op jit(solution)/shard_map/ppermute | solution.py:449
  8.2 0.0 collective-permute-done.1
  8.2 1.3 %collective-permute-start.2 = (f32[4,256]{1,0:T(4,128)S(1)}, f32[4,256]{1,0:T(4,128)S(1)}, u32[]{:S(2)}, u32[]{:S(2)}) collective-permute-start(f32[4,256]{1,0:T(4,128)S(1)} %pad_maximum_fusion.1.force_in), channel_id=1, source_target_pairs={{0,3},{1,2},{2,1},{3,0},{4,196},{5,197},{6,198},{7,199},{8,11},{9,... | collective-permute-start | bytes 12296 | tf_op jit(solution)/shard_map/ppermute | solution.py:413
  9.5 0.0 copy-done.3
  9.5 0.0 copy-done.4
  9.5 1.6 %shard_map.104 = (f32[4,256]{1,0:T(4,128)S(1)}, bf16[512,768]{1,0:T(8,128)(2,1)S(1)}) custom-call(f32[4,256]{1,0:T(4,128)S(1)} %pad_maximum_fusion.1.force_in, s32[8,2048]{1,0:T(8,128)S(1)} %copy-done.3, bf16[8,2048]{1,0:T(8,128)(2,1)S(1)} %copy-done.4, bf16[512,2048]{1,0:T(8,128)(2,1)S(1)} %get-tuple-element.26.shapes_t), custom_call_target="tpu_custom_call" | custom-call | flops 17600000000 | tf_op jit(solution)/shard_map/pallas_call | solution.py:33
  11.2 0.0 collective-permute-done.2.there
  11.2 1.7 %collective-permute-start.3 = (f32[2,256]{1,0:T(2,128)S(1)}, f32[2,256]{1,0:T(2,128)S(1)}, u32[]{:S(2)}, u32[]{:S(2)}) collective-permute-start(f32[2,256]{1,0:T(2,128)S(1)} %slice_add_fusion.message_in), channel_id=1, source_target_pairs={{0,1},{1,0},{2,3},{3,2},{4,12},{5,13},{6,14},{7,15},{8,9},{9,8},{1... | collective-permute-start | bytes 6152 | tf_op jit(solution)/shard_map/ppermute | solution.py:413
  12.9 1.3 %shard_map.105 = (f32[2,256]{1,0:T(2,128)S(1)}, bf16[528,512]{1,0:T(8,128)(2,1)S(1)}) custom-call(f32[2,256]{1,0:T(2,128)S(1)} %slice_add_fusion.message_in, f32[1,256]{1,0:T(1,128)S(1)} %slice.26.speeds, s32[1,512]{1,0:T(1,128)S(1)} %bitcast.9, s32[1,512]{1,0:T(1,128)S(1)} %bitcast.11, bf16[512,2048]{1,0:T(8,128)(2,1)S(1)} %get-tuple-element.26.shapes_t), custom_call_target="tpu_custom_call" | custom-call | flops 14400000000 | tf_op jit(solution)/shard_map/pallas_call | solution.py:33
  14.2 4.4 %collective-permute-start.6 = (bf16[528,512]{1,0:T(8,128)(2,1)S(1)}, bf16[528,512]{1,0:T(8,128)(2,1)S(1)}, u32[]{:S(2)}, u32[]{:S(2)}) collective-permute-start(bf16[528,512]{1,0:T(8,128)(2,1)S(1)} %get-tuple-element.32), channel_id=1, source_target_pairs={{0,4},{4,0},{8,12},{12,8},{16,20},{20,16},{24,28},{28,24},{32,36},... | collective-permute-start | bytes 1622024 | tf_op jit(solution)/shard_map/ppermute | solution.py:463
  18.6 0.0 collective-permute-done.3
  18.6 0.0 collective-permute-start.5
  18.6 0.0 collective-permute-done.4.halo
  18.6 1.6 %shard_map.106 = (f32[2,256]{1,0:T(2,128)S(1)}, bf16[512,768]{1,0:T(8,128)(2,1)S(1)}) custom-call(f32[2,256]{1,0:T(2,128)S(1)} %add.21.force_in, s32[8,2048]{1,0:T(8,128)S(1)} %copy-done.3, bf16[8,2048]{1,0:T(8,128)(2,1)S(1)} %copy-done.4, bf16[512,2048]{1,0:T(8,128)(2,1)S(1)} %get-tuple-element.26.shapes_t, bf16[512,512]{1,0:T(8,128)(2,1)S(1)} %collective-permute-done.4.halo), custom_call_target="tpu_custom_call" | custom-call | flops 12800000000 | tf_op jit(solution)/shard_map/pallas_call | solution.py:33
  20.2 1.7 %collective-permute-done.5 = f32[2,256]{1,0:T(2,128)S(1)} collective-permute-done((f32[2,256]{1,0:T(2,128)S(1)}, f32[2,256]{1,0:T(2,128)S(1)}, u32[]{:S(2)}, u32[]{:S(2)}) %collective-permute-start.5) | collective-permute-done | bytes 2080 | tf_op jit(solution)/shard_map/ppermute | solution.py:413
  21.9 0.0 copy-start.2
  21.9 0.0 copy-start.7
  21.9 0.0 copy-start.8
  21.9 2.3 %collective-permute-start.7 = (f32[2,256]{1,0:T(2,128)S(1)}, f32[2,256]{1,0:T(2,128)S(1)}, u32[]{:S(2)}, u32[]{:S(2)}) collective-permute-start(f32[2,256]{1,0:T(2,128)S(1)} %add.22.force_in), channel_id=1, source_target_pairs={{0,1},{1,0},{2,3},{3,2},{4,60},{5,61},{6,62},{7,63},{8,9},{9,8},{1... | collective-permute-start | bytes 6152 | tf_op jit(solution)/shard_map/ppermute | solution.py:413
  24.2 0.0 collective-permute-done.6.halo
  24.2 1.1 %shard_map.107 = (f32[2,256]{1,0:T(2,128)S(1)}, bf16[512,512]{1,0:T(8,128)(2,1)S(1)}) custom-call(f32[2,256]{1,0:T(2,128)S(1)} %add.22.force_in, s32[8,2048]{1,0:T(8,128)S(1)} %copy-done.3, bf16[8,2048]{1,0:T(8,128)(2,1)S(1)} %copy-done.4, bf16[512,2048]{1,0:T(8,128)(2,1)S(1)} %get-tuple-element.26.shapes_t, bf16[528,512]{1,0:T(8,128)(2,1)S(1)} %collective-permute-done.6.halo), custom_call_target="tpu_custom_call" | custom-call | flops 12800000000 | tf_op jit(solution)/shard_map/pallas_call | solution.py:33
  25.3 0.0 copy-done.2
  25.3 0.0 copy-done.7
  25.3 0.0 copy-done.8
  25.3 0.4 %shard_map.108 = (f32[2,256]{1,0:T(2,128)S(1)}, f32[512,256]{1,0:T(8,128)S(1)}, f32[512,256]{1,0:T(8,128)S(1)}, f32[512,128]{1,0:T(8,128)S(1)}, bf16[256,256]{1,...) custom-call(f32[2,256]{1,0:T(2,128)S(1)} %get-tuple-element.33.message_in, s32[1,256]{1,0:T(1,128)S(1)} %bitcast.7, ...), custom_call_target="tpu_custom_call" | custom-call | flops 900000000 | tf_op jit(solution)/shard_map/pallas_call | solution.py:33
  25.7 0.0 collective-permute-done.7
  25.8 1.0 %collective-permute-start.8 = (f32[2,256]{1,0:T(2,128)S(1)}, f32[2,256]{1,0:T(2,128)S(1)}, u32[]{:S(2)}, u32[]{:S(2)}) collective-permute-start(f32[2,256]{1,0:T(2,128)S(1)} %add.23.mine), channel_id=1, source_target_pairs={{0,4},{4,0},{8,12},{12,8},{16,20},{20,16},{24,28},{28,24},{32,36},... | collective-permute-start | bytes 6152 | tf_op jit(solution)/shard_map/ppermute | solution.py:472
  26.8 0.8 %collective-permute-done.8.other = f32[2,256]{1,0:T(2,128)S(1)} collective-permute-done((f32[2,256]{1,0:T(2,128)S(1)}, f32[2,256]{1,0:T(2,128)S(1)}, u32[]{:S(2)}, u32[]{:S(2)}) %collective-permute-start.8) | collective-permute-done | bytes 2080 | tf_op jit(solution)/shard_map/ppermute | solution.py:472
  27.6 2.0 %shard_map.109 = (bf16[512,512]{1,0:T(8,128)(2,1)S(1)}, bf16[512,512]{1,0:T(8,128)(2,1)S(1)}) custom-call(f32[2,256]{1,0:T(2,128)S(1)} %add.23.mine, f32[2,256]{1,0:T(2,128)S(1)} %collective-permute-done.8.other, f32[512,256]{1,0:T(8,128)S(1)} %get-tuple-element.35.u_re, f32[512,256]{1,0:T(8,128)S(1)} %get-tuple-element.36.u_im, ...), custom_call_target="tpu_custom_call" | custom-call | flops 4000000000 | tf_op jit(solution)/shard_map/pallas_call | solution.py:33
  29.7 0.4 %collective-permute-start.9 = (bf16[512,512]{1,0:T(8,128)(2,1)S(1)}, bf16[512,512]{1,0:T(8,128)(2,1)S(1)}, u32[]{:S(2)}, u32[]{:S(2)}) collective-permute-start(bf16[512,512]{1,0:T(8,128)(2,1)S(1)} %get-tuple-element.40.for_im), channel_id=1, source_target_pairs={{0,4},{4,0},{8,12},{12,8},{16,20},{20,16},{24,28},{28,24},{32,36},... | collective-permute-start | bytes 1572872 | tf_op jit(solution)/shard_map/ppermute | solution.py:366
  30.1 2.4 %shard_map.110.before = f32[8,2048]{1,0:T(8,128)S(1)} custom-call(bf16[512,512]{1,0:T(8,128)(2,1)S(1)} %get-tuple-element.41.for_re, bf16[512,512]{1,0:T(8,128)(2,1)S(1)} %get-tuple-element.40.for_im, bf16[512,768]{1,0:T(8,128)(2,1)S(1)} %get-tuple-element.42.far, bf16[512,768]{1,0:T(8,128)(2,1)S(1)} %get-tuple-element.43.middle, ...), custom_call_target="tpu_custom_call" | custom-call | flops 2500000000 | tf_op jit(solution)/shard_map/pallas_call | solution.py:33
  32.5 0.0 collective-permute-done.9.for_im
  32.5 3.0 %shard_map.111 = f32[1,2048]{1,0:T(1,128)} custom-call(bf16[512,512]{1,0:T(8,128)(2,1)S(1)} %collective-permute-done.9.for_im, f32[8,2048]{1,0:T(8,128)S(1)} %shard_map.110.before, bf16[512,768]{1,0:T(8,128)(2,1)S(1)} %get-tuple-element.42.far, bf16[512,768]{1,0:T(8,128)(2,1)S(1)} %get-tuple-element.43.middle, bf16[512,512]{1,0:T(8,128)(2,1)S(1)} %get-tuple-element.44.near), custom_call_target="tpu_custom_call" | custom-call | flops 2500000000 | tf_op jit(solution)/shard_map/pallas_call | solution.py:33
  (11 shorter events, 0.1 us)
Async XLA Ops:
  0.0 1.6 %copy-start = (bf16[2,2048]{1,0:T(2,128)(2,1)S(1)}, bf16[2,2048]{1,0:T(2,128)(2,1)}, u32[]{:S(2)}) copy-start(bf16[2,2048]{1,0:T(2,128)(2,1)} %unbalance.1) | copy-start | bytes 24580
  2.0 1.4 %copy-start.1 = (s32[256]{0:T(256)S(1)}, s32[256]{0:T(256)}, u32[]{:S(2)}) copy-start(s32[256]{0:T(256)} %param.19) | copy-start | bytes 3076
  2.0 2.0 %copy-start.5 = (s32[512]{0:T(512)S(1)}, s32[512]{0:T(512)}, u32[]{:S(2)}) copy-start(s32[512]{0:T(512)} %param.14) | copy-start | bytes 6148
  2.0 2.0 %copy-start.6 = (s32[512]{0:T(512)S(1)}, s32[512]{0:T(512)}, u32[]{:S(2)}) copy-start(s32[512]{0:T(512)} %param.15) | copy-start | bytes 6148
  2.0 1.6 %collective-permute-start = (f32[2,256]{1,0:T(2,128)S(1)}, f32[2,256]{1,0:T(2,128)S(1)}, u32[]{:S(2)}, u32[]{:S(2)}) collective-permute-start(f32[2,256]{1,0:T(2,128)S(1)} %shard_map.101.force_in), channel_id=1, source_target_pairs={{0,4},{4,0},{8,12},{12,8},{16,20},{20,16},{24,28},{28,24},{32,36},... | collective-permute-start | bytes 6152 | tf_op jit(solution)/shard_map/ppermute | solution.py:434
  3.6 4.6 %collective-permute-start.1 = (f32[4,256]{1,0:T(4,128)S(1)}, f32[4,256]{1,0:T(4,128)S(1)}, u32[]{:S(2)}, u32[]{:S(2)}) collective-permute-start(f32[4,256]{1,0:T(4,128)S(1)} %pad_maximum_fusion.message_in), channel_id=1, source_target_pairs={{0,1},{1,0},{2,3},{3,2},{4,68},{5,69},{6,70},{7,71},{8,9},{9,8},{1... | collective-permute-start | bytes 12296 | tf_op jit(solution)/shard_map/ppermute | solution.py:413
  3.9 5.6 %copy-start.3 = (s32[8,2048]{1,0:T(8,128)S(1)}, s32[8,2048]{1,0:T(8,128)}, u32[]{:S(2)}) copy-start(s32[8,2048]{1,0:T(8,128)} %links.5) | copy-start | bytes 196612
  3.9 5.6 %copy-start.4 = (bf16[8,2048]{1,0:T(8,128)(2,1)S(1)}, bf16[8,2048]{1,0:T(8,128)(2,1)}, u32[]{:S(2)}) copy-start(bf16[8,2048]{1,0:T(8,128)(2,1)} %weights.5) | copy-start | bytes 98308
  5.2 13.4 %collective-permute-start.4 = (bf16[512,512]{1,0:T(8,128)(2,1)S(1)}, bf16[512,512]{1,0:T(8,128)(2,1)S(1)}, u32[]{:S(2)}, u32[]{:S(2)}) collective-permute-start(bf16[512,512]{1,0:T(8,128)(2,1)S(1)} %get-tuple-element.30), channel_id=1, source_target_pairs={{0,1},{1,0},{2,3},{3,2},{4,8},{5,9},{6,10},{7,11},{8,4},{9,5},{10,... | collective-permute-start | bytes 1572872 | tf_op jit(solution)/shard_map/ppermute | solution.py:449
  8.2 3.0 %collective-permute-start.2 = (f32[4,256]{1,0:T(4,128)S(1)}, f32[4,256]{1,0:T(4,128)S(1)}, u32[]{:S(2)}, u32[]{:S(2)}) collective-permute-start(f32[4,256]{1,0:T(4,128)S(1)} %pad_maximum_fusion.1.force_in), channel_id=1, source_target_pairs={{0,3},{1,2},{2,1},{3,0},{4,196},{5,197},{6,198},{7,199},{8,11},{9,... | collective-permute-start | bytes 12296 | tf_op jit(solution)/shard_map/ppermute | solution.py:413
  11.2 7.4 %collective-permute-start.3 = (f32[2,256]{1,0:T(2,128)S(1)}, f32[2,256]{1,0:T(2,128)S(1)}, u32[]{:S(2)}, u32[]{:S(2)}) collective-permute-start(f32[2,256]{1,0:T(2,128)S(1)} %slice_add_fusion.message_in), channel_id=1, source_target_pairs={{0,1},{1,0},{2,3},{3,2},{4,12},{5,13},{6,14},{7,15},{8,9},{9,8},{1... | collective-permute-start | bytes 6152 | tf_op jit(solution)/shard_map/ppermute | solution.py:413
  14.2 10.0 %collective-permute-start.6 = (bf16[528,512]{1,0:T(8,128)(2,1)S(1)}, bf16[528,512]{1,0:T(8,128)(2,1)S(1)}, u32[]{:S(2)}, u32[]{:S(2)}) collective-permute-start(bf16[528,512]{1,0:T(8,128)(2,1)S(1)} %get-tuple-element.32), channel_id=1, source_target_pairs={{0,4},{4,0},{8,12},{12,8},{16,20},{20,16},{24,28},{28,24},{32,36},... | collective-permute-start | bytes 1622024 | tf_op jit(solution)/shard_map/ppermute | solution.py:463
  18.6 3.3 %collective-permute-start.5 = (f32[2,256]{1,0:T(2,128)S(1)}, f32[2,256]{1,0:T(2,128)S(1)}, u32[]{:S(2)}, u32[]{:S(2)}) collective-permute-start(f32[2,256]{1,0:T(2,128)S(1)} %add.21.force_in), channel_id=1, source_target_pairs={{0,1},{1,0},{2,3},{3,2},{4,20},{5,21},{6,22},{7,23},{8,9},{9,8},{1... | collective-permute-start | bytes 6152 | tf_op jit(solution)/shard_map/ppermute | solution.py:413
  21.9 3.4 %copy-start.2 = (f32[256,256]{1,0:T(8,128)S(1)}, f32[256,256]{1,0:T(8,128)}, u32[]{:S(2)}) copy-start(f32[256,256]{1,0:T(8,128)} %coupling.1) | copy-start | bytes 786436
  21.9 3.4 %copy-start.7 = (f32[256]{0:T(256)S(1)}, f32[256]{0:T(256)}, u32[]{:S(2)}) copy-start(f32[256]{0:T(256)} %param.16) | copy-start | bytes 3076
  21.9 3.4 %copy-start.8 = (f32[256]{0:T(256)S(1)}, f32[256]{0:T(256)}, u32[]{:S(2)}) copy-start(f32[256]{0:T(256)} %param.17) | copy-start | bytes 3076
  21.9 3.8 %collective-permute-start.7 = (f32[2,256]{1,0:T(2,128)S(1)}, f32[2,256]{1,0:T(2,128)S(1)}, u32[]{:S(2)}, u32[]{:S(2)}) collective-permute-start(f32[2,256]{1,0:T(2,128)S(1)} %add.22.force_in), channel_id=1, source_target_pairs={{0,1},{1,0},{2,3},{3,2},{4,60},{5,61},{6,62},{7,63},{8,9},{9,8},{1... | collective-permute-start | bytes 6152 | tf_op jit(solution)/shard_map/ppermute | solution.py:413
  25.8 1.9 %collective-permute-start.8 = (f32[2,256]{1,0:T(2,128)S(1)}, f32[2,256]{1,0:T(2,128)S(1)}, u32[]{:S(2)}, u32[]{:S(2)}) collective-permute-start(f32[2,256]{1,0:T(2,128)S(1)} %add.23.mine), channel_id=1, source_target_pairs={{0,4},{4,0},{8,12},{12,8},{16,20},{20,16},{24,28},{28,24},{32,36},... | collective-permute-start | bytes 6152 | tf_op jit(solution)/shard_map/ppermute | solution.py:472
  29.7 2.8 %collective-permute-start.9 = (bf16[512,512]{1,0:T(8,128)(2,1)S(1)}, bf16[512,512]{1,0:T(8,128)(2,1)S(1)}, u32[]{:S(2)}, u32[]{:S(2)}) collective-permute-start(bf16[512,512]{1,0:T(8,128)(2,1)S(1)} %get-tuple-element.40.for_im), channel_id=1, source_target_pairs={{0,4},{4,0},{8,12},{12,8},{16,20},{20,16},{24,28},{28,24},{32,36},... | collective-permute-start | bytes 1572872 | tf_op jit(solution)/shard_map/ppermute | solution.py:366

commit v7 on v6

--- a/solution.py
+++ b/solution.py
@@ -9,7 +9,7 @@
 from jax.sharding import PartitionSpec as P
 
 ITERS = 6
-EARLY = 4
+EARLY = 5
 NGRID = 4096
 X, Y, Z, CORES = 4, 4, 8, 2
 BLOCK = 256

time: 35.9 us -> 35.6 us (level)
  no operation moved by 1% of the time
where the time goes in v7:
time: 35.6 us; the launch traced here: 35.2 us
  Pallas kernels  16.9 us (47%)
  starting transfers between devices  15.2 us (43%)
  waiting for transfers between devices  2.69 us (8%)
    pallas_call x12, Pallas kernels, call(): pl.pallas_call(body, out_shape=out_shape, in_specs=specs or [VMEM] * len(...  16.9 us
    ppermute x5, starting transfers between devices, swap(): return lax.ppermute(x, ('slab', 'spd'), ROUNDS[number])  5.67 us
    ppermute x1, starting transfers between devices, on_device(): near_halo = lax.ppermute(near_rows, 'slab', CORE_PAIRS)  4.37 us
    ppermute x1, starting transfers between devices, on_device(): far_halo = lax.ppermute(far_rows, ('slab', 'spd'), FAR_PAIRS)  2.97 us
    ppermute x5, waiting for transfers between devices, swap(): return lax.ppermute(x, ('slab', 'spd'), ROUNDS[number])  1.71 us
    ppermute x1, starting transfers between devices, on_device(): lax.ppermute(force, 'slab', CORE_PAIRS)  1.04 us
    ppermute x1, waiting for transfers between devices, on_device(): lax.ppermute(force, 'slab', CORE_PAIRS)  0.82 us
    ppermute x1, starting transfers between devices, on_device(): arrived = lax.ppermute(force, 'slab', CORE_PAIRS)  0.76 us
  transfers between devices with their start and end apart: 10, of which 3 were waited for; matrix products, arithmetic and copies ran while one was open for 0% of the time, Pallas kernels for 29%

profile of v7, /device:TPU:19, one launch (start us, length us, event | category | flops | bytes accessed | tf_op | source)
XLA Modules:
  0.0 35.2 jit_solution(17080358091405886575)
XLA Ops:
  0.0 0.0 copy-start
  0.0 1.6 %shard_map.100.shapes = bf16[2048,512]{1,0:T(8,128)(2,1)S(1)} custom-call(bf16[2048,512]{1,0:T(8,128)(2,1)} %shapes.1), custom_call_target="tpu_custom_call" | custom-call | flops 1500000000 | tf_op jit(solution)/shard_map/pallas_call | solution.py:33
  1.6 0.0 copy-done
  1.6 0.4 %shard_map.101.force_in = f32[2,256]{1,0:T(2,128)S(1)} custom-call(bf16[2,2048]{1,0:T(2,128)(2,1)S(1)} %copy-done, bf16[2048,512]{1,0:T(8,128)(2,1)S(1)} %shard_map.100.shapes), custom_call_target="tpu_custom_call" | custom-call | flops 500000000 | tf_op jit(solution)/shard_map/pallas_call | solution.py:33
  2.0 0.0 copy-start.1
  2.0 0.0 copy-start.5
  2.0 0.0 copy-start.6
  2.0 0.8 %collective-permute-start = (f32[2,256]{1,0:T(2,128)S(1)}, f32[2,256]{1,0:T(2,128)S(1)}, u32[]{:S(2)}, u32[]{:S(2)}) collective-permute-start(f32[2,256]{1,0:T(2,128)S(1)} %shard_map.101.force_in), channel_id=1, source_target_pairs={{0,4},{4,0},{8,12},{12,8},{16,20},{20,16},{24,28},{28,24},{32,36},... | collective-permute-start | bytes 6152 | tf_op jit(solution)/shard_map/ppermute | solution.py:434
  2.7 0.6 %shard_map.102 = (f32[2,256]{1,0:T(2,128)S(1)}, bf16[512,2048]{1,0:T(8,128)(2,1)S(1)}) custom-call(f32[2,256]{1,0:T(2,128)S(1)} %shard_map.101.force_in, bf16[2048,512]{1,0:T(8,128)(2,1)S(1)} %shard_map.100.shapes), custom_call_target="tpu_custom_call" | custom-call | flops 4800000000 | tf_op jit(solution)/shard_map/pallas_call | solution.py:33
  3.4 0.0 copy-done.1
  3.4 0.2 collective-permute-done
  3.6 0.3 collective-permute-start.1
  3.9 0.0 copy-done.5
  3.9 0.0 copy-done.6
  3.9 0.0 copy-start.3
  3.9 0.0 copy-start.4
  3.9 1.3 %shard_map.103 = (f32[4,256]{1,0:T(4,128)S(1)}, bf16[512,512]{1,0:T(8,128)(2,1)S(1)}) custom-call(f32[4,256]{1,0:T(4,128)S(1)} %pad_maximum_fusion.message_in, s32[1,512]{1,0:T(1,128)S(1)} %bitcast.8, s32[1,512]{1,0:T(1,128)S(1)} %bitcast.10, bf16[512,2048]{1,0:T(8,128)(2,1)S(1)} %get-tuple-element.26.shapes_t), custom_call_target="tpu_custom_call" | custom-call | flops 14400000000 | tf_op jit(solution)/shard_map/pallas_call | solution.py:33
  5.2 3.0 %collective-permute-start.4 = (bf16[512,512]{1,0:T(8,128)(2,1)S(1)}, bf16[512,512]{1,0:T(8,128)(2,1)S(1)}, u32[]{:S(2)}, u32[]{:S(2)}) collective-permute-start(bf16[512,512]{1,0:T(8,128)(2,1)S(1)} %get-tuple-element.30), channel_id=1, source_target_pairs={{0,1},{1,0},{2,3},{3,2},{4,8},{5,9},{6,10},{7,11},{8,4},{9,5},{10,... | collective-permute-start | bytes 1572872 | tf_op jit(solution)/shard_map/ppermute | solution.py:449
  8.2 0.0 collective-permute-done.1
  8.2 1.3 %collective-permute-start.2 = (f32[4,256]{1,0:T(4,128)S(1)}, f32[4,256]{1,0:T(4,128)S(1)}, u32[]{:S(2)}, u32[]{:S(2)}) collective-permute-start(f32[4,256]{1,0:T(4,128)S(1)} %pad_maximum_fusion.1.force_in), channel_id=1, source_target_pairs={{0,3},{1,2},{2,1},{3,0},{4,196},{5,197},{6,198},{7,199},{8,11},{9,... | collective-permute-start | bytes 12296 | tf_op jit(solution)/shard_map/ppermute | solution.py:413
  9.5 0.0 copy-done.3
  9.5 0.0 copy-done.4
  9.5 1.6 %shard_map.104 = (f32[4,256]{1,0:T(4,128)S(1)}, bf16[512,768]{1,0:T(8,128)(2,1)S(1)}) custom-call(f32[4,256]{1,0:T(4,128)S(1)} %pad_maximum_fusion.1.force_in, s32[8,2048]{1,0:T(8,128)S(1)} %copy-done.3, bf16[8,2048]{1,0:T(8,128)(2,1)S(1)} %copy-done.4, bf16[512,2048]{1,0:T(8,128)(2,1)S(1)} %get-tuple-element.26.shapes_t), custom_call_target="tpu_custom_call" | custom-call | flops 17600000000 | tf_op jit(solution)/shard_map/pallas_call | solution.py:33
  11.2 0.0 collective-permute-done.2.there
  11.2 1.7 %collective-permute-start.3 = (f32[2,256]{1,0:T(2,128)S(1)}, f32[2,256]{1,0:T(2,128)S(1)}, u32[]{:S(2)}, u32[]{:S(2)}) collective-permute-start(f32[2,256]{1,0:T(2,128)S(1)} %slice_add_fusion.message_in), channel_id=1, source_target_pairs={{0,1},{1,0},{2,3},{3,2},{4,12},{5,13},{6,14},{7,15},{8,9},{9,8},{1... | collective-permute-start | bytes 6152 | tf_op jit(solution)/shard_map/ppermute | solution.py:413
  12.9 1.3 %shard_map.105 = (f32[2,256]{1,0:T(2,128)S(1)}, bf16[528,512]{1,0:T(8,128)(2,1)S(1)}) custom-call(f32[2,256]{1,0:T(2,128)S(1)} %slice_add_fusion.message_in, f32[1,256]{1,0:T(1,128)S(1)} %slice.26.speeds, s32[1,512]{1,0:T(1,128)S(1)} %bitcast.9, s32[1,512]{1,0:T(1,128)S(1)} %bitcast.11, bf16[512,2048]{1,0:T(8,128)(2,1)S(1)} %get-tuple-element.26.shapes_t), custom_call_target="tpu_custom_call" | custom-call | flops 14400000000 | tf_op jit(solution)/shard_map/pallas_call | solution.py:33
  14.2 4.4 %collective-permute-start.6 = (bf16[528,512]{1,0:T(8,128)(2,1)S(1)}, bf16[528,512]{1,0:T(8,128)(2,1)S(1)}, u32[]{:S(2)}, u32[]{:S(2)}) collective-permute-start(bf16[528,512]{1,0:T(8,128)(2,1)S(1)} %get-tuple-element.32), channel_id=1, source_target_pairs={{0,4},{4,0},{8,12},{12,8},{16,20},{20,16},{24,28},{28,24},{32,36},... | collective-permute-start | bytes 1622024 | tf_op jit(solution)/shard_map/ppermute | solution.py:463
  18.6 0.0 collective-permute-done.3
  18.6 0.0 collective-permute-start.5
  18.6 0.0 collective-permute-done.4.halo
  18.6 1.6 %shard_map.106 = (f32[2,256]{1,0:T(2,128)S(1)}, bf16[512,768]{1,0:T(8,128)(2,1)S(1)}) custom-call(f32[2,256]{1,0:T(2,128)S(1)} %add.21.force_in, s32[8,2048]{1,0:T(8,128)S(1)} %copy-done.3, bf16[8,2048]{1,0:T(8,128)(2,1)S(1)} %copy-done.4, bf16[512,2048]{1,0:T(8,128)(2,1)S(1)} %get-tuple-element.26.shapes_t, bf16[512,512]{1,0:T(8,128)(2,1)S(1)} %collective-permute-done.4.halo), custom_call_target="tpu_custom_call" | custom-call | flops 12800000000 | tf_op jit(solution)/shard_map/pallas_call | solution.py:33
  20.2 1.7 %collective-permute-done.5 = f32[2,256]{1,0:T(2,128)S(1)} collective-permute-done((f32[2,256]{1,0:T(2,128)S(1)}, f32[2,256]{1,0:T(2,128)S(1)}, u32[]{:S(2)}, u32[]{:S(2)}) %collective-permute-start.5) | collective-permute-done | bytes 2080 | tf_op jit(solution)/shard_map/ppermute | solution.py:413
  21.9 0.0 copy-start.2
  21.9 0.0 copy-start.7
  21.9 0.0 copy-start.8
  21.9 2.3 %collective-permute-start.7 = (f32[2,256]{1,0:T(2,128)S(1)}, f32[2,256]{1,0:T(2,128)S(1)}, u32[]{:S(2)}, u32[]{:S(2)}) collective-permute-start(f32[2,256]{1,0:T(2,128)S(1)} %add.22.force_in), channel_id=1, source_target_pairs={{0,1},{1,0},{2,3},{3,2},{4,60},{5,61},{6,62},{7,63},{8,9},{9,8},{1... | collective-permute-start | bytes 6152 | tf_op jit(solution)/shard_map/ppermute | solution.py:413
  24.2 0.0 collective-permute-done.6.halo
  24.2 1.1 %shard_map.107 = (f32[2,256]{1,0:T(2,128)S(1)}, bf16[512,512]{1,0:T(8,128)(2,1)S(1)}) custom-call(f32[2,256]{1,0:T(2,128)S(1)} %add.22.force_in, s32[8,2048]{1,0:T(8,128)S(1)} %copy-done.3, bf16[8,2048]{1,0:T(8,128)(2,1)S(1)} %copy-done.4, bf16[512,2048]{1,0:T(8,128)(2,1)S(1)} %get-tuple-element.26.shapes_t, bf16[528,512]{1,0:T(8,128)(2,1)S(1)} %collective-permute-done.6.halo), custom_call_target="tpu_custom_call" | custom-call | flops 12800000000 | tf_op jit(solution)/shard_map/pallas_call | solution.py:33
  25.3 0.0 copy-done.2
  25.3 0.0 copy-done.7
  25.3 0.0 copy-done.8
  25.3 0.4 %shard_map.108 = (f32[2,256]{1,0:T(2,128)S(1)}, f32[512,256]{1,0:T(8,128)S(1)}, f32[512,256]{1,0:T(8,128)S(1)}, f32[512,128]{1,0:T(8,128)S(1)}, bf16[256,256]{1,...) custom-call(f32[2,256]{1,0:T(2,128)S(1)} %get-tuple-element.33.message_in, s32[1,256]{1,0:T(1,128)S(1)} %bitcast.7, ...), custom_call_target="tpu_custom_call" | custom-call | flops 900000000 | tf_op jit(solution)/shard_map/pallas_call | solution.py:33
  25.7 0.0 collective-permute-done.7
  25.8 1.0 %collective-permute-start.8 = (f32[2,256]{1,0:T(2,128)S(1)}, f32[2,256]{1,0:T(2,128)S(1)}, u32[]{:S(2)}, u32[]{:S(2)}) collective-permute-start(f32[2,256]{1,0:T(2,128)S(1)} %add.23.mine), channel_id=1, source_target_pairs={{0,4},{4,0},{8,12},{12,8},{16,20},{20,16},{24,28},{28,24},{32,36},... | collective-permute-start | bytes 6152 | tf_op jit(solution)/shard_map/ppermute | solution.py:472
  26.8 0.8 %collective-permute-done.8.other = f32[2,256]{1,0:T(2,128)S(1)} collective-permute-done((f32[2,256]{1,0:T(2,128)S(1)}, f32[2,256]{1,0:T(2,128)S(1)}, u32[]{:S(2)}, u32[]{:S(2)}) %collective-permute-start.8) | collective-permute-done | bytes 2080 | tf_op jit(solution)/shard_map/ppermute | solution.py:472
  27.6 1.8 %shard_map.109 = (bf16[512,512]{1,0:T(8,128)(2,1)S(1)}, bf16[512,512]{1,0:T(8,128)(2,1)S(1)}) custom-call(f32[2,256]{1,0:T(2,128)S(1)} %add.23.mine, f32[2,256]{1,0:T(2,128)S(1)} %collective-permute-done.8.other, f32[512,256]{1,0:T(8,128)S(1)} %get-tuple-element.35.u_re, f32[512,256]{1,0:T(8,128)S(1)} %get-tuple-element.36.u_im, ...), custom_call_target="tpu_custom_call" | custom-call | flops 4000000000 | tf_op jit(solution)/shard_map/pallas_call | solution.py:33
  29.4 0.4 %collective-permute-start.9 = (bf16[512,512]{1,0:T(8,128)(2,1)S(1)}, bf16[512,512]{1,0:T(8,128)(2,1)S(1)}, u32[]{:S(2)}, u32[]{:S(2)}) collective-permute-start(bf16[512,512]{1,0:T(8,128)(2,1)S(1)} %get-tuple-element.40.for_im), channel_id=1, source_target_pairs={{0,4},{4,0},{8,12},{12,8},{16,20},{20,16},{24,28},{28,24},{32,36},... | collective-permute-start | bytes 1572872 | tf_op jit(solution)/shard_map/ppermute | solution.py:366
  29.8 2.4 %shard_map.110.before = f32[8,2048]{1,0:T(8,128)S(1)} custom-call(bf16[512,512]{1,0:T(8,128)(2,1)S(1)} %get-tuple-element.41.for_re, bf16[512,512]{1,0:T(8,128)(2,1)S(1)} %get-tuple-element.40.for_im, bf16[512,768]{1,0:T(8,128)(2,1)S(1)} %get-tuple-element.42.far, bf16[512,768]{1,0:T(8,128)(2,1)S(1)} %get-tuple-element.43.middle, ...), custom_call_target="tpu_custom_call" | custom-call | flops 2500000000 | tf_op jit(solution)/shard_map/pallas_call | solution.py:33
  32.2 0.0 collective-permute-done.9.for_im
  32.2 3.0 %shard_map.111 = f32[1,2048]{1,0:T(1,128)} custom-call(bf16[512,512]{1,0:T(8,128)(2,1)S(1)} %collective-permute-done.9.for_im, f32[8,2048]{1,0:T(8,128)S(1)} %shard_map.110.before, bf16[512,768]{1,0:T(8,128)(2,1)S(1)} %get-tuple-element.42.far, bf16[512,768]{1,0:T(8,128)(2,1)S(1)} %get-tuple-element.43.middle, bf16[512,512]{1,0:T(8,128)(2,1)S(1)} %get-tuple-element.44.near), custom_call_target="tpu_custom_call" | custom-call | flops 2500000000 | tf_op jit(solution)/shard_map/pallas_call | solution.py:33
  (11 shorter events, 0.1 us)
Async XLA Ops:
  0.0 1.6 %copy-start = (bf16[2,2048]{1,0:T(2,128)(2,1)S(1)}, bf16[2,2048]{1,0:T(2,128)(2,1)}, u32[]{:S(2)}) copy-start(bf16[2,2048]{1,0:T(2,128)(2,1)} %unbalance.1) | copy-start | bytes 24580
  2.0 1.4 %copy-start.1 = (s32[256]{0:T(256)S(1)}, s32[256]{0:T(256)}, u32[]{:S(2)}) copy-start(s32[256]{0:T(256)} %param.19) | copy-start | bytes 3076
  2.0 2.0 %copy-start.5 = (s32[512]{0:T(512)S(1)}, s32[512]{0:T(512)}, u32[]{:S(2)}) copy-start(s32[512]{0:T(512)} %param.14) | copy-start | bytes 6148
  2.0 2.0 %copy-start.6 = (s32[512]{0:T(512)S(1)}, s32[512]{0:T(512)}, u32[]{:S(2)}) copy-start(s32[512]{0:T(512)} %param.15) | copy-start | bytes 6148
  2.0 1.6 %collective-permute-start = (f32[2,256]{1,0:T(2,128)S(1)}, f32[2,256]{1,0:T(2,128)S(1)}, u32[]{:S(2)}, u32[]{:S(2)}) collective-permute-start(f32[2,256]{1,0:T(2,128)S(1)} %shard_map.101.force_in), channel_id=1, source_target_pairs={{0,4},{4,0},{8,12},{12,8},{16,20},{20,16},{24,28},{28,24},{32,36},... | collective-permute-start | bytes 6152 | tf_op jit(solution)/shard_map/ppermute | solution.py:434
  3.6 4.6 %collective-permute-start.1 = (f32[4,256]{1,0:T(4,128)S(1)}, f32[4,256]{1,0:T(4,128)S(1)}, u32[]{:S(2)}, u32[]{:S(2)}) collective-permute-start(f32[4,256]{1,0:T(4,128)S(1)} %pad_maximum_fusion.message_in), channel_id=1, source_target_pairs={{0,1},{1,0},{2,3},{3,2},{4,68},{5,69},{6,70},{7,71},{8,9},{9,8},{1... | collective-permute-start | bytes 12296 | tf_op jit(solution)/shard_map/ppermute | solution.py:413
  3.9 5.6 %copy-start.3 = (s32[8,2048]{1,0:T(8,128)S(1)}, s32[8,2048]{1,0:T(8,128)}, u32[]{:S(2)}) copy-start(s32[8,2048]{1,0:T(8,128)} %links.5) | copy-start | bytes 196612
  3.9 5.6 %copy-start.4 = (bf16[8,2048]{1,0:T(8,128)(2,1)S(1)}, bf16[8,2048]{1,0:T(8,128)(2,1)}, u32[]{:S(2)}) copy-start(bf16[8,2048]{1,0:T(8,128)(2,1)} %weights.5) | copy-start | bytes 98308
  5.2 13.4 %collective-permute-start.4 = (bf16[512,512]{1,0:T(8,128)(2,1)S(1)}, bf16[512,512]{1,0:T(8,128)(2,1)S(1)}, u32[]{:S(2)}, u32[]{:S(2)}) collective-permute-start(bf16[512,512]{1,0:T(8,128)(2,1)S(1)} %get-tuple-element.30), channel_id=1, source_target_pairs={{0,1},{1,0},{2,3},{3,2},{4,8},{5,9},{6,10},{7,11},{8,4},{9,5},{10,... | collective-permute-start | bytes 1572872 | tf_op jit(solution)/shard_map/ppermute | solution.py:449
  8.2 3.0 %collective-permute-start.2 = (f32[4,256]{1,0:T(4,128)S(1)}, f32[4,256]{1,0:T(4,128)S(1)}, u32[]{:S(2)}, u32[]{:S(2)}) collective-permute-start(f32[4,256]{1,0:T(4,128)S(1)} %pad_maximum_fusion.1.force_in), channel_id=1, source_target_pairs={{0,3},{1,2},{2,1},{3,0},{4,196},{5,197},{6,198},{7,199},{8,11},{9,... | collective-permute-start | bytes 12296 | tf_op jit(solution)/shard_map/ppermute | solution.py:413
  11.2 7.4 %collective-permute-start.3 = (f32[2,256]{1,0:T(2,128)S(1)}, f32[2,256]{1,0:T(2,128)S(1)}, u32[]{:S(2)}, u32[]{:S(2)}) collective-permute-start(f32[2,256]{1,0:T(2,128)S(1)} %slice_add_fusion.message_in), channel_id=1, source_target_pairs={{0,1},{1,0},{2,3},{3,2},{4,12},{5,13},{6,14},{7,15},{8,9},{9,8},{1... | collective-permute-start | bytes 6152 | tf_op jit(solution)/shard_map/ppermute | solution.py:413
  14.2 10.0 %collective-permute-start.6 = (bf16[528,512]{1,0:T(8,128)(2,1)S(1)}, bf16[528,512]{1,0:T(8,128)(2,1)S(1)}, u32[]{:S(2)}, u32[]{:S(2)}) collective-permute-start(bf16[528,512]{1,0:T(8,128)(2,1)S(1)} %get-tuple-element.32), channel_id=1, source_target_pairs={{0,4},{4,0},{8,12},{12,8},{16,20},{20,16},{24,28},{28,24},{32,36},... | collective-permute-start | bytes 1622024 | tf_op jit(solution)/shard_map/ppermute | solution.py:463
  18.6 3.3 %collective-permute-start.5 = (f32[2,256]{1,0:T(2,128)S(1)}, f32[2,256]{1,0:T(2,128)S(1)}, u32[]{:S(2)}, u32[]{:S(2)}) collective-permute-start(f32[2,256]{1,0:T(2,128)S(1)} %add.21.force_in), channel_id=1, source_target_pairs={{0,1},{1,0},{2,3},{3,2},{4,20},{5,21},{6,22},{7,23},{8,9},{9,8},{1... | collective-permute-start | bytes 6152 | tf_op jit(solution)/shard_map/ppermute | solution.py:413
  21.9 3.4 %copy-start.2 = (f32[256,256]{1,0:T(8,128)S(1)}, f32[256,256]{1,0:T(8,128)}, u32[]{:S(2)}) copy-start(f32[256,256]{1,0:T(8,128)} %coupling.1) | copy-start | bytes 786436
  21.9 3.4 %copy-start.7 = (f32[256]{0:T(256)S(1)}, f32[256]{0:T(256)}, u32[]{:S(2)}) copy-start(f32[256]{0:T(256)} %param.16) | copy-start | bytes 3076
  21.9 3.4 %copy-start.8 = (f32[256]{0:T(256)S(1)}, f32[256]{0:T(256)}, u32[]{:S(2)}) copy-start(f32[256]{0:T(256)} %param.17) | copy-start | bytes 3076
  21.9 3.8 %collective-permute-start.7 = (f32[2,256]{1,0:T(2,128)S(1)}, f32[2,256]{1,0:T(2,128)S(1)}, u32[]{:S(2)}, u32[]{:S(2)}) collective-permute-start(f32[2,256]{1,0:T(2,128)S(1)} %add.22.force_in), channel_id=1, source_target_pairs={{0,1},{1,0},{2,3},{3,2},{4,60},{5,61},{6,62},{7,63},{8,9},{9,8},{1... | collective-permute-start | bytes 6152 | tf_op jit(solution)/shard_map/ppermute | solution.py:413
  25.8 1.9 %collective-permute-start.8 = (f32[2,256]{1,0:T(2,128)S(1)}, f32[2,256]{1,0:T(2,128)S(1)}, u32[]{:S(2)}, u32[]{:S(2)}) collective-permute-start(f32[2,256]{1,0:T(2,128)S(1)} %add.23.mine), channel_id=1, source_target_pairs={{0,4},{4,0},{8,12},{12,8},{16,20},{20,16},{24,28},{28,24},{32,36},... | collective-permute-start | bytes 6152 | tf_op jit(solution)/shard_map/ppermute | solution.py:472
  29.4 2.8 %collective-permute-start.9 = (bf16[512,512]{1,0:T(8,128)(2,1)S(1)}, bf16[512,512]{1,0:T(8,128)(2,1)S(1)}, u32[]{:S(2)}, u32[]{:S(2)}) collective-permute-start(bf16[512,512]{1,0:T(8,128)(2,1)S(1)} %get-tuple-element.40.for_im), channel_id=1, source_target_pairs={{0,4},{4,0},{8,12},{12,8},{16,20},{20,16},{24,28},{28,24},{32,36},... | collective-permute-start | bytes 1572872 | tf_op jit(solution)/shard_map/ppermute | solution.py:366

commit v8 on v7

--- a/solution.py
+++ b/solution.py
@@ -448,19 +448,19 @@
     )
     far_halo = lax.ppermute(far_rows, ("slab", "spd"), FAR_PAIRS)
     message = jnp.concatenate([message[:2] + arrived[:2], message[2:3], arrived[2:3]])
-    there = swap(message, 1)
-    message, central = middle((2, 3, 4), message)
-    force = message[:2] + there[:2]
-    arrived, neighbour = swap(force, 2), arrived[2:3]
-    force, near_rows = call(
+    there, neighbour = swap(message, 1), message[3:4]
+    message, near_rows = call(
         near_gather_body,
-        [small, sds((width + 16, reach), bf16)],
-        (force, neighbour, low, high, shapes_t),
+        [letter, sds((width + 16, reach), bf16)],
+        (message, neighbour, low, high, shapes_t),
         [table],
         [VMEM] * 5,
         MICRO * 1.8,
     )
     near_halo = lax.ppermute(near_rows, "slab", CORE_PAIRS)
+    force = message[:2] + there[:2]
+    arrived = swap(force, 2)
+    force, central = middle((2, 3, 4), force)
     force = force + arrived
     arrived = swap(force, 3)
     force, far = end(far_halo, 0, (5,), force)

time: 35.6 us -> 35.6 us (level)
  transfers between devices with their start and end apart: 10 -> 10, of which waited for: 3 -> 4; matrix products, arithmetic and copies ran while one was open for 0% -> 0% of each run, Pallas kernels for 29% -> 29%
where the time goes in v8:
time: 35.6 us; the launch traced here: 35.2 us
  Pallas kernels  16.9 us (47%)
  starting transfers between devices  15.1 us (42%)
  waiting for transfers between devices  2.81 us (8%)
    pallas_call x12, Pallas kernels, call(): pl.pallas_call(body, out_shape=out_shape, in_specs=specs or [VMEM] * len(...  16.9 us
    ppermute x5, starting transfers between devices, swap(): return lax.ppermute(x, ('slab', 'spd'), ROUNDS[number])  5.43 us
    ppermute x1, starting transfers between devices, on_device(): near_halo = lax.ppermute(near_rows, 'slab', CORE_PAIRS)  4.17 us
    ppermute x1, starting transfers between devices, on_device(): far_halo = lax.ppermute(far_rows, ('slab', 'spd'), FAR_PAIRS)  2.97 us
    ppermute x5, waiting for transfers between devices, swap(): return lax.ppermute(x, ('slab', 'spd'), ROUNDS[number])  1.83 us
    ppermute x1, starting transfers between devices, on_device(): lax.ppermute(force, 'slab', CORE_PAIRS)  1.36 us
    ppermute x1, waiting for transfers between devices, on_device(): lax.ppermute(force, 'slab', CORE_PAIRS)  0.82 us
    ppermute x1, starting transfers between devices, on_device(): arrived = lax.ppermute(force, 'slab', CORE_PAIRS)  0.76 us
  transfers between devices with their start and end apart: 10, of which 4 were waited for; matrix products, arithmetic and copies ran while one was open for 0% of the time, Pallas kernels for 29%

profile of v8, /device:TPU:19, one launch (start us, length us, event | category | flops | bytes accessed | tf_op | source)
XLA Modules:
  0.0 35.2 jit_solution(5796157610959106243)
XLA Ops:
  0.0 0.0 copy-start
  0.0 1.6 %shard_map.100.shapes = bf16[2048,512]{1,0:T(8,128)(2,1)S(1)} custom-call(bf16[2048,512]{1,0:T(8,128)(2,1)} %shapes.1), custom_call_target="tpu_custom_call" | custom-call | flops 1500000000 | tf_op jit(solution)/shard_map/pallas_call | solution.py:33
  1.6 0.0 copy-done
  1.6 0.4 %shard_map.101.force_in = f32[2,256]{1,0:T(2,128)S(1)} custom-call(bf16[2,2048]{1,0:T(2,128)(2,1)S(1)} %copy-done, bf16[2048,512]{1,0:T(8,128)(2,1)S(1)} %shard_map.100.shapes), custom_call_target="tpu_custom_call" | custom-call | flops 500000000 | tf_op jit(solution)/shard_map/pallas_call | solution.py:33
  2.0 0.0 copy-start.1
  2.0 0.0 copy-start.5
  2.0 0.0 copy-start.6
  2.0 0.8 %collective-permute-start = (f32[2,256]{1,0:T(2,128)S(1)}, f32[2,256]{1,0:T(2,128)S(1)}, u32[]{:S(2)}, u32[]{:S(2)}) collective-permute-start(f32[2,256]{1,0:T(2,128)S(1)} %shard_map.101.force_in), channel_id=1, source_target_pairs={{0,4},{4,0},{8,12},{12,8},{16,20},{20,16},{24,28},{28,24},{32,36},... | collective-permute-start | bytes 6152 | tf_op jit(solution)/shard_map/ppermute | solution.py:434
  2.7 0.6 %shard_map.102 = (f32[2,256]{1,0:T(2,128)S(1)}, bf16[512,2048]{1,0:T(8,128)(2,1)S(1)}) custom-call(f32[2,256]{1,0:T(2,128)S(1)} %shard_map.101.force_in, bf16[2048,512]{1,0:T(8,128)(2,1)S(1)} %shard_map.100.shapes), custom_call_target="tpu_custom_call" | custom-call | flops 4800000000 | tf_op jit(solution)/shard_map/pallas_call | solution.py:33
  3.4 0.0 copy-done.1
  3.4 0.2 collective-permute-done
  3.6 0.3 collective-permute-start.1
  3.9 0.0 copy-done.5
  3.9 0.0 copy-done.6
  3.9 1.3 %shard_map.103 = (f32[4,256]{1,0:T(4,128)S(1)}, bf16[512,512]{1,0:T(8,128)(2,1)S(1)}) custom-call(f32[4,256]{1,0:T(4,128)S(1)} %pad_maximum_fusion.message_in, s32[1,512]{1,0:T(1,128)S(1)} %bitcast.8, s32[1,512]{1,0:T(1,128)S(1)} %bitcast.10, bf16[512,2048]{1,0:T(8,128)(2,1)S(1)} %get-tuple-element.26.shapes_t), custom_call_target="tpu_custom_call" | custom-call | flops 14400000000 | tf_op jit(solution)/shard_map/pallas_call | solution.py:33
  5.2 3.0 %collective-permute-start.4 = (bf16[512,512]{1,0:T(8,128)(2,1)S(1)}, bf16[512,512]{1,0:T(8,128)(2,1)S(1)}, u32[]{:S(2)}, u32[]{:S(2)}) collective-permute-start(bf16[512,512]{1,0:T(8,128)(2,1)S(1)} %get-tuple-element.30), channel_id=1, source_target_pairs={{0,1},{1,0},{2,3},{3,2},{4,8},{5,9},{6,10},{7,11},{8,4},{9,5},{10,... | collective-permute-start | bytes 1572872 | tf_op jit(solution)/shard_map/ppermute | solution.py:449
  8.2 0.0 collective-permute-done.1
  8.2 0.0 copy-start.3
  8.2 0.0 copy-start.4
  8.2 1.3 %collective-permute-start.2 = (f32[4,256]{1,0:T(4,128)S(1)}, f32[4,256]{1,0:T(4,128)S(1)}, u32[]{:S(2)}, u32[]{:S(2)}) collective-permute-start(f32[4,256]{1,0:T(4,128)S(1)} %pad_maximum_fusion.1.message_in), channel_id=1, source_target_pairs={{0,3},{1,2},{2,1},{3,0},{4,196},{5,197},{6,198},{7,199},{8,11},{9,... | collective-permute-start | bytes 12296 | tf_op jit(solution)/shard_map/ppermute | solution.py:413
  9.5 1.3 %shard_map.104 = (f32[4,256]{1,0:T(4,128)S(1)}, bf16[528,512]{1,0:T(8,128)(2,1)S(1)}) custom-call(f32[4,256]{1,0:T(4,128)S(1)} %pad_maximum_fusion.1.message_in, f32[1,256]{1,0:T(1,128)S(1)} %slice.25.speeds, s32[1,512]{1,0:T(1,128)S(1)} %bitcast.9, s32[1,512]{1,0:T(1,128)S(1)} %bitcast.11, bf16[512,2048]{1,0:T(8,128)(2,1)S(1)} %get-tuple-element.26.shapes_t), custom_call_target="tpu_custom_call" | custom-call | flops 14400000000 | tf_op jit(solution)/shard_map/pallas_call | solution.py:33
  10.8 4.2 %collective-permute-start.6 = (bf16[528,512]{1,0:T(8,128)(2,1)S(1)}, bf16[528,512]{1,0:T(8,128)(2,1)S(1)}, u32[]{:S(2)}, u32[]{:S(2)}) collective-permute-start(bf16[528,512]{1,0:T(8,128)(2,1)S(1)} %get-tuple-element.32), channel_id=1, source_target_pairs={{0,4},{4,0},{8,12},{12,8},{16,20},{20,16},{24,28},{28,24},{32,36},... | collective-permute-start | bytes 1622024 | tf_op jit(solution)/shard_map/ppermute | solution.py:460
  15.0 0.0 collective-permute-done.2.there
  15.0 0.0 collective-permute-start.3
  15.0 0.0 copy-done.3
  15.0 0.0 copy-done.4
  15.0 1.6 %shard_map.105 = (f32[2,256]{1,0:T(2,128)S(1)}, bf16[512,768]{1,0:T(8,128)(2,1)S(1)}) custom-call(f32[2,256]{1,0:T(2,128)S(1)} %slice_add_fusion.force_in, s32[8,2048]{1,0:T(8,128)S(1)} %copy-done.3, bf16[8,2048]{1,0:T(8,128)(2,1)S(1)} %copy-done.4, bf16[512,2048]{1,0:T(8,128)(2,1)S(1)} %get-tuple-element.26.shapes_t), custom_call_target="tpu_custom_call" | custom-call | flops 17600000000 | tf_op jit(solution)/shard_map/pallas_call | solution.py:33
  16.7 1.1 %collective-permute-done.3 = f32[2,256]{1,0:T(2,128)S(1)} collective-permute-done((f32[2,256]{1,0:T(2,128)S(1)}, f32[2,256]{1,0:T(2,128)S(1)}, u32[]{:S(2)}, u32[]{:S(2)}) %collective-permute-start.3) | collective-permute-done | bytes 2080 | tf_op jit(solution)/shard_map/ppermute | solution.py:413
  17.7 1.0 %collective-permute-start.5 = (f32[2,256]{1,0:T(2,128)S(1)}, f32[2,256]{1,0:T(2,128)S(1)}, u32[]{:S(2)}, u32[]{:S(2)}) collective-permute-start(f32[2,256]{1,0:T(2,128)S(1)} %add.21.force_in), channel_id=1, source_target_pairs={{0,1},{1,0},{2,3},{3,2},{4,20},{5,21},{6,22},{7,23},{8,9},{9,8},{1... | collective-permute-start | bytes 6152 | tf_op jit(solution)/shard_map/ppermute | solution.py:413
  18.7 0.0 collective-permute-done.4.halo
  18.7 1.6 %shard_map.106 = (f32[2,256]{1,0:T(2,128)S(1)}, bf16[512,768]{1,0:T(8,128)(2,1)S(1)}) custom-call(f32[2,256]{1,0:T(2,128)S(1)} %add.21.force_in, s32[8,2048]{1,0:T(8,128)S(1)} %copy-done.3, bf16[8,2048]{1,0:T(8,128)(2,1)S(1)} %copy-done.4, bf16[512,2048]{1,0:T(8,128)(2,1)S(1)} %get-tuple-element.26.shapes_t, bf16[512,512]{1,0:T(8,128)(2,1)S(1)} %collective-permute-done.4.halo), custom_call_target="tpu_custom_call" | custom-call | flops 12800000000 | tf_op jit(solution)/shard_map/pallas_call | solution.py:33
  20.3 0.8 %collective-permute-done.5 = f32[2,256]{1,0:T(2,128)S(1)} collective-permute-done((f32[2,256]{1,0:T(2,128)S(1)}, f32[2,256]{1,0:T(2,128)S(1)}, u32[]{:S(2)}, u32[]{:S(2)}) %collective-permute-start.5) | collective-permute-done | bytes 2080 | tf_op jit(solution)/shard_map/ppermute | solution.py:413
  21.1 0.0 copy-start.2
  21.1 0.0 copy-start.7
  21.1 0.0 copy-start.8
  21.1 2.8 %collective-permute-start.7 = (f32[2,256]{1,0:T(2,128)S(1)}, f32[2,256]{1,0:T(2,128)S(1)}, u32[]{:S(2)}, u32[]{:S(2)}) collective-permute-start(f32[2,256]{1,0:T(2,128)S(1)} %add.22.force_in), channel_id=1, source_target_pairs={{0,1},{1,0},{2,3},{3,2},{4,60},{5,61},{6,62},{7,63},{8,9},{9,8},{1... | collective-permute-start | bytes 6152 | tf_op jit(solution)/shard_map/ppermute | solution.py:413
  23.9 0.0 collective-permute-done.6.halo
  23.9 1.1 %shard_map.107 = (f32[2,256]{1,0:T(2,128)S(1)}, bf16[512,512]{1,0:T(8,128)(2,1)S(1)}) custom-call(f32[2,256]{1,0:T(2,128)S(1)} %add.22.force_in, s32[8,2048]{1,0:T(8,128)S(1)} %copy-done.3, bf16[8,2048]{1,0:T(8,128)(2,1)S(1)} %copy-done.4, bf16[512,2048]{1,0:T(8,128)(2,1)S(1)} %get-tuple-element.26.shapes_t, bf16[528,512]{1,0:T(8,128)(2,1)S(1)} %collective-permute-done.6.halo), custom_call_target="tpu_custom_call" | custom-call | flops 12800000000 | tf_op jit(solution)/shard_map/pallas_call | solution.py:33
  25.0 0.0 copy-done.2
  25.0 0.0 copy-done.7
  25.0 0.0 copy-done.8
  25.0 0.4 %shard_map.108 = (f32[2,256]{1,0:T(2,128)S(1)}, f32[512,256]{1,0:T(8,128)S(1)}, f32[512,256]{1,0:T(8,128)S(1)}, f32[512,128]{1,0:T(8,128)S(1)}, bf16[256,256]{1,...) custom-call(f32[2,256]{1,0:T(2,128)S(1)} %get-tuple-element.33.message_in, s32[1,256]{1,0:T(1,128)S(1)} %bitcast.7, ...), custom_call_target="tpu_custom_call" | custom-call | flops 900000000 | tf_op jit(solution)/shard_map/pallas_call | solution.py:33
  25.4 0.0 collective-permute-done.7
  25.5 1.4 %collective-permute-start.8 = (f32[2,256]{1,0:T(2,128)S(1)}, f32[2,256]{1,0:T(2,128)S(1)}, u32[]{:S(2)}, u32[]{:S(2)}) collective-permute-start(f32[2,256]{1,0:T(2,128)S(1)} %add.23.mine), channel_id=1, source_target_pairs={{0,4},{4,0},{8,12},{12,8},{16,20},{20,16},{24,28},{28,24},{32,36},... | collective-permute-start | bytes 6152 | tf_op jit(solution)/shard_map/ppermute | solution.py:472
  26.8 0.8 %collective-permute-done.8.other = f32[2,256]{1,0:T(2,128)S(1)} collective-permute-done((f32[2,256]{1,0:T(2,128)S(1)}, f32[2,256]{1,0:T(2,128)S(1)}, u32[]{:S(2)}, u32[]{:S(2)}) %collective-permute-start.8) | collective-permute-done | bytes 2080 | tf_op jit(solution)/shard_map/ppermute | solution.py:472
  27.6 1.8 %shard_map.109 = (bf16[512,512]{1,0:T(8,128)(2,1)S(1)}, bf16[512,512]{1,0:T(8,128)(2,1)S(1)}) custom-call(f32[2,256]{1,0:T(2,128)S(1)} %add.23.mine, f32[2,256]{1,0:T(2,128)S(1)} %collective-permute-done.8.other, f32[512,256]{1,0:T(8,128)S(1)} %get-tuple-element.35.u_re, f32[512,256]{1,0:T(8,128)S(1)} %get-tuple-element.36.u_im, ...), custom_call_target="tpu_custom_call" | custom-call | flops 4000000000 | tf_op jit(solution)/shard_map/pallas_call | solution.py:33
  29.4 0.4 %collective-permute-start.9 = (bf16[512,512]{1,0:T(8,128)(2,1)S(1)}, bf16[512,512]{1,0:T(8,128)(2,1)S(1)}, u32[]{:S(2)}, u32[]{:S(2)}) collective-permute-start(bf16[512,512]{1,0:T(8,128)(2,1)S(1)} %get-tuple-element.40.for_im), channel_id=1, source_target_pairs={{0,4},{4,0},{8,12},{12,8},{16,20},{20,16},{24,28},{28,24},{32,36},... | collective-permute-start | bytes 1572872 | tf_op jit(solution)/shard_map/ppermute | solution.py:366
  29.8 2.4 %shard_map.110.before = f32[8,2048]{1,0:T(8,128)S(1)} custom-call(bf16[512,512]{1,0:T(8,128)(2,1)S(1)} %get-tuple-element.41.for_re, bf16[512,512]{1,0:T(8,128)(2,1)S(1)} %get-tuple-element.40.for_im, bf16[512,768]{1,0:T(8,128)(2,1)S(1)} %get-tuple-element.42.far, bf16[512,768]{1,0:T(8,128)(2,1)S(1)} %get-tuple-element.43.middle, ...), custom_call_target="tpu_custom_call" | custom-call | flops 2500000000 | tf_op jit(solution)/shard_map/pallas_call | solution.py:33
  32.2 0.0 collective-permute-done.9.for_im
  32.2 3.0 %shard_map.111 = f32[1,2048]{1,0:T(1,128)} custom-call(bf16[512,512]{1,0:T(8,128)(2,1)S(1)} %collective-permute-done.9.for_im, f32[8,2048]{1,0:T(8,128)S(1)} %shard_map.110.before, bf16[512,768]{1,0:T(8,128)(2,1)S(1)} %get-tuple-element.42.far, bf16[512,768]{1,0:T(8,128)(2,1)S(1)} %get-tuple-element.43.middle, bf16[512,512]{1,0:T(8,128)(2,1)S(1)} %get-tuple-element.44.near), custom_call_target="tpu_custom_call" | custom-call | flops 2500000000 | tf_op jit(solution)/shard_map/pallas_call | solution.py:33
  (11 shorter events, 0.1 us)
Async XLA Ops:
  0.0 1.6 %copy-start = (bf16[2,2048]{1,0:T(2,128)(2,1)S(1)}, bf16[2,2048]{1,0:T(2,128)(2,1)}, u32[]{:S(2)}) copy-start(bf16[2,2048]{1,0:T(2,128)(2,1)} %unbalance.1) | copy-start | bytes 24580
  2.0 1.4 %copy-start.1 = (s32[256]{0:T(256)S(1)}, s32[256]{0:T(256)}, u32[]{:S(2)}) copy-start(s32[256]{0:T(256)} %param.19) | copy-start | bytes 3076
  2.0 2.0 %copy-start.5 = (s32[512]{0:T(512)S(1)}, s32[512]{0:T(512)}, u32[]{:S(2)}) copy-start(s32[512]{0:T(512)} %param.14) | copy-start | bytes 6148
  2.0 2.0 %copy-start.6 = (s32[512]{0:T(512)S(1)}, s32[512]{0:T(512)}, u32[]{:S(2)}) copy-start(s32[512]{0:T(512)} %param.15) | copy-start | bytes 6148
  2.0 1.6 %collective-permute-start = (f32[2,256]{1,0:T(2,128)S(1)}, f32[2,256]{1,0:T(2,128)S(1)}, u32[]{:S(2)}, u32[]{:S(2)}) collective-permute-start(f32[2,256]{1,0:T(2,128)S(1)} %shard_map.101.force_in), channel_id=1, source_target_pairs={{0,4},{4,0},{8,12},{12,8},{16,20},{20,16},{24,28},{28,24},{32,36},... | collective-permute-start | bytes 6152 | tf_op jit(solution)/shard_map/ppermute | solution.py:434
  3.6 4.6 %collective-permute-start.1 = (f32[4,256]{1,0:T(4,128)S(1)}, f32[4,256]{1,0:T(4,128)S(1)}, u32[]{:S(2)}, u32[]{:S(2)}) collective-permute-start(f32[4,256]{1,0:T(4,128)S(1)} %pad_maximum_fusion.message_in), channel_id=1, source_target_pairs={{0,1},{1,0},{2,3},{3,2},{4,68},{5,69},{6,70},{7,71},{8,9},{9,8},{1... | collective-permute-start | bytes 12296 | tf_op jit(solution)/shard_map/ppermute | solution.py:413
  5.2 13.5 %collective-permute-start.4 = (bf16[512,512]{1,0:T(8,128)(2,1)S(1)}, bf16[512,512]{1,0:T(8,128)(2,1)S(1)}, u32[]{:S(2)}, u32[]{:S(2)}) collective-permute-start(bf16[512,512]{1,0:T(8,128)(2,1)S(1)} %get-tuple-element.30), channel_id=1, source_target_pairs={{0,1},{1,0},{2,3},{3,2},{4,8},{5,9},{6,10},{7,11},{8,4},{9,5},{10,... | collective-permute-start | bytes 1572872 | tf_op jit(solution)/shard_map/ppermute | solution.py:449
  8.2 6.8 %copy-start.3 = (s32[8,2048]{1,0:T(8,128)S(1)}, s32[8,2048]{1,0:T(8,128)}, u32[]{:S(2)}) copy-start(s32[8,2048]{1,0:T(8,128)} %links.5) | copy-start | bytes 196612
  8.2 6.8 %copy-start.4 = (bf16[8,2048]{1,0:T(8,128)(2,1)S(1)}, bf16[8,2048]{1,0:T(8,128)(2,1)}, u32[]{:S(2)}) copy-start(bf16[8,2048]{1,0:T(8,128)(2,1)} %weights.5) | copy-start | bytes 98308
  8.2 6.7 %collective-permute-start.2 = (f32[4,256]{1,0:T(4,128)S(1)}, f32[4,256]{1,0:T(4,128)S(1)}, u32[]{:S(2)}, u32[]{:S(2)}) collective-permute-start(f32[4,256]{1,0:T(4,128)S(1)} %pad_maximum_fusion.1.message_in), channel_id=1, source_target_pairs={{0,3},{1,2},{2,1},{3,0},{4,196},{5,197},{6,198},{7,199},{8,11},{9,... | collective-permute-start | bytes 12296 | tf_op jit(solution)/shard_map/ppermute | solution.py:413
  10.8 13.1 %collective-permute-start.6 = (bf16[528,512]{1,0:T(8,128)(2,1)S(1)}, bf16[528,512]{1,0:T(8,128)(2,1)S(1)}, u32[]{:S(2)}, u32[]{:S(2)}) collective-permute-start(bf16[528,512]{1,0:T(8,128)(2,1)S(1)} %get-tuple-element.32), channel_id=1, source_target_pairs={{0,4},{4,0},{8,12},{12,8},{16,20},{20,16},{24,28},{28,24},{32,36},... | collective-permute-start | bytes 1622024 | tf_op jit(solution)/shard_map/ppermute | solution.py:460
  15.0 2.7 %collective-permute-start.3 = (f32[2,256]{1,0:T(2,128)S(1)}, f32[2,256]{1,0:T(2,128)S(1)}, u32[]{:S(2)}, u32[]{:S(2)}) collective-permute-start(f32[2,256]{1,0:T(2,128)S(1)} %slice_add_fusion.force_in), channel_id=1, source_target_pairs={{0,1},{1,0},{2,3},{3,2},{4,12},{5,13},{6,14},{7,15},{8,9},{9,8},{1... | collective-permute-start | bytes 6152 | tf_op jit(solution)/shard_map/ppermute | solution.py:413
  17.7 3.3 %collective-permute-start.5 = (f32[2,256]{1,0:T(2,128)S(1)}, f32[2,256]{1,0:T(2,128)S(1)}, u32[]{:S(2)}, u32[]{:S(2)}) collective-permute-start(f32[2,256]{1,0:T(2,128)S(1)} %add.21.force_in), channel_id=1, source_target_pairs={{0,1},{1,0},{2,3},{3,2},{4,20},{5,21},{6,22},{7,23},{8,9},{9,8},{1... | collective-permute-start | bytes 6152 | tf_op jit(solution)/shard_map/ppermute | solution.py:413
  21.1 3.9 %copy-start.2 = (f32[256,256]{1,0:T(8,128)S(1)}, f32[256,256]{1,0:T(8,128)}, u32[]{:S(2)}) copy-start(f32[256,256]{1,0:T(8,128)} %coupling.1) | copy-start | bytes 786436
  21.1 3.9 %copy-start.7 = (f32[256]{0:T(256)S(1)}, f32[256]{0:T(256)}, u32[]{:S(2)}) copy-start(f32[256]{0:T(256)} %param.16) | copy-start | bytes 3076
  21.1 3.9 %copy-start.8 = (f32[256]{0:T(256)S(1)}, f32[256]{0:T(256)}, u32[]{:S(2)}) copy-start(f32[256]{0:T(256)} %param.17) | copy-start | bytes 3076
  21.1 4.4 %collective-permute-start.7 = (f32[2,256]{1,0:T(2,128)S(1)}, f32[2,256]{1,0:T(2,128)S(1)}, u32[]{:S(2)}, u32[]{:S(2)}) collective-permute-start(f32[2,256]{1,0:T(2,128)S(1)} %add.22.force_in), channel_id=1, source_target_pairs={{0,1},{1,0},{2,3},{3,2},{4,60},{5,61},{6,62},{7,63},{8,9},{9,8},{1... | collective-permute-start | bytes 6152 | tf_op jit(solution)/shard_map/ppermute | solution.py:413
  25.5 2.2 %collective-permute-start.8 = (f32[2,256]{1,0:T(2,128)S(1)}, f32[2,256]{1,0:T(2,128)S(1)}, u32[]{:S(2)}, u32[]{:S(2)}) collective-permute-start(f32[2,256]{1,0:T(2,128)S(1)} %add.23.mine), channel_id=1, source_target_pairs={{0,4},{4,0},{8,12},{12,8},{16,20},{20,16},{24,28},{28,24},{32,36},... | collective-permute-start | bytes 6152 | tf_op jit(solution)/shard_map/ppermute | solution.py:472
  29.4 2.8 %collective-permute-start.9 = (bf16[512,512]{1,0:T(8,128)(2,1)S(1)}, bf16[512,512]{1,0:T(8,128)(2,1)S(1)}, u32[]{:S(2)}, u32[]{:S(2)}) collective-permute-start(bf16[512,512]{1,0:T(8,128)(2,1)S(1)} %get-tuple-element.40.for_im), channel_id=1, source_target_pairs={{0,4},{4,0},{8,12},{12,8},{16,20},{20,16},{24,28},{28,24},{32,36},... | collective-permute-start | bytes 1572872 | tf_op jit(solution)/shard_map/ppermute | solution.py:366
